TPU v7x, 512 devices: a whole 4x4x16 slice. The times are simulated.
512 devices in a mesh: expert: 16 (over x, y), tensor: 32 (over z, core).
Axes of the slice: x: 4, y: 4, z: 16, core: 2. Of those that a mesh axis runs over, the one named last changes fastest.
Arguments:
- query: bfloat16 [2048, 4096], P('tensor', 'expert'), may hold values from -140 to 140
- keys: bfloat16 [2048, 1024], P('tensor'), may hold values from -6 to 6
- values: bfloat16 [2048, 1024], P('tensor'), may hold values from -6 to 6
- resid: bfloat16 [2048, 4096], P('tensor', 'expert'), may hold values from -16 to 16
- route_ids: int32 [2048, 4], P('tensor'), may hold values from 0 to 15, all different within a row; in each aligned block of 64 rows (0 to 63, 64 to 127, ...) at most 32 rows name the same one
- route_weight: float32 [2048, 4], P('tensor'), may hold values from 0.1 to 1
- w_in: bfloat16 [16, 4096, 8192], P('expert', None, 'tensor'), may hold values from -0.09375 to 0.09375
- expert_down_matrix: bfloat16 [16, 8192, 4096], P('expert', 'tensor'), may hold values from -0.0625 to 0.0625
Outputs:
- mixed: bfloat16 [2048, 4096], P('tensor', 'expert')
Inputs may be any that keep to these rules, and one draw needn't show every extreme that they name: `route_ids`: each token names 4 different experts. In each aligned block of 64 positions no expert is named by more than 32 of them, and some expert reaches 32 in some block.
All inputs are finite; a program needn't handle non-finite values.
Results may differ from a plain program's by a relative error of at most 0.014.
Values may be sent and summed in bfloat16 or wider, within the bound.
No kernel may reach another device: no remote copies, remote signals or barrier semaphores. Data moves between devices by JAX's collectives and lax.ppermute only.
A program may use at most 64 MiB of HBM per device.

v0:
```python
import math

import jax
import jax.numpy as jnp
from jax import lax
from jax.sharding import PartitionSpec as P

HEADS = 32
KV_HEADS = 8
HEAD_DIM = 128
EXPERTS = 16
EXP_CAP = 32


def router_logit_matrix(ids_part, weight_part):
    route_norm = weight_part / jnp.sum(weight_part, axis=1, keepdims=True)
    expert_grid = jnp.arange(EXPERTS, dtype=jnp.int32)
    picked = ids_part[:, :, None] == expert_grid[None, None, :]
    gate_table = jnp.sum(jnp.where(picked, route_norm[:, :, None], 0.0), axis=1)
    live_rows = jnp.any(picked, axis=1).astype(jnp.bfloat16)
    return (gate_table, live_rows)


def per_device(query, keys, values, resid, route_ids, route_weight, w_in, expert_down_matrix):
    expert_place = lax.axis_index("expert")
    tensor_place = lax.axis_index("tensor")
    block_length = query.shape[0]
    heads_here = query.shape[1] // HEAD_DIM
    group_size = HEADS // KV_HEADS
    kv_count = max(heads_here // group_size, 1)
    kv_first = expert_place * heads_here // group_size
    key_mine = lax.dynamic_slice_in_dim(keys, kv_first * HEAD_DIM, kv_count * HEAD_DIM, 1)
    value_mine = lax.dynamic_slice_in_dim(values, kv_first * HEAD_DIM, kv_count * HEAD_DIM, 1)
    all_keys, all_values = (
        lax.all_gather(key_mine, "tensor", axis=0, tiled=True),
        lax.all_gather(value_mine, "tensor", axis=0, tiled=True),
    )
    seq_total = all_keys.shape[0]
    repeat_by = heads_here // kv_count
    key_heads = jnp.repeat(all_keys.reshape(seq_total, kv_count, HEAD_DIM), repeat_by, axis=1)
    value_heads = jnp.repeat(all_values.reshape(seq_total, kv_count, HEAD_DIM), repeat_by, axis=1)
    query_heads = query.reshape(block_length, heads_here, HEAD_DIM)
    scores = jnp.einsum("qhd,khd->hqk", query_heads, key_heads, preferred_element_type=jnp.float32)
    scores = scores / math.sqrt(HEAD_DIM)
    query_pos = tensor_place * block_length + jnp.arange(block_length)
    causal = query_pos[:, None] >= jnp.arange(seq_total)[None, :]
    scores = jnp.where(causal[None], scores, -1e30)
    top_score = jnp.max(scores, axis=-1, keepdims=True)
    raised = jnp.exp(scores - top_score)
    probs = (raised / jnp.sum(raised, axis=-1, keepdims=True)).astype(jnp.bfloat16)
    attended = jnp.einsum("hqk,khd->qhd", probs, value_heads, preferred_element_type=jnp.float32)
    attended = attended.reshape(block_length, heads_here * HEAD_DIM)
    state = (resid.astype(jnp.float32) + attended).astype(jnp.bfloat16)
    token_rows = lax.all_to_all(state, "expert", split_axis=0, concat_axis=1, tiled=True)
    tokens_here = token_rows.shape[0]
    state_wide = token_rows.astype(jnp.float32)
    center = jnp.mean(state_wide, axis=1, keepdims=True)
    variance = jnp.mean((state_wide - center) ** 2, axis=1, keepdims=True)
    normed = ((state_wide - center) * lax.rsqrt(variance + 1e-05)).astype(jnp.bfloat16)
    my_ids = lax.dynamic_slice_in_dim(route_ids, expert_place * tokens_here, tokens_here, 0)
    local_mixing_factor = lax.dynamic_slice_in_dim(
        route_weight, expert_place * tokens_here, tokens_here, 0
    )
    gate_table, live_rows = router_logit_matrix(my_ids, local_mixing_factor)
    send_rows = live_rows.T[:, :, None] * normed[None, :, :]
    received = lax.all_to_all(send_rows, "expert", split_axis=0, concat_axis=1, tiled=True)
    experts_here = w_in.shape[0]
    capacity = EXP_CAP
    own_experts = expert_place * experts_here + jnp.arange(experts_here, dtype=jnp.int32)
    chosen = jnp.any(route_ids[None, :, :] == own_experts[:, None, None], axis=2).astype(jnp.int32)
    rank = jnp.cumsum(chosen, axis=1) - 1
    slot_grid = jnp.arange(capacity, dtype=jnp.int32)
    selector = jnp.logical_and(rank[:, None, :] == slot_grid[None, :, None], chosen[:, None, :] > 0)
    selector = selector.astype(jnp.bfloat16)
    outgoing = jnp.einsum(
        "akr,ard->akd", selector, received, preferred_element_type=jnp.float32
    ).astype(jnp.bfloat16)
    hidden_activation = jnp.einsum(
        "ard,adf->arf",
        lax.all_gather(outgoing, "tensor", axis=1, tiled=True),
        w_in,
        preferred_element_type=jnp.float32,
    )
    hidden_activation = jax.nn.silu(hidden_activation).astype(jnp.bfloat16)
    incomplete_summands = jnp.einsum(
        "xui,xig->xug", hidden_activation, expert_down_matrix, preferred_element_type=jnp.float32
    )
    summed = lax.psum_scatter(
        incomplete_summands.astype(jnp.bfloat16), "tensor", scatter_dimension=1, tiled=True
    )
    back_rows = jnp.einsum(
        "akr,akd->ard", selector, summed, preferred_element_type=jnp.float32
    ).astype(jnp.bfloat16)
    gathered_back = lax.all_to_all(back_rows, "expert", split_axis=1, concat_axis=0, tiled=True)
    mixture = jnp.einsum("te,etd->td", gate_table, gathered_back.astype(jnp.float32))
    mixed_rows = (state_wide + mixture).astype(jnp.bfloat16)
    return lax.all_to_all(mixed_rows, "expert", split_axis=1, concat_axis=0, tiled=True)


def solution(mesh):
    placed = (
        P("tensor", "expert"),
        P("tensor", None),
        P("tensor", None),
        P("tensor", "expert"),
        P("tensor", None),
        P("tensor", None),
        P("expert", None, "tensor"),
        P("expert", "tensor", None),
    )
    return jax.shard_map(
        per_device, mesh=mesh, in_specs=placed, out_specs=P("tensor", "expert"), check_vma=False
    )
```

profile of v0, /device:TPU:6, one launch (start us, length us, event | category | flops | bytes accessed | tf_op | source)
XLA Modules:
  0.0 364.3 jit_solution(15089456767487024905)
XLA Ops:
  6.5 0.0 copy-start
  6.5 0.9 constant_dynamic-slice_fusion.2
  7.4 37.6 %all_gather.9 = bf16[2048,128]{1,0:T(8,128)(2,1)S(1)} all-gather(bf16[64,128]{1,0:T(8,128)(2,1)S(1)} %constant_dynamic-slice_fusion.2), channel_id=1, replica_groups=mesh['expert'=16,'tensor'=32] {'tensor'}, dimensions={0}, use_global_device_ids=true | all-gather | bytes 540672 | tf_op jit(solution)/shard_map/all_gather | solution.py:36
  45.0 0.7 constant_dynamic-slice_fusion.1
  45.8 28.5 %all_gather.10 = bf16[2048,128]{1,0:T(8,128)(2,1)S(1)} all-gather(bf16[64,128]{1,0:T(8,128)(2,1)S(1)} %constant_dynamic-slice_fusion.1), channel_id=1, replica_groups=mesh['expert'=16,'tensor'=32] {'tensor'}, dimensions={0}, use_global_device_ids=true | all-gather | bytes 540672 | tf_op jit(solution)/shard_map/all_gather | solution.py:35
  74.3 0.1 iota_compare_fusion
  74.4 2.4 fusion.41
  76.8 0.0 copy-start.1
  76.9 0.0 copy-start.2
  76.9 1.6 convolution_bitcast_fusion
  78.5 0.0 copy-done.1
  78.5 0.6 all_to_all.40
  79.1 7.4 %all-to-all-start = ((bf16[16,4,256]{2,1,0:T(4,128)(2,1)}), bf16[16,4,256]{2,1,0:T(4,128)(2,1)S(1)}, u32[]{:S(2)}, u32[]{:S(2)}) async-start(bf16[16,4,256]{2,1,0:T(4,128)(2,1)} %all_to_all.40), calls=%async_computation | async-start | bytes 65536 | tf_op jit(solution)/shard_map/all_to_all | solution.py:54
  86.6 0.0 copy-done.2
  86.6 0.1 constant_dynamic-slice_fusion
  86.6 0.1 copy.36
  86.7 0.1 fusion.36
  86.8 0.1 copy.39
  86.9 5.2 %all-to-all-done = bf16[16,4,256]{2,1,0:T(4,128)(2,1)S(1)} async-done(((bf16[16,4,256]{2,1,0:T(4,128)(2,1)}), bf16[16,4,256]{2,1,0:T(4,128)(2,1)S(1)}, u32[]{:S(2)}, u32[]{:S(2)}) %all-to-all-start) | async-done | bytes 32800 | tf_op jit(solution)/shard_map/all_to_all | solution.py:54
  92.2 0.1 convert_reduce_fusion
  92.3 0.2 multiply_reduce_fusion
  92.6 0.1 multiply_convert_fusion.1
  92.7 1.0 broadcast_multiply_fusion
  93.7 5.5 %all-to-all-start.1 = ((bf16[16,4,4096]{2,1,0:T(4,128)(2,1)}), bf16[16,4,4096]{2,1,0:T(4,128)(2,1)S(1)}, u32[]{:S(2)}, u32[]{:S(2)}) async-start(bf16[16,4,4096]{2,1,0:T(4,128)(2,1)} %broadcast_multiply_fusion), calls=%async_computation.1 | async-start | bytes 1048576 | tf_op jit(solution)/shard_map/all_to_all | solution.py:66
  99.2 0.0 all-gather.3.cloned.1.call-start
  99.3 0.1 copy.38
  99.4 0.1 reduce-window.7
  99.5 0.1 add_reduce_fusion
  99.6 8.4 %all-to-all-done.1 = bf16[16,4,4096]{2,1,0:T(4,128)(2,1)S(1)} async-done(((bf16[16,4,4096]{2,1,0:T(4,128)(2,1)}), bf16[16,4,4096]{2,1,0:T(4,128)(2,1)S(1)}, u32[]{:S(2)}, u32[]{:S(2)}) %all-to-all-start.1) | async-done | bytes 524320 | tf_op jit(solution)/shard_map/all_to_all | solution.py:66
  108.0 0.1 reshape.230
  108.1 0.9 convolution_convert_fusion.1
  109.1 0.0 all-gather.3.cloned.1.call-update
  109.1 0.2 reduce-scatter.2.cloned.1.call-start
  109.3 74.2 %all-gather.3.cloned.1.call-done = bf16[1024,4096]{1,0:T(8,128)(2,1)} async-done(((bf16[32,4096]{1,0:T(8,128)(2,1)}), bf16[1024,4096]{1,0:T(8,128)(2,1)}) %all-gather.3.cloned.1.call-update) | async-done | bytes 8388624 | tf_op jit(solution)/shard_map/all_gather | solution.py:80
  183.5 6.3 %multiply_convert_fusion = bf16[1024,256]{1,0:T(8,128)(2,1)S(1)} fusion(bf16[1024,4096]{1,0:T(8,128)(2,1)} %all-gather.3.cloned.1.call-done, bf16[1,4096,256]{2,1,0:T(8,128)(2,1)} %param.14), kind=kOutput, calls=%fused_computation.14 | convolution fusion | flops 2148794368 | bytes 11010048 | tf_op jit(solution)/shard_map/ard,adf->arf/dot_general | solution.py:78
  189.9 0.0 copy-done
  189.9 5.6 %convert_bitcast_fusion = bf16[1,1024,4096]{2,1,0:T(8,128)(2,1)} fusion(bf16[1024,256]{1,0:T(8,128)(2,1)S(1)} %multiply_convert_fusion, bf16[1,256,4096]{2,1,0:T(8,128)(2,1)S(1)} %copy-done), kind=kOutput, calls=%fused_computation.1 | convolution fusion | flops 2151677952 | bytes 11010048 | tf_op jit(solution)/shard_map/xui,xig->xug/dot_general | solution.py:85
  195.5 0.0 reduce-scatter.2.cloned.1.call-update
  195.5 117.4 %reduce-scatter.2.cloned.1.call-done = bf16[1,32,4096]{2,1,0:T(8,128)(2,1)} async-done(((bf16[1,1024,4096]{2,1,0:T(8,128)(2,1)}), bf16[1,32,4096]{2,1,0:T(8,128)(2,1)}) %reduce-scatter.2.cloned.1.call-update) | async-done | bytes 262160 | tf_op jit(solution)/shard_map/reduce_scatter | solution.py:88
  312.9 1.3 fusion.1
  314.2 1.2 copy.63
  315.4 0.0 copy-start.3
  315.4 0.5 broadcast.123
  315.9 4.7 %reduce.10 = bf16[64,4096]{1,0:T(8,128)(2,1)} reduce(bf16[64,1,4096]{2,1,0:T(2,128)(2,1)S(1)} %bitcast.72, bf16[]{:T(256)} %broadcast.123), dimensions={1}, to_apply=%bitcast.71.reduce_sub_computation | reduce | bytes 1048578
  320.6 2.2 reshape.251
  322.9 6.9 %all-to-all-start.2 = ((bf16[16,2,8192]{2,1,0:T(2,128)(2,1)}), bf16[16,2,8192]{2,1,0:T(2,128)(2,1)}, u32[]{:S(2)}, u32[]{:S(2)}) async-start(bf16[16,2,8192]{2,1,0:T(2,128)(2,1)} %reshape.251), calls=%async_computation.3 | async-start | bytes 1048576 | tf_op jit(solution)/shard_map/all_to_all | solution.py:94
  329.7 0.0 copy-done.3
  329.7 0.1 dynamic-slice_reduce_fusion
  329.8 0.1 dynamic-slice_divide_fusion
  329.9 0.1 copy.37
  330.0 0.1 select_reduce_fusion
  330.1 7.8 %all-to-all-done.2 = bf16[16,2,8192]{2,1,0:T(2,128)(2,1)} async-done(((bf16[16,2,8192]{2,1,0:T(2,128)(2,1)}), bf16[16,2,8192]{2,1,0:T(2,128)(2,1)}, u32[]{:S(2)}, u32[]{:S(2)}) %all-to-all-start.2) | async-done | bytes 524320 | tf_op jit(solution)/shard_map/all_to_all | solution.py:94
  337.9 2.2 reshape.252
  340.1 3.9 %bitcast_reduce_fusion = bf16[64,4096]{1,0:T(8,128)(2,1)} fusion(bf16[64,1,4096]{2,1,0:T(2,128)(2,1)S(1)} %reshape.252), kind=kLoop, calls=%fused_computation.60 | loop fusion | bytes 1048576 | tf_op jit(solution)/shard_map/all_to_all | solution.py:94
  344.0 1.2 all_to_all.44
  345.2 0.7 fusion.11
  345.9 0.1 fusion.17
  346.0 10.9 %all_to_all.53 = bf16[4,16,256]{2,0,1:T(4,128)(2,1)S(1)} all-to-all(bf16[4,16,256]{2,0,1:T(4,128)(2,1)S(1)} %bitcast.75), channel_id=1, replica_groups=mesh['expert'=16,'tensor'=32] {'expert'}, dimensions={1} | all-to-all | bytes 65536 | tf_op jit(solution)/shard_map/all_to_all | solution.py:97
  356.9 0.6 all_to_all.48
  (8 shorter events, 0.1 us)
Async XLA Ops:
  6.5 183.3 %copy-start = (bf16[1,256,4096]{2,1,0:T(8,128)(2,1)S(1)}, bf16[1,256,4096]{2,1,0:T(8,128)(2,1)}, u32[]{:S(2)}) copy-start(bf16[1,256,4096]{2,1,0:T(8,128)(2,1)} %param.15) | copy-start | bytes 6291460
  76.8 1.6 copy-start.1
  76.9 9.7 %copy-start.2 = (s32[64,4]{0,1:T(4,128)S(1)}, s32[64,4]{0,1:T(4,128)}, u32[]{:S(2)}) copy-start(s32[64,4]{0,1:T(4,128)} %param.12) | copy-start | bytes 3076
  79.1 13.1 %all-to-all-start = ((bf16[16,4,256]{2,1,0:T(4,128)(2,1)}), bf16[16,4,256]{2,1,0:T(4,128)(2,1)S(1)}, u32[]{:S(2)}, u32[]{:S(2)}) async-start(bf16[16,4,256]{2,1,0:T(4,128)(2,1)} %all_to_all.40), calls=%async_computation | async-start | bytes 65536 | tf_op jit(solution)/shard_map/all_to_all | solution.py:54
  93.7 14.3 %all-to-all-start.1 = ((bf16[16,4,4096]{2,1,0:T(4,128)(2,1)}), bf16[16,4,4096]{2,1,0:T(4,128)(2,1)S(1)}, u32[]{:S(2)}, u32[]{:S(2)}) async-start(bf16[16,4,4096]{2,1,0:T(4,128)(2,1)} %broadcast_multiply_fusion), calls=%async_computation.1 | async-start | bytes 1048576 | tf_op jit(solution)/shard_map/all_to_all | solution.py:66
  99.2 84.3 %all-gather.3.cloned.1.call-start = ((), (), s32[]{:S(2)}) async-start(), calls=%async_computation.6 | async-start | bytes 8650752 | tf_op jit(solution)/shard_map/all_gather | solution.py:80
  109.1 203.8 %reduce-scatter.2.cloned.1.call-start = ((), (), s32[]{:S(2)}) async-start(), calls=%async_computation.5 | async-start | bytes 8650752 | tf_op jit(solution)/shard_map/reduce_scatter | solution.py:88
  315.4 14.4 %copy-start.3 = (f32[64,4]{0,1:T(4,128)S(1)}, f32[64,4]{0,1:T(4,128)}, u32[]{:S(2)}) copy-start(f32[64,4]{0,1:T(4,128)} %param.13) | copy-start | bytes 3076
  322.9 15.0 %all-to-all-start.2 = ((bf16[16,2,8192]{2,1,0:T(2,128)(2,1)}), bf16[16,2,8192]{2,1,0:T(2,128)(2,1)}, u32[]{:S(2)}, u32[]{:S(2)}) async-start(bf16[16,2,8192]{2,1,0:T(2,128)(2,1)} %reshape.251), calls=%async_computation.3 | async-start | bytes 1048576 | tf_op jit(solution)/shard_map/all_to_all | solution.py:94
Sparse Core Ops, SparseCore 0:
  109.2 74.2 all-gather.2
  195.6 117.2 reduce-scatter.1
where the time goes:
time: 366 us; the launch traced here: 364 us
  waiting for transfers between devices  213 us (58%)
  blocking collectives  77 us (21%)
  starting transfers between devices  20.1 us (5%)
  matrix products  18.8 us (5%)
  local copies, waits for them, and re-layouts  14.7 us (4%)
  between operations  13.5 us (4%)
  other arithmetic  7.06 us (2%)
    reduce_scatter x1, waiting for transfers between devices, per_device(): lax.psum_scatter(incomplete_summands.astype(jnp.bfloat16), 'tensor', scat...  117 us
    all_gather x1, waiting for transfers between devices, per_device(): lax.all_gather(outgoing, 'tensor', axis=1, tiled=True)  74.2 us
    all_gather x1, blocking collectives, per_device(): lax.all_gather(value_mine, 'tensor', axis=0, tiled=True)  37.6 us
    all_gather x1, blocking collectives, per_device(): lax.all_gather(key_mine, 'tensor', axis=0, tiled=True)  28.5 us
    all_to_all x1, blocking collectives, per_device(): lax.all_to_all(mixed_rows, 'expert', split_axis=1, concat_axis=0, tiled=T...  10.9 us
    all_to_all x1, waiting for transfers between devices, per_device(): lax.all_to_all(send_rows, 'expert', split_axis=0, concat_axis=1, tiled=True)  8.39 us
    all_to_all x1, waiting for transfers between devices, per_device(): lax.all_to_all(back_rows, 'expert', split_axis=1, concat_axis=0, tiled=True)  7.8 us
    all_to_all x1, starting transfers between devices, per_device(): lax.all_to_all(state, 'expert', split_axis=0, concat_axis=1, tiled=True)  7.43 us
  transfers between devices with their start and end apart: 5, of which 5 were waited for; matrix products, arithmetic and copies ran while one was open for 0% of the time, Pallas kernels for 0%

commit v1 on v0

v1 whole, which is shorter than its diff:
```python
import math

import jax
import jax.numpy as jnp
from jax import lax
from jax.sharding import Mesh
from jax.sharding import PartitionSpec as P

HEADS = 32
KV_HEADS = 8
HEAD_DIM = 128
EXPERTS = 16
EXP_CAP = 32
TOPK = 4

E = ("x", "y")
T = ("z", "core")


def gather_kv(keys, values):
    place = lax.axis_index(E)
    group = place // 2
    odd = (place % 2) == 1
    k = lax.dynamic_slice_in_dim(keys, group * HEAD_DIM, HEAD_DIM, 1)
    v = lax.dynamic_slice_in_dim(values, group * HEAD_DIM, HEAD_DIM, 1)
    mine = lax.all_gather(jnp.where(odd, v, k), T, axis=0, tiled=True)
    other = lax.ppermute(mine, "y", [(0, 1), (1, 0), (2, 3), (3, 2)])
    return jnp.where(odd, other, mine), jnp.where(odd, mine, other)


def attend(query, k, v, tensor_place):
    block = query.shape[0]
    heads = query.shape[1] // HEAD_DIM
    total = k.shape[0]
    q = query.reshape(block, heads, HEAD_DIM)
    scores = jnp.einsum("qhd,kd->hqk", q, k, preferred_element_type=jnp.float32)
    scores = scores / math.sqrt(HEAD_DIM)
    query_pos = tensor_place * block + jnp.arange(block)
    causal = query_pos[:, None] >= jnp.arange(total)[None, :]
    scores = jnp.where(causal[None], scores, -1e30)
    top = jnp.max(scores, axis=-1, keepdims=True)
    raised = jnp.exp(scores - top)
    probs = (raised / jnp.sum(raised, axis=-1, keepdims=True)).astype(jnp.bfloat16)
    out = jnp.einsum("hqk,kd->qhd", probs, v, preferred_element_type=jnp.float32)
    return out.reshape(block, heads * HEAD_DIM)


def slots_of(ids):
    grid = jnp.arange(EXPERTS, dtype=jnp.int32)
    picked = ids[:, :, None] == grid[None, None, :]
    chosen = jnp.any(picked, axis=1)
    rows = ids.shape[0]
    lower = (jnp.arange(rows)[:, None] > jnp.arange(rows)[None, :]).astype(jnp.bfloat16)
    rank = jnp.dot(lower, chosen.astype(jnp.bfloat16), preferred_element_type=jnp.float32).astype(jnp.int32)
    rank_of = jnp.sum(jnp.where(picked, rank[:, None, :], 0), axis=2)
    return ids * EXP_CAP + rank_of


def per_device(query, keys, values, resid, route_ids, route_weight, w_in, w_down):
    tensor_place = lax.axis_index(T)
    core = lax.axis_index("core")
    block, width = query.shape
    k, v = gather_kv(keys, values)
    attended = attend(query, k, v, tensor_place)
    state = (resid.astype(jnp.float32) + attended).astype(jnp.bfloat16)

    slots = slots_of(route_ids)
    slot_grid = jnp.arange(EXPERTS * EXP_CAP, dtype=jnp.int32)
    takes = (slots[:, :, None] == slot_grid[None, None, :]).astype(jnp.bfloat16)
    sent = jnp.einsum("tps,td->sd", takes, state, preferred_element_type=jnp.float32).astype(jnp.bfloat16)
    rows = lax.all_to_all(
        sent.reshape(EXPERTS, EXP_CAP, width), E, split_axis=0, concat_axis=0, tiled=True
    )
    rows = rows.transpose(1, 0, 2).reshape(EXP_CAP, EXPERTS * width)
    wide = rows.astype(jnp.float32)
    center = jnp.mean(wide, axis=1, keepdims=True)
    variance = jnp.mean((wide - center) ** 2, axis=1, keepdims=True)
    normed = ((wide - center) * lax.rsqrt(variance + 1e-05)).astype(jnp.bfloat16)

    tokens = lax.all_gather(normed, T, axis=0, tiled=True)
    hidden = jnp.dot(tokens, w_in[0], preferred_element_type=jnp.float32)
    hidden = jax.nn.silu(hidden).astype(jnp.bfloat16)
    hidden = hidden.reshape(-1, 2, EXP_CAP, hidden.shape[1])
    z_count = hidden.shape[0]
    theirs = lax.dynamic_index_in_dim(hidden, 1 - core, 1, keepdims=False)
    ours = lax.dynamic_index_in_dim(hidden, core, 1, keepdims=False)
    theirs = theirs.reshape(z_count * EXP_CAP, -1)
    ours = ours.reshape(z_count * EXP_CAP, -1)
    away = jnp.dot(theirs, w_down[0], preferred_element_type=jnp.float32).astype(jnp.bfloat16)
    came = lax.ppermute(away, "core", [(0, 1), (1, 0)])
    here = jnp.dot(ours, w_down[0], preferred_element_type=jnp.float32)
    pair = (here + came.astype(jnp.float32)).astype(jnp.bfloat16)
    summed = lax.psum_scatter(pair, "z", scatter_dimension=0, tiled=True)

    back = summed.reshape(EXP_CAP, EXPERTS, width).transpose(1, 0, 2)
    back = lax.all_to_all(back, E, split_axis=0, concat_axis=0, tiled=True)
    back = back.reshape(EXPERTS * EXP_CAP, width)
    outs = jnp.einsum("tps,sd->tpd", takes, back, preferred_element_type=jnp.float32)
    gates = route_weight / jnp.sum(route_weight, axis=1, keepdims=True)
    mixture = jnp.sum(gates[:, :, None] * outs, axis=1)
    return (state.astype(jnp.float32) + mixture).astype(jnp.bfloat16)


def solution(mesh):
    fine = Mesh(mesh.devices.reshape(4, 4, 16, 2), ("x", "y", "z", "core"))
    placed = (
        P(T, E),
        P(T, None),
        P(T, None),
        P(T, E),
        P(T, None),
        P(T, None),
        P(E, None, T),
        P(E, T, None),
    )
    return jax.shard_map(per_device, mesh=fine, in_specs=placed, out_specs=P(T, E), check_vma=False)
```

time: 366 us -> 274 us (0.75)
  waiting for transfers between devices: 213 us -> 174 us
  blocking collectives: 77 us -> 51.3 us
  local copies, waits for them, and re-layouts: 14.7 us -> 1.77 us
  starting transfers between devices: 20.1 us -> 13 us
  matrix products: 18.8 us -> 14.4 us
    reduce_scatter x1, waiting for transfers between devices: 117 us -> 76.2 us  [per_device(): summed = lax.psum_scatter(pair, 'z', scatter_dimension=0, tiled=True)]
    all_gather x2 -> x1, blocking collectives: 66.1 us -> 37.7 us  [gather_kv(): mine = lax.all_gather(jnp.where(odd, v, k), T, axis=0, tiled=True)]
    ppermute x0 -> x2, waiting for transfers between devices: none -> 17 us  [the longest x1 10.1 us: gather_kv(): other = lax.ppermute(mine, 'y', [(0, 1), (1, 0), (2, 3), (3, 2)])]
    all_to_all x3 -> x1, waiting for transfers between devices: 21.4 us -> 6.37 us  [per_device(): back = lax.all_to_all(back, E, split_axis=0, concat_axis=0, tiled=True)]
    all_to_all x3 -> x1, starting transfers between devices: 19.8 us -> 7.3 us  [per_device(): back = lax.all_to_all(back, E, split_axis=0, concat_axis=0, tiled=True)]
    all_to_all x4 -> x0, local copies, waits for them, and re-layouts: 6.36 us -> none  [the longest x2 5.1 us: per_device(): lax.all_to_all(back_rows, 'expert', split_axis=1, concat_axis=0, tiled=True)]
    ppermute x0 -> x2, starting transfers between devices: none -> 5.62 us  [the longest x1 3.47 us: gather_kv(): other = lax.ppermute(mine, 'y', [(0, 1), (1, 0), (2, 3), (3, 2)])]
    unnamed x11 -> x8, local copies, waits for them, and re-layouts: 4.98 us -> 0.02 us
  transfers between devices with their start and end apart: 5 -> 5, of which waited for: 5 -> 5; matrix products, arithmetic and copies ran while one was open for 0% -> 1% of each run, Pallas kernels for 0% -> 0%
where the time goes in v1:
time: 274 us; the launch traced here: 273 us
  waiting for transfers between devices  174 us (64%)
  blocking collectives  51.3 us (19%)
  matrix products  14.4 us (5%)
  between operations  13.6 us (5%)
  starting transfers between devices  13 us (5%)
  other arithmetic  5.53 us (2%)
    reduce_scatter x1, waiting for transfers between devices, per_device(): summed = lax.psum_scatter(pair, 'z', scatter_dimension=0, tiled=True)  76.2 us
    all_gather x1, waiting for transfers between devices, per_device(): tokens = lax.all_gather(normed, T, axis=0, tiled=True)  73.9 us
    all_gather x1, blocking collectives, gather_kv(): mine = lax.all_gather(jnp.where(odd, v, k), T, axis=0, tiled=True)  37.7 us
    all_to_all x1, blocking collectives, per_device(): lax.all_to_all(sent.reshape(EXPERTS, EXP_CAP, width), E, split_axis=0, co...  13.6 us
    ppermute x1, waiting for transfers between devices, gather_kv(): other = lax.ppermute(mine, 'y', [(0, 1), (1, 0), (2, 3), (3, 2)])  10.1 us
    all_to_all x1, starting transfers between devices, per_device(): back = lax.all_to_all(back, E, split_axis=0, concat_axis=0, tiled=True)  7.3 us
    ppermute x1, waiting for transfers between devices, per_device(): came = lax.ppermute(away, 'core', [(0, 1), (1, 0)])  6.9 us
    all_to_all x1, waiting for transfers between devices, per_device(): back = lax.all_to_all(back, E, split_axis=0, concat_axis=0, tiled=True)  6.37 us
  transfers between devices with their start and end apart: 5, of which 5 were waited for; matrix products, arithmetic and copies ran while one was open for 1% of the time, Pallas kernels for 0%

profile of v1, /device:TPU:6, one launch (start us, length us, event | category | flops | bytes accessed | tf_op | source)
XLA Modules:
  0.0 273.0 jit_solution(12278813830300232545)
XLA Ops:
  6.5 0.0 copy-start
  6.5 0.0 all-gather.2.cloned.1.call-start
  6.5 0.9 dynamic-slice_select_fusion
  7.4 37.7 %all_gather.6 = bf16[2048,128]{1,0:T(8,128)(2,1)S(1)} all-gather(bf16[64,128]{1,0:T(8,128)(2,1)S(1)} %dynamic-slice_select_fusion), channel_id=1, replica_groups=mesh['x'=4,'y'=4,'z'=16,'core'=2] {'z','core'}, dimensions={0}, use_global_device_ids=true | all-gather | bytes 540672 | tf_op jit(solution)/shard_map/all_gather | solution.py:26
  45.1 0.0 copy-start.1
  45.1 3.5 %collective-permute-start = (bf16[2048,128]{1,0:T(8,128)(2,1)S(1)}, bf16[2048,128]{1,0:T(8,128)(2,1)}, u32[]{:S(2)}, u32[]{:S(2)}) collective-permute-start(bf16[2048,128]{1,0:T(8,128)(2,1)S(1)} %all_gather.6), channel_id=1, source_target_pairs={{0,32},{32,0},{64,96},{96,64},{1,33},{33,1},{65,97},{97,65},{2,34}... | collective-permute-start | bytes 1572872 | tf_op jit(solution)/shard_map/ppermute | solution.py:27
  48.6 0.7 fusion.28
  49.3 0.1 convolution_convert_fusion.2
  49.4 0.7 select_reduce_fusion
  50.1 0.7 multiply_add_fusion
  50.8 0.1 convert_reduce_fusion.1
  50.9 0.1 iota_compare_fusion.2
  51.1 0.0 copy-done.1
  51.1 0.0 copy-start.2
  51.1 10.1 %collective-permute-done = bf16[2048,128]{1,0:T(8,128)(2,1)} collective-permute-done((bf16[2048,128]{1,0:T(8,128)(2,1)S(1)}, bf16[2048,128]{1,0:T(8,128)(2,1)}, u32[]{:S(2)}, u32[]{:S(2)}) %collective-permute-start) | collective-permute-done | bytes 524320 | tf_op jit(solution)/shard_map/ppermute | solution.py:27
  61.3 1.4 fusion.4
  62.6 0.3 fusion.31
  63.0 1.5 convolution_bitcast_fusion
  64.5 0.0 copy-done.2
  64.5 0.2 convolution_convert_fusion.1
  64.8 13.6 %all_to_all.10 = bf16[16,32,256]{2,1,0:T(8,128)(2,1)S(1)} all-to-all(bf16[16,32,256]{2,1,0:T(8,128)(2,1)S(1)} %bitcast.68), channel_id=1, replica_groups=mesh['x'=4,'y'=4,'z'=16,'core'=2] {'x','y'}, dimensions={0} | all-to-all | bytes 524288 | tf_op jit(solution)/shard_map/all_to_all | solution.py:71
  78.4 0.2 convert_reduce_fusion
  78.5 0.3 fusion.16
  78.9 0.8 multiply_convert_fusion.1
  79.7 0.0 all-gather.2.cloned.1.call-update
  79.8 0.0 reduce-scatter.2.cloned.1.call-start
  79.8 73.9 %all-gather.2.cloned.1.call-done = bf16[1024,4096]{1,0:T(8,128)(2,1)} async-done(((bf16[32,4096]{1,0:T(8,128)(2,1)}), bf16[1024,4096]{1,0:T(8,128)(2,1)}) %all-gather.2.cloned.1.call-update) | async-done | bytes 8388624 | tf_op jit(solution)/shard_map/all_gather | solution.py:80
  153.8 6.3 %multiply_convert_fusion = bf16[1024,256]{1,0:T(8,128)(2,1)S(1)} fusion(bf16[1024,4096]{1,0:T(8,128)(2,1)} %all-gather.2.cloned.1.call-done, bf16[1,4096,256]{2,1,0:T(8,128)(2,1)} %param.14), kind=kOutput, calls=%fused_computation.18 | convolution fusion | flops 2148794368 | bytes 11010048 | tf_op jit(solution)/shard_map/dot_general | solution.py:81
  160.1 0.0 copy-done
  160.1 1.3 convolution_convert_fusion
  161.4 2.1 collective-permute-start.1
  163.6 6.9 %collective-permute-done.1 = bf16[512,4096]{1,0:T(8,128)(2,1)S(1)} collective-permute-done((bf16[512,4096]{1,0:T(8,128)(2,1)S(1)}, bf16[512,4096]{1,0:T(8,128)(2,1)S(1)}, u32[]{:S(2)}, u32[]{:S(2)}) %collective-permute-start.1) | collective-permute-done | bytes 4194336 | tf_op jit(solution)/shard_map/ppermute | solution.py:90
  170.5 3.2 %add_convert_fusion = bf16[512,4096]{1,0:T(8,128)(2,1)} fusion(bf16[512,4096]{1,0:T(8,128)(2,1)S(1)} %collective-permute-done.1, bf16[512,256]{1,0:T(8,128)(2,1)S(1)} %bitcast.66, bf16[1,256,4096]{2,1,0:T(8,128)(2,1)S(1)} %copy-done), kind=kOutput, calls=%fused_computation.1 | convolution fusion | flops 1080033280 | bytes 10747904 | tf_op jit(solution)/shard_map/dot_general | solution.py:91
  173.7 0.0 copy-start.3
  173.7 0.0 reduce-scatter.2.cloned.1.call-update
  173.7 76.2 %reduce-scatter.2.cloned.1.call-done = bf16[32,4096]{1,0:T(8,128)(2,1)} async-done(((bf16[512,4096]{1,0:T(8,128)(2,1)}), bf16[32,4096]{1,0:T(8,128)(2,1)}) %reduce-scatter.2.cloned.1.call-update) | async-done | bytes 262160 | tf_op jit(solution)/shard_map/reduce_scatter | solution.py:93
  249.9 1.7 copy.42
  251.6 7.3 %all-to-all-start.1 = ((bf16[16,32,256]{2,1,0:T(8,128)(2,1)}), bf16[16,32,256]{2,1,0:T(8,128)(2,1)S(1)}, u32[]{:S(2)}, u32[]{:S(2)}) async-start(bf16[16,32,256]{2,1,0:T(8,128)(2,1)} %bitcast.64), calls=%async_computation.2 | async-start | bytes 524288 | tf_op jit(solution)/shard_map/all_to_all | solution.py:96
  258.9 0.0 copy-done.3
  258.9 6.4 %all-to-all-done.1 = bf16[16,32,256]{2,1,0:T(8,128)(2,1)S(1)} async-done(((bf16[16,32,256]{2,1,0:T(8,128)(2,1)}), bf16[16,32,256]{2,1,0:T(8,128)(2,1)S(1)}, u32[]{:S(2)}, u32[]{:S(2)}) %all-to-all-start.1) | async-done | bytes 262176 | tf_op jit(solution)/shard_map/all_to_all | solution.py:96
  265.3 0.3 fusion.12
  265.6 0.6 add_convert_fusion.1
  (8 shorter events, 0.2 us)
Async XLA Ops:
  6.5 153.6 %copy-start = (bf16[1,256,4096]{2,1,0:T(8,128)(2,1)S(1)}, bf16[1,256,4096]{2,1,0:T(8,128)(2,1)}, u32[]{:S(2)}) copy-start(bf16[1,256,4096]{2,1,0:T(8,128)(2,1)} %param.15) | copy-start | bytes 6291460
  6.5 147.2 %all-gather.2.cloned.1.call-start = ((), (), s32[]{:S(2)}) async-start(), calls=%async_computation.3 | async-start | bytes 8650752 | tf_op jit(solution)/shard_map/all_gather | solution.py:80
  45.1 6.0 %copy-start.1 = (bf16[2048,128]{1,0:T(8,128)(2,1)}, bf16[2048,128]{1,0:T(8,128)(2,1)S(1)}, u32[]{:S(2)}) copy-start(bf16[2048,128]{1,0:T(8,128)(2,1)S(1)} %all_gather.6) | copy-start | bytes 1572868
  45.1 16.2 %collective-permute-start = (bf16[2048,128]{1,0:T(8,128)(2,1)S(1)}, bf16[2048,128]{1,0:T(8,128)(2,1)}, u32[]{:S(2)}, u32[]{:S(2)}) collective-permute-start(bf16[2048,128]{1,0:T(8,128)(2,1)S(1)} %all_gather.6), channel_id=1, source_target_pairs={{0,32},{32,0},{64,96},{96,64},{1,33},{33,1},{65,97},{97,65},{2,34}... | collective-permute-start | bytes 1572872 | tf_op jit(solution)/shard_map/ppermute | solution.py:27
  51.1 13.4 %copy-start.2 = (bf16[64,256]{1,0:T(8,128)(2,1)S(1)}, bf16[64,256]{1,0:T(8,128)(2,1)}, u32[]{:S(2)}) copy-start(bf16[64,256]{1,0:T(8,128)(2,1)} %param.11) | copy-start | bytes 98308
  79.8 170.1 %reduce-scatter.2.cloned.1.call-start = ((), (), s32[]{:S(2)}) async-start(), calls=%async_computation.4 | async-start | bytes 4456448 | tf_op jit(solution)/shard_map/reduce_scatter | solution.py:93
  161.4 9.1 %collective-permute-start.1 = (bf16[512,4096]{1,0:T(8,128)(2,1)S(1)}, bf16[512,4096]{1,0:T(8,128)(2,1)S(1)}, u32[]{:S(2)}, u32[]{:S(2)}) collective-permute-start(bf16[512,4096]{1,0:T(8,128)(2,1)S(1)} %convolution_convert_fusion), channel_id=1, source_target_pairs={{0,1},{1,0},{2,3},{3,2},{4,5},{5,4},{6,7},{7,6},{8,9},{9,8},{10,11... | collective-permute-start | bytes 12582920 | tf_op jit(solution)/shard_map/ppermute | solution.py:90
  173.7 85.2 %copy-start.3 = (f32[64,4]{0,1:T(4,128)S(1)}, f32[64,4]{0,1:T(4,128)}, u32[]{:S(2)}) copy-start(f32[64,4]{0,1:T(4,128)} %param.13) | copy-start | bytes 3076
  251.6 13.7 %all-to-all-start.1 = ((bf16[16,32,256]{2,1,0:T(8,128)(2,1)}), bf16[16,32,256]{2,1,0:T(8,128)(2,1)S(1)}, u32[]{:S(2)}, u32[]{:S(2)}) async-start(bf16[16,32,256]{2,1,0:T(8,128)(2,1)} %bitcast.64), calls=%async_computation.2 | async-start | bytes 524288 | tf_op jit(solution)/shard_map/all_to_all | solution.py:96
Sparse Core Ops, SparseCore 0:
  79.9 73.8 all-gather.1
  173.8 76.0 reduce-scatter.1

commit v2 on v1

--- a/solution.py
+++ b/solution.py
@@ -12,20 +12,77 @@
 EXPERTS = 16
 EXP_CAP = 32
 TOPK = 4
+Z = 16
 
 E = ("x", "y")
 T = ("z", "core")
 
 
+def swap_cores(x):
+    return lax.ppermute(x, "core", [(0, 1), (1, 0)])
+
+
 def gather_kv(keys, values):
-    place = lax.axis_index(E)
-    group = place // 2
-    odd = (place % 2) == 1
+    group = lax.axis_index(E) // 2
+    core = lax.axis_index("core")
     k = lax.dynamic_slice_in_dim(keys, group * HEAD_DIM, HEAD_DIM, 1)
     v = lax.dynamic_slice_in_dim(values, group * HEAD_DIM, HEAD_DIM, 1)
-    mine = lax.all_gather(jnp.where(odd, v, k), T, axis=0, tiled=True)
-    other = lax.ppermute(mine, "y", [(0, 1), (1, 0), (2, 3), (3, 2)])
-    return jnp.where(odd, other, mine), jnp.where(odd, mine, other)
+    first = core == 0
+    came = swap_cores(jnp.where(first, v, k))
+    kept = jnp.where(first, k, v)
+    chip = jnp.concatenate([jnp.where(first, kept, came), jnp.where(first, came, kept)], axis=0)
+    mine = lax.all_gather(chip, "z", axis=0, tiled=True)
+    other = swap_cores(mine)
+    return jnp.where(first, mine, other), jnp.where(first, other, mine)
+
+
+def up(x):
+    return lax.ppermute(x, "z", [(i, (i + 1) % Z) for i in range(Z)])
+
+
+def down(x):
+    return lax.ppermute(x, "z", [((i + 1) % Z, i) for i in range(Z)])
+
+
+def experts(normed, w_in, w_down):
+    w_in = lax.all_gather(w_in, "core", axis=0, tiled=True)
+    w_down = lax.all_gather(w_down, "core", axis=0, tiled=True)
+
+    def share(blocks):
+        rows = jnp.concatenate(blocks, axis=0)
+        hidden = jnp.einsum("rd,cdf->rcf", rows, w_in, preferred_element_type=jnp.float32)
+        hidden = jax.nn.silu(hidden).astype(jnp.bfloat16)
+        out = jnp.einsum("rcf,cfd->rd", hidden, w_down, preferred_element_type=jnp.float32)
+        out = out.astype(jnp.bfloat16)
+        return [out[i * EXP_CAP : (i + 1) * EXP_CAP] for i in range(len(blocks))]
+
+    above, below = Z // 2, Z // 2 - 1
+    from_below, from_above = [normed], [normed]
+    for _ in range(above):
+        from_below.append(up(from_below[-1]))
+        if len(from_above) <= below:
+            from_above.append(down(from_above[-1]))
+    half = above // 2
+    near = from_below[: half + 1] + from_above[1:half]
+    far = from_below[half + 1 :] + from_above[half:]
+    near, far = share(near), share(far)
+    sums_below = near[: half + 1] + far[: above - half]
+    sums_above = near[:1] + near[half + 1 :] + far[above - half :]
+
+    def add(a, b):
+        return (a.astype(jnp.float32) + b.astype(jnp.float32)).astype(jnp.bfloat16)
+
+    low, high = sums_below[above], sums_above[below]
+    for i in range(1, above + 1):
+        low = down(low)
+        if i < above:
+            low = add(low, sums_below[above - i])
+        if i <= below:
+            high = up(high)
+            if i < below:
+                high = add(high, sums_above[below - i])
+    total = near[0].astype(jnp.float32) + low.astype(jnp.float32) + high.astype(jnp.float32)
+    return total.astype(jnp.bfloat16)
 
 
 def attend(query, k, v, tensor_place):
@@ -58,7 +115,6 @@
 
 def per_device(query, keys, values, resid, route_ids, route_weight, w_in, w_down):
     tensor_place = lax.axis_index(T)
-    core = lax.axis_index("core")
     block, width = query.shape
     k, v = gather_kv(keys, values)
     attended = attend(query, k, v, tensor_place)
@@ -77,20 +133,7 @@
     variance = jnp.mean((wide - center) ** 2, axis=1, keepdims=True)
     normed = ((wide - center) * lax.rsqrt(variance + 1e-05)).astype(jnp.bfloat16)
 
-    tokens = lax.all_gather(normed, T, axis=0, tiled=True)
-    hidden = jnp.dot(tokens, w_in[0], preferred_element_type=jnp.float32)
-    hidden = jax.nn.silu(hidden).astype(jnp.bfloat16)
-    hidden = hidden.reshape(-1, 2, EXP_CAP, hidden.shape[1])
-    z_count = hidden.shape[0]
-    theirs = lax.dynamic_index_in_dim(hidden, 1 - core, 1, keepdims=False)
-    ours = lax.dynamic_index_in_dim(hidden, core, 1, keepdims=False)
-    theirs = theirs.reshape(z_count * EXP_CAP, -1)
-    ours = ours.reshape(z_count * EXP_CAP, -1)
-    away = jnp.dot(theirs, w_down[0], preferred_element_type=jnp.float32).astype(jnp.bfloat16)
-    came = lax.ppermute(away, "core", [(0, 1), (1, 0)])
-    here = jnp.dot(ours, w_down[0], preferred_element_type=jnp.float32)
-    pair = (here + came.astype(jnp.float32)).astype(jnp.bfloat16)
-    summed = lax.psum_scatter(pair, "z", scatter_dimension=0, tiled=True)
+    summed = experts(normed, w_in, w_down)
 
     back = summed.reshape(EXP_CAP, EXPERTS, width).transpose(1, 0, 2)
     back = lax.all_to_all(back, E, split_axis=0, concat_axis=0, tiled=True)

time: 274 us -> 284 us (1.036)
  starting transfers between devices: 13 us -> 106 us
  waiting for transfers between devices: 174 us -> 82 us
  local copies, waits for them, and re-layouts: 1.77 us -> 9.11 us
    ppermute x2 -> x32, starting transfers between devices: 5.62 us -> 100 us  [the longest x15 58.3 us: down(): return lax.ppermute(x, 'z', [((i + 1) % Z, i) for i in range(Z)])]
    reduce_scatter x1 -> x0, waiting for transfers between devices: 76.2 us -> none  [per_device(): summed = lax.psum_scatter(pair, 'z', scatter_dimension=0, tiled=True)]
    all_gather x1 -> x2, waiting for transfers between devices: 73.9 us -> 0.01 us  [the longest x1 0.01 us: experts(): w_in = lax.all_gather(w_in, 'core', axis=0, tiled=True)]
    ppermute x2 -> x32, waiting for transfers between devices: 17 us -> 75.6 us  [the longest x15 50.3 us: up(): return lax.ppermute(x, 'z', [(i, (i + 1) % Z) for i in range(Z)])]
    unnamed x8 -> x23, local copies, waits for them, and re-layouts: 0.02 us -> 6.83 us
    dot_general x3 -> x2, matrix products: 10.8 us -> 13.1 us  [share(): jnp.einsum('rcf,cfd->rd', hidden, w_down, preferred_element_type=jnp.floa...]
  transfers between devices with their start and end apart: 5 -> 35, of which waited for: 5 -> 26; matrix products, arithmetic and copies ran while one was open for 1% -> 6% of each run, Pallas kernels for 0% -> 0%
where the time goes in v2:
time: 284 us; the launch traced here: 282 us
  starting transfers between devices  106 us (37%)
  waiting for transfers between devices  82 us (29%)
  blocking collectives  52.1 us (18%)
  matrix products  14.6 us (5%)
  between operations  13.9 us (5%)
  local copies, waits for them, and re-layouts  9.11 us (3%)
  other arithmetic  4.34 us (2%)
    ppermute x15, starting transfers between devices, down(): return lax.ppermute(x, 'z', [((i + 1) % Z, i) for i in range(Z)])  58.3 us
    ppermute x15, waiting for transfers between devices, up(): return lax.ppermute(x, 'z', [(i, (i + 1) % Z) for i in range(Z)])  50.3 us
    all_gather x1, blocking collectives, gather_kv(): mine = lax.all_gather(chip, 'z', axis=0, tiled=True)  38.2 us
    ppermute x15, starting transfers between devices, up(): return lax.ppermute(x, 'z', [(i, (i + 1) % Z) for i in range(Z)])  38.1 us
    ppermute x15, waiting for transfers between devices, down(): return lax.ppermute(x, 'z', [((i + 1) % Z, i) for i in range(Z)])  22.8 us
    all_to_all x1, blocking collectives, per_device(): lax.all_to_all(sent.reshape(EXPERTS, EXP_CAP, width), E, split_axis=0, co...  13.9 us
    dot_general x2, matrix products, share(): jnp.einsum('rcf,cfd->rd', hidden, w_down, preferred_element_type=jnp.floa...  13.1 us
    unnamed x23, local copies, waits for them, and re-layouts  6.83 us
  transfers between devices with their start and end apart: 35, of which 26 were waited for; matrix products, arithmetic and copies ran while one was open for 6% of the time, Pallas kernels for 0%

profile of v2, /device:TPU:6, one launch (start us, length us, event | category | flops | bytes accessed | tf_op | source)
XLA Modules:
  0.0 282.1 jit_solution(18223067124937054372)
XLA Ops:
  6.5 0.8 broadcast_select_fusion.2
  7.3 1.9 collective-permute-start
  10.4 0.8 broadcast_select_fusion.1
  11.2 38.2 %all_gather.9 = bf16[2048,128]{1,0:T(8,128)(2,1)S(1)} all-gather(bf16[128,128]{1,0:T(8,128)(2,1)S(1)} %pad_maximum_fusion), channel_id=1, replica_groups=mesh['x'=4,'y'=4,'z'=16,'core'=2] {'z'}, dimensions={0}, use_global_device_ids=true | all-gather | bytes 557056 | tf_op jit(solution)/shard_map/all_gather | solution.py:34
  49.4 1.9 collective-permute-start.1
  51.4 1.7 collective-permute-done.1
  54.8 13.9 %all_to_all.10 = bf16[16,32,256]{2,1,0:T(8,128)(2,1)S(1)} all-to-all(bf16[16,32,256]{2,1,0:T(8,128)(2,1)S(1)} %bitcast.74), channel_id=1, replica_groups=mesh['x'=4,'y'=4,'z'=16,'core'=2] {'x','y'}, dimensions={0} | all-to-all | bytes 524288 | tf_op jit(solution)/shard_map/all_to_all | solution.py:127
  69.4 1.9 collective-permute-start.2
  71.3 5.1 %collective-permute-start.6 = (bf16[32,4096]{1,0:T(8,128)(2,1)S(1)}, bf16[32,4096]{1,0:T(8,128)(2,1)S(1)}, u32[]{:S(2)}, u32[]{:S(2)}) collective-permute-start(bf16[32,4096]{1,0:T(8,128)(2,1)S(1)} %get-tuple-element.6), channel_id=1, source_target_pairs={{2,0},{4,2},{6,4},{8,6},{10,8},{12,10},{14,12},{16,14},{18,16},{20... | collective-permute-start | bytes 786440 | tf_op jit(solution)/shard_map/ppermute | solution.py:44
  76.5 3.2 %collective-permute-done.2 = bf16[32,4096]{1,0:T(8,128)(2,1)S(1)} collective-permute-done((bf16[32,4096]{1,0:T(8,128)(2,1)S(1)}, bf16[32,4096]{1,0:T(8,128)(2,1)S(1)}, u32[]{:S(2)}, u32[]{:S(2)}) %collective-permute-start.2) | collective-permute-done | bytes 262176 | tf_op jit(solution)/shard_map/ppermute | solution.py:40
  79.7 1.9 collective-permute-start.3
  81.6 5.1 %collective-permute-start.7 = (bf16[32,4096]{1,0:T(8,128)(2,1)S(1)}, bf16[32,4096]{1,0:T(8,128)(2,1)S(1)}, u32[]{:S(2)}, u32[]{:S(2)}) collective-permute-start(bf16[32,4096]{1,0:T(8,128)(2,1)S(1)} %collective-permute-done.6), channel_id=1, source_target_pairs={{2,0},{4,2},{6,4},{8,6},{10,8},{12,10},{14,12},{16,14},{18,16},{20... | collective-permute-start | bytes 786440 | tf_op jit(solution)/shard_map/ppermute | solution.py:44
  86.8 2.4 collective-permute-done.3
  89.1 1.9 collective-permute-start.4
  91.1 5.1 %collective-permute-start.8 = (bf16[32,4096]{1,0:T(8,128)(2,1)S(1)}, bf16[32,4096]{1,0:T(8,128)(2,1)S(1)}, u32[]{:S(2)}, u32[]{:S(2)}) collective-permute-start(bf16[32,4096]{1,0:T(8,128)(2,1)S(1)} %collective-permute-done.7), channel_id=1, source_target_pairs={{2,0},{4,2},{6,4},{8,6},{10,8},{12,10},{14,12},{16,14},{18,16},{20... | collective-permute-start | bytes 786440 | tf_op jit(solution)/shard_map/ppermute | solution.py:44
  96.2 2.4 collective-permute-done.4
  98.6 1.9 collective-permute-start.5
  100.5 5.1 %collective-permute-start.13 = (bf16[32,4096]{1,0:T(8,128)(2,1)S(1)}, bf16[32,4096]{1,0:T(8,128)(2,1)S(1)}, u32[]{:S(2)}, u32[]{:S(2)}) collective-permute-start(bf16[32,4096]{1,0:T(8,128)(2,1)S(1)} %collective-permute-done.8), channel_id=1, source_target_pairs={{2,0},{4,2},{6,4},{8,6},{10,8},{12,10},{14,12},{16,14},{18,16},{20... | collective-permute-start | bytes 786440 | tf_op jit(solution)/shard_map/ppermute | solution.py:44
  105.7 2.4 collective-permute-done.5
  108.1 1.9 collective-permute-start.9
  110.0 5.1 %collective-permute-start.14 = (bf16[32,4096]{1,0:T(8,128)(2,1)S(1)}, bf16[32,4096]{1,0:T(8,128)(2,1)S(1)}, u32[]{:S(2)}, u32[]{:S(2)}) collective-permute-start(bf16[32,4096]{1,0:T(8,128)(2,1)S(1)} %collective-permute-done.13), channel_id=1, source_target_pairs={{2,0},{4,2},{6,4},{8,6},{10,8},{12,10},{14,12},{16,14},{18,16},{20... | collective-permute-start | bytes 786440 | tf_op jit(solution)/shard_map/ppermute | solution.py:44
  115.2 3.1 %collective-permute-done.9 = bf16[32,4096]{1,0:T(8,128)(2,1)S(1)} collective-permute-done((bf16[32,4096]{1,0:T(8,128)(2,1)S(1)}, bf16[32,4096]{1,0:T(8,128)(2,1)S(1)}, u32[]{:S(2)}, u32[]{:S(2)}) %collective-permute-start.9) | collective-permute-done | bytes 262176 | tf_op jit(solution)/shard_map/ppermute | solution.py:40
  118.3 1.9 collective-permute-start.10
  120.2 5.4 %collective-permute-start.15 = (bf16[32,4096]{1,0:T(8,128)(2,1)S(1)}, bf16[32,4096]{1,0:T(8,128)(2,1)S(1)}, u32[]{:S(2)}, u32[]{:S(2)}) collective-permute-start(bf16[32,4096]{1,0:T(8,128)(2,1)S(1)} %collective-permute-done.14), channel_id=1, source_target_pairs={{2,0},{4,2},{6,4},{8,6},{10,8},{12,10},{14,12},{16,14},{18,16},{20... | collective-permute-start | bytes 786440 | tf_op jit(solution)/shard_map/ppermute | solution.py:44
  126.4 3.4 %collective-permute-done.10 = bf16[32,4096]{1,0:T(8,128)(2,1)S(1)} collective-permute-done((bf16[32,4096]{1,0:T(8,128)(2,1)S(1)}, bf16[32,4096]{1,0:T(8,128)(2,1)S(1)}, u32[]{:S(2)}, u32[]{:S(2)}) %collective-permute-start.10) | collective-permute-done | bytes 262176 | tf_op jit(solution)/shard_map/ppermute | solution.py:40
  129.7 1.9 collective-permute-start.11
  131.8 5.6 %collective-permute-start.16 = (bf16[32,4096]{1,0:T(8,128)(2,1)S(1)}, bf16[32,4096]{1,0:T(8,128)(2,1)S(1)}, u32[]{:S(2)}, u32[]{:S(2)}) collective-permute-start(bf16[32,4096]{1,0:T(8,128)(2,1)S(1)} %collective-permute-done.15), channel_id=1, source_target_pairs={{2,0},{4,2},{6,4},{8,6},{10,8},{12,10},{14,12},{16,14},{18,16},{20... | collective-permute-start | bytes 786440 | tf_op jit(solution)/shard_map/ppermute | solution.py:44
  138.1 3.6 %collective-permute-done.11 = bf16[32,4096]{1,0:T(8,128)(2,1)S(1)} collective-permute-done((bf16[32,4096]{1,0:T(8,128)(2,1)S(1)}, bf16[32,4096]{1,0:T(8,128)(2,1)S(1)}, u32[]{:S(2)}, u32[]{:S(2)}) %collective-permute-start.11) | collective-permute-done | bytes 262176 | tf_op jit(solution)/shard_map/ppermute | solution.py:40
  141.7 1.9 collective-permute-start.12
  144.4 6.8 %collective-permute-done.12 = bf16[32,4096]{1,0:T(8,128)(2,1)S(1)} collective-permute-done((bf16[32,4096]{1,0:T(8,128)(2,1)S(1)}, bf16[32,4096]{1,0:T(8,128)(2,1)S(1)}, u32[]{:S(2)}, u32[]{:S(2)}) %collective-permute-start.12) | collective-permute-done | bytes 262176 | tf_op jit(solution)/shard_map/ppermute | solution.py:40
  154.8 6.6 %fusion.2 = bf16[256,4096]{1,0:T(8,128)(2,1)S(1)} fusion(bf16[2,256,4096]{2,1,0:T(8,128)(2,1)} %all-gather.5.cloned.1.call-done, bf16[2,4096,256]{2,1,0:T(8,128)(2,1)} %all-gather.3.cloned.1.call-done, bf16[256,4096]{1,0:T(8,128)(2,1)} %constant_dynamic-update-slice_fusion.8), kind=kOutput, calls=%fused_computation.4 | convolution fusion | flops 2149187584 | bytes 12582912 | tf_op jit(solution)/shard_map/rcf,cfd->rd/dot_general | solution.py:55
  161.4 1.9 collective-permute-start.17
  163.3 3.9 %collective-permute-start.25 = (bf16[32,4096]{1,0:T(8,128)(2,1)S(1)}, bf16[32,4096]{1,0:T(8,128)(2,1)S(1)}, u32[]{:S(2)}, u32[]{:S(2)}) collective-permute-start(bf16[32,4096]{1,0:T(8,128)(2,1)S(1)} %get-tuple-element.20), channel_id=1, source_target_pairs={{0,2},{2,4},{4,6},{6,8},{8,10},{10,12},{12,14},{14,16},{16,18},{18... | collective-permute-start | bytes 786440 | tf_op jit(solution)/shard_map/ppermute | solution.py:40
  168.0 4.3 %collective-permute-done.17 = bf16[32,4096]{1,0:T(8,128)(2,1)S(1)} collective-permute-done((bf16[32,4096]{1,0:T(8,128)(2,1)S(1)}, bf16[32,4096]{1,0:T(8,128)(2,1)S(1)}, u32[]{:S(2)}, u32[]{:S(2)}) %collective-permute-start.17) | collective-permute-done | bytes 262176 | tf_op jit(solution)/shard_map/ppermute | solution.py:44
  172.2 3.1 %collective-permute-done.25 = bf16[32,4096]{1,0:T(8,128)(2,1)S(1)} collective-permute-done((bf16[32,4096]{1,0:T(8,128)(2,1)S(1)}, bf16[32,4096]{1,0:T(8,128)(2,1)S(1)}, u32[]{:S(2)}, u32[]{:S(2)}) %collective-permute-start.25) | collective-permute-done | bytes 262176 | tf_op jit(solution)/shard_map/ppermute | solution.py:40
  175.5 1.9 collective-permute-start.18
  177.4 3.9 %collective-permute-start.26 = (bf16[32,4096]{1,0:T(8,128)(2,1)S(1)}, bf16[32,4096]{1,0:T(8,128)(2,1)S(1)}, u32[]{:S(2)}, u32[]{:S(2)}) collective-permute-start(bf16[32,4096]{1,0:T(8,128)(2,1)S(1)} %get-tuple-element.18), channel_id=1, source_target_pairs={{0,2},{2,4},{4,6},{6,8},{8,10},{10,12},{12,14},{14,16},{16,18},{18... | collective-permute-start | bytes 786440 | tf_op jit(solution)/shard_map/ppermute | solution.py:40
  182.1 3.4 %collective-permute-done.18 = bf16[32,4096]{1,0:T(8,128)(2,1)S(1)} collective-permute-done((bf16[32,4096]{1,0:T(8,128)(2,1)S(1)}, bf16[32,4096]{1,0:T(8,128)(2,1)S(1)}, u32[]{:S(2)}, u32[]{:S(2)}) %collective-permute-start.18) | collective-permute-done | bytes 262176 | tf_op jit(solution)/shard_map/ppermute | solution.py:44
  185.5 3.1 %collective-permute-done.26 = bf16[32,4096]{1,0:T(8,128)(2,1)S(1)} collective-permute-done((bf16[32,4096]{1,0:T(8,128)(2,1)S(1)}, bf16[32,4096]{1,0:T(8,128)(2,1)S(1)}, u32[]{:S(2)}, u32[]{:S(2)}) %collective-permute-start.26) | collective-permute-done | bytes 262176 | tf_op jit(solution)/shard_map/ppermute | solution.py:40
  188.7 2.9 %collective-permute-start.19 = (bf16[32,4096]{1,0:T(8,128)(2,1)S(1)}, bf16[32,4096]{1,0:T(8,128)(2,1)S(1)}, u32[]{:S(2)}, u32[]{:S(2)}) collective-permute-start(bf16[32,4096]{1,0:T(8,128)(2,1)S(1)} %get-tuple-element.15), channel_id=1, source_target_pairs={{2,0},{4,2},{6,4},{8,6},{10,8},{12,10},{14,12},{16,14},{18,16},{20... | collective-permute-start | bytes 786440 | tf_op jit(solution)/shard_map/ppermute | solution.py:44
  191.6 3.0 %collective-permute-start.27 = (bf16[32,4096]{1,0:T(8,128)(2,1)S(1)}, bf16[32,4096]{1,0:T(8,128)(2,1)S(1)}, u32[]{:S(2)}, u32[]{:S(2)}) collective-permute-start(bf16[32,4096]{1,0:T(8,128)(2,1)S(1)} %get-tuple-element.16), channel_id=1, source_target_pairs={{0,2},{2,4},{4,6},{6,8},{8,10},{10,12},{12,14},{14,16},{16,18},{18... | collective-permute-start | bytes 786440 | tf_op jit(solution)/shard_map/ppermute | solution.py:40
  195.3 2.5 collective-permute-done.19
  197.9 3.2 %collective-permute-done.27 = bf16[32,4096]{1,0:T(8,128)(2,1)S(1)} collective-permute-done((bf16[32,4096]{1,0:T(8,128)(2,1)S(1)}, bf16[32,4096]{1,0:T(8,128)(2,1)S(1)}, u32[]{:S(2)}, u32[]{:S(2)}) %collective-permute-start.27) | collective-permute-done | bytes 262176 | tf_op jit(solution)/shard_map/ppermute | solution.py:40
  201.2 1.9 collective-permute-start.20
  203.2 6.6 %fusion.1 = bf16[256,4096]{1,0:T(8,128)(2,1)S(1)} fusion(bf16[2,256,4096]{2,1,0:T(8,128)(2,1)} %all-gather.5.cloned.1.call-done, bf16[2,4096,256]{2,1,0:T(8,128)(2,1)} %all-gather.3.cloned.1.call-done, bf16[256,4096]{1,0:T(8,128)(2,1)} %constant_dynamic-update-slice_fusion), kind=kOutput, calls=%fused_computation.3 | convolution fusion | flops 2149187584 | bytes 12582912 | tf_op jit(solution)/shard_map/rcf,cfd->rd/dot_general | solution.py:55
  209.7 3.9 %collective-permute-start.28 = (bf16[32,4096]{1,0:T(8,128)(2,1)S(1)}, bf16[32,4096]{1,0:T(8,128)(2,1)S(1)}, u32[]{:S(2)}, u32[]{:S(2)}) collective-permute-start(bf16[32,4096]{1,0:T(8,128)(2,1)S(1)} %get-tuple-element.14), channel_id=1, source_target_pairs={{0,2},{2,4},{4,6},{6,8},{8,10},{10,12},{12,14},{14,16},{16,18},{18... | collective-permute-start | bytes 786440 | tf_op jit(solution)/shard_map/ppermute | solution.py:40
  213.7 3.1 %collective-permute-start.21 = (bf16[32,4096]{1,0:T(8,128)(2,1)S(1)}, bf16[32,4096]{1,0:T(8,128)(2,1)S(1)}, u32[]{:S(2)}, u32[]{:S(2)}) collective-permute-start(bf16[32,4096]{1,0:T(8,128)(2,1)S(1)} %add_convert_fusion.10), channel_id=1, source_target_pairs={{2,0},{4,2},{6,4},{8,6},{10,8},{12,10},{14,12},{16,14},{18,16},{20... | collective-permute-start | bytes 786440 | tf_op jit(solution)/shard_map/ppermute | solution.py:44
  216.9 2.3 collective-permute-done.28
  219.2 2.8 collective-permute-done.21
  222.1 4.3 %collective-permute-start.22 = (bf16[32,4096]{1,0:T(8,128)(2,1)S(1)}, bf16[32,4096]{1,0:T(8,128)(2,1)S(1)}, u32[]{:S(2)}, u32[]{:S(2)}) collective-permute-start(bf16[32,4096]{1,0:T(8,128)(2,1)S(1)} %get-tuple-element.11), channel_id=1, source_target_pairs={{2,0},{4,2},{6,4},{8,6},{10,8},{12,10},{14,12},{16,14},{18,16},{20... | collective-permute-start | bytes 786440 | tf_op jit(solution)/shard_map/ppermute | solution.py:44
  226.5 1.9 collective-permute-start.29
  228.4 4.7 %collective-permute-done.22 = bf16[32,4096]{1,0:T(8,128)(2,1)S(1)} collective-permute-done((bf16[32,4096]{1,0:T(8,128)(2,1)S(1)}, bf16[32,4096]{1,0:T(8,128)(2,1)S(1)}, u32[]{:S(2)}, u32[]{:S(2)}) %collective-permute-start.22) | collective-permute-done | bytes 262176 | tf_op jit(solution)/shard_map/ppermute | solution.py:44
  233.1 3.3 %collective-permute-done.29 = bf16[32,4096]{1,0:T(8,128)(2,1)S(1)} collective-permute-done((bf16[32,4096]{1,0:T(8,128)(2,1)S(1)}, bf16[32,4096]{1,0:T(8,128)(2,1)S(1)}, u32[]{:S(2)}, u32[]{:S(2)}) %collective-permute-start.29) | collective-permute-done | bytes 262176 | tf_op jit(solution)/shard_map/ppermute | solution.py:40
  236.6 1.9 collective-permute-start.23
  238.5 3.9 %collective-permute-start.30 = (bf16[32,4096]{1,0:T(8,128)(2,1)S(1)}, bf16[32,4096]{1,0:T(8,128)(2,1)S(1)}, u32[]{:S(2)}, u32[]{:S(2)}) collective-permute-start(bf16[32,4096]{1,0:T(8,128)(2,1)S(1)} %get-tuple-element.10), channel_id=1, source_target_pairs={{0,2},{2,4},{4,6},{6,8},{8,10},{10,12},{12,14},{14,16},{16,18},{18... | collective-permute-start | bytes 786440 | tf_op jit(solution)/shard_map/ppermute | solution.py:40
  242.4 2.6 collective-permute-done.23
  245.0 3.1 %collective-permute-done.30 = bf16[32,4096]{1,0:T(8,128)(2,1)S(1)} collective-permute-done((bf16[32,4096]{1,0:T(8,128)(2,1)S(1)}, bf16[32,4096]{1,0:T(8,128)(2,1)S(1)}, u32[]{:S(2)}, u32[]{:S(2)}) %collective-permute-start.30) | collective-permute-done | bytes 262176 | tf_op jit(solution)/shard_map/ppermute | solution.py:40
  248.2 3.6 %collective-permute-start.24 = (bf16[32,4096]{1,0:T(8,128)(2,1)S(1)}, bf16[32,4096]{1,0:T(8,128)(2,1)S(1)}, u32[]{:S(2)}, u32[]{:S(2)}) collective-permute-start(bf16[32,4096]{1,0:T(8,128)(2,1)S(1)} %get-tuple-element.7), channel_id=1, source_target_pairs={{2,0},{4,2},{6,4},{8,6},{10,8},{12,10},{14,12},{16,14},{18,16},{20... | collective-permute-start | bytes 786440 | tf_op jit(solution)/shard_map/ppermute | solution.py:44
  251.9 2.2 collective-permute-start.31
  254.1 2.4 collective-permute-done.24
  256.5 4.9 %collective-permute-done.31 = bf16[32,4096]{1,0:T(8,128)(2,1)S(1)} collective-permute-done((bf16[32,4096]{1,0:T(8,128)(2,1)S(1)}, bf16[32,4096]{1,0:T(8,128)(2,1)S(1)}, u32[]{:S(2)}, u32[]{:S(2)}) %collective-permute-start.31) | collective-permute-done | bytes 262176 | tf_op jit(solution)/shard_map/ppermute | solution.py:40
  261.5 0.7 copy.43
  262.2 5.7 %all-to-all-start.1 = ((bf16[16,32,256]{2,1,0:T(8,128)(2,1)}), bf16[16,32,256]{2,1,0:T(8,128)(2,1)S(1)}, u32[]{:S(2)}, u32[]{:S(2)}) async-start(bf16[16,32,256]{2,1,0:T(8,128)(2,1)} %bitcast.72), calls=%async_computation.1 | async-start | bytes 524288 | tf_op jit(solution)/shard_map/all_to_all | solution.py:139
  268.0 6.4 %all-to-all-done.1 = bf16[16,32,256]{2,1,0:T(8,128)(2,1)S(1)} async-done(((bf16[16,32,256]{2,1,0:T(8,128)(2,1)}), bf16[16,32,256]{2,1,0:T(8,128)(2,1)S(1)}, u32[]{:S(2)}, u32[]{:S(2)}) %all-to-all-start.1) | async-done | bytes 262176 | tf_op jit(solution)/shard_map/all_to_all | solution.py:139
  (72 shorter events, 13.6 us)
Async XLA Ops:
  6.5 46.6 %copy-start = (bf16[64,256]{1,0:T(8,128)(2,1)S(1)}, bf16[64,256]{1,0:T(8,128)(2,1)}, u32[]{:S(2)}) copy-start(bf16[64,256]{1,0:T(8,128)(2,1)} %param.8) | copy-start | bytes 98308
  6.5 2.8 copy-start.3
  6.5 148.3 %all-gather.3.cloned.1.call-start = ((), (), s32[]{:S(2)}) async-start(), calls=%async_computation.2 | async-start | bytes 6291456 | tf_op jit(solution)/shard_map/all_gather | solution.py:48
  7.3 3.1 %collective-permute-start = (bf16[64,128]{1,0:T(8,128)(2,1)S(1)}, bf16[64,128]{1,0:T(8,128)(2,1)S(1)}, u32[]{:S(2)}, u32[]{:S(2)}) collective-permute-start(bf16[64,128]{1,0:T(8,128)(2,1)S(1)} %broadcast_select_fusion.2), channel_id=1, source_target_pairs={{0,1},{1,0},{2,3},{3,2},{4,5},{5,4},{6,7},{7,6},{8,9},{9,8},{10,11... | collective-permute-start | bytes 49160 | tf_op jit(solution)/shard_map/ppermute | solution.py:22
  9.3 145.5 %all-gather.5.cloned.1.call-start = ((), (), s32[]{:S(2)}) async-start(), calls=%async_computation.3 | async-start | bytes 6291456 | tf_op jit(solution)/shard_map/all_gather | solution.py:49
  49.4 3.8 %collective-permute-start.1 = (bf16[2048,128]{1,0:T(8,128)(2,1)S(1)}, bf16[2048,128]{1,0:T(8,128)(2,1)S(1)}, u32[]{:S(2)}, u32[]{:S(2)}) collective-permute-start(bf16[2048,128]{1,0:T(8,128)(2,1)S(1)} %all_gather.9), channel_id=1, source_target_pairs={{0,1},{1,0},{2,3},{3,2},{4,5},{5,4},{6,7},{7,6},{8,9},{9,8},{10,11... | collective-permute-start | bytes 1572872 | tf_op jit(solution)/shard_map/ppermute | solution.py:22
  53.8 0.8 copy-start.1
  69.4 10.3 %collective-permute-start.2 = (bf16[32,4096]{1,0:T(8,128)(2,1)S(1)}, bf16[32,4096]{1,0:T(8,128)(2,1)S(1)}, u32[]{:S(2)}, u32[]{:S(2)}) collective-permute-start(bf16[32,4096]{1,0:T(8,128)(2,1)S(1)} %get-tuple-element.6), channel_id=1, source_target_pairs={{0,2},{2,4},{4,6},{6,8},{8,10},{10,12},{12,14},{14,16},{16,18},{18... | collective-permute-start | bytes 786440 | tf_op jit(solution)/shard_map/ppermute | solution.py:40
  71.3 10.3 %collective-permute-start.6 = (bf16[32,4096]{1,0:T(8,128)(2,1)S(1)}, bf16[32,4096]{1,0:T(8,128)(2,1)S(1)}, u32[]{:S(2)}, u32[]{:S(2)}) collective-permute-start(bf16[32,4096]{1,0:T(8,128)(2,1)S(1)} %get-tuple-element.6), channel_id=1, source_target_pairs={{2,0},{4,2},{6,4},{8,6},{10,8},{12,10},{14,12},{16,14},{18,16},{20... | collective-permute-start | bytes 786440 | tf_op jit(solution)/shard_map/ppermute | solution.py:44
  79.7 9.5 %collective-permute-start.3 = (bf16[32,4096]{1,0:T(8,128)(2,1)S(1)}, bf16[32,4096]{1,0:T(8,128)(2,1)S(1)}, u32[]{:S(2)}, u32[]{:S(2)}) collective-permute-start(bf16[32,4096]{1,0:T(8,128)(2,1)S(1)} %collective-permute-done.2), channel_id=1, source_target_pairs={{0,2},{2,4},{4,6},{6,8},{8,10},{10,12},{12,14},{14,16},{16,18},{18... | collective-permute-start | bytes 786440 | tf_op jit(solution)/shard_map/ppermute | solution.py:40
  81.6 9.5 %collective-permute-start.7 = (bf16[32,4096]{1,0:T(8,128)(2,1)S(1)}, bf16[32,4096]{1,0:T(8,128)(2,1)S(1)}, u32[]{:S(2)}, u32[]{:S(2)}) collective-permute-start(bf16[32,4096]{1,0:T(8,128)(2,1)S(1)} %collective-permute-done.6), channel_id=1, source_target_pairs={{2,0},{4,2},{6,4},{8,6},{10,8},{12,10},{14,12},{16,14},{18,16},{20... | collective-permute-start | bytes 786440 | tf_op jit(solution)/shard_map/ppermute | solution.py:44
  89.1 9.5 %collective-permute-start.4 = (bf16[32,4096]{1,0:T(8,128)(2,1)S(1)}, bf16[32,4096]{1,0:T(8,128)(2,1)S(1)}, u32[]{:S(2)}, u32[]{:S(2)}) collective-permute-start(bf16[32,4096]{1,0:T(8,128)(2,1)S(1)} %collective-permute-done.3), channel_id=1, source_target_pairs={{0,2},{2,4},{4,6},{6,8},{8,10},{10,12},{12,14},{14,16},{16,18},{18... | collective-permute-start | bytes 786440 | tf_op jit(solution)/shard_map/ppermute | solution.py:40
  91.1 9.5 %collective-permute-start.8 = (bf16[32,4096]{1,0:T(8,128)(2,1)S(1)}, bf16[32,4096]{1,0:T(8,128)(2,1)S(1)}, u32[]{:S(2)}, u32[]{:S(2)}) collective-permute-start(bf16[32,4096]{1,0:T(8,128)(2,1)S(1)} %collective-permute-done.7), channel_id=1, source_target_pairs={{2,0},{4,2},{6,4},{8,6},{10,8},{12,10},{14,12},{16,14},{18,16},{20... | collective-permute-start | bytes 786440 | tf_op jit(solution)/shard_map/ppermute | solution.py:44
  98.6 9.5 %collective-permute-start.5 = (bf16[32,4096]{1,0:T(8,128)(2,1)S(1)}, bf16[32,4096]{1,0:T(8,128)(2,1)S(1)}, u32[]{:S(2)}, u32[]{:S(2)}) collective-permute-start(bf16[32,4096]{1,0:T(8,128)(2,1)S(1)} %collective-permute-done.4), channel_id=1, source_target_pairs={{0,2},{2,4},{4,6},{6,8},{8,10},{10,12},{12,14},{14,16},{16,18},{18... | collective-permute-start | bytes 786440 | tf_op jit(solution)/shard_map/ppermute | solution.py:40
  100.5 9.5 %collective-permute-start.13 = (bf16[32,4096]{1,0:T(8,128)(2,1)S(1)}, bf16[32,4096]{1,0:T(8,128)(2,1)S(1)}, u32[]{:S(2)}, u32[]{:S(2)}) collective-permute-start(bf16[32,4096]{1,0:T(8,128)(2,1)S(1)} %collective-permute-done.8), channel_id=1, source_target_pairs={{2,0},{4,2},{6,4},{8,6},{10,8},{12,10},{14,12},{16,14},{18,16},{20... | collective-permute-start | bytes 786440 | tf_op jit(solution)/shard_map/ppermute | solution.py:44
  108.1 10.3 %collective-permute-start.9 = (bf16[32,4096]{1,0:T(8,128)(2,1)S(1)}, bf16[32,4096]{1,0:T(8,128)(2,1)S(1)}, u32[]{:S(2)}, u32[]{:S(2)}) collective-permute-start(bf16[32,4096]{1,0:T(8,128)(2,1)S(1)} %collective-permute-done.5), channel_id=1, source_target_pairs={{0,2},{2,4},{4,6},{6,8},{8,10},{10,12},{12,14},{14,16},{16,18},{18... | collective-permute-start | bytes 786440 | tf_op jit(solution)/shard_map/ppermute | solution.py:40
  110.0 10.2 %collective-permute-start.14 = (bf16[32,4096]{1,0:T(8,128)(2,1)S(1)}, bf16[32,4096]{1,0:T(8,128)(2,1)S(1)}, u32[]{:S(2)}, u32[]{:S(2)}) collective-permute-start(bf16[32,4096]{1,0:T(8,128)(2,1)S(1)} %collective-permute-done.13), channel_id=1, source_target_pairs={{2,0},{4,2},{6,4},{8,6},{10,8},{12,10},{14,12},{16,14},{18,16},{20... | collective-permute-start | bytes 786440 | tf_op jit(solution)/shard_map/ppermute | solution.py:44
  115.2 39.6 %copy-start.2 = (bf16[256,4096]{1,0:T(8,128)(2,1)}, bf16[256,4096]{1,0:T(8,128)(2,1)S(1)}, u32[]{:S(2)}) copy-start(bf16[256,4096]{1,0:T(8,128)(2,1)S(1)} %constant_dynamic-update-slice_fusion.3) | copy-start | bytes 6291460
  118.3 11.4 %collective-permute-start.10 = (bf16[32,4096]{1,0:T(8,128)(2,1)S(1)}, bf16[32,4096]{1,0:T(8,128)(2,1)S(1)}, u32[]{:S(2)}, u32[]{:S(2)}) collective-permute-start(bf16[32,4096]{1,0:T(8,128)(2,1)S(1)} %collective-permute-done.9), channel_id=1, source_target_pairs={{0,2},{2,4},{4,6},{6,8},{8,10},{10,12},{12,14},{14,16},{16,18},{18... | collective-permute-start | bytes 786440 | tf_op jit(solution)/shard_map/ppermute | solution.py:40
  120.2 11.6 %collective-permute-start.15 = (bf16[32,4096]{1,0:T(8,128)(2,1)S(1)}, bf16[32,4096]{1,0:T(8,128)(2,1)S(1)}, u32[]{:S(2)}, u32[]{:S(2)}) collective-permute-start(bf16[32,4096]{1,0:T(8,128)(2,1)S(1)} %collective-permute-done.14), channel_id=1, source_target_pairs={{2,0},{4,2},{6,4},{8,6},{10,8},{12,10},{14,12},{16,14},{18,16},{20... | collective-permute-start | bytes 786440 | tf_op jit(solution)/shard_map/ppermute | solution.py:44
  129.7 12.0 %collective-permute-start.11 = (bf16[32,4096]{1,0:T(8,128)(2,1)S(1)}, bf16[32,4096]{1,0:T(8,128)(2,1)S(1)}, u32[]{:S(2)}, u32[]{:S(2)}) collective-permute-start(bf16[32,4096]{1,0:T(8,128)(2,1)S(1)} %collective-permute-done.10), channel_id=1, source_target_pairs={{0,2},{2,4},{4,6},{6,8},{8,10},{10,12},{12,14},{14,16},{16,18},{18... | collective-permute-start | bytes 786440 | tf_op jit(solution)/shard_map/ppermute | solution.py:40
  131.8 22.2 %collective-permute-start.16 = (bf16[32,4096]{1,0:T(8,128)(2,1)S(1)}, bf16[32,4096]{1,0:T(8,128)(2,1)S(1)}, u32[]{:S(2)}, u32[]{:S(2)}) collective-permute-start(bf16[32,4096]{1,0:T(8,128)(2,1)S(1)} %collective-permute-done.15), channel_id=1, source_target_pairs={{2,0},{4,2},{6,4},{8,6},{10,8},{12,10},{14,12},{16,14},{18,16},{20... | collective-permute-start | bytes 786440 | tf_op jit(solution)/shard_map/ppermute | solution.py:44
  141.7 9.5 %collective-permute-start.12 = (bf16[32,4096]{1,0:T(8,128)(2,1)S(1)}, bf16[32,4096]{1,0:T(8,128)(2,1)S(1)}, u32[]{:S(2)}, u32[]{:S(2)}) collective-permute-start(bf16[32,4096]{1,0:T(8,128)(2,1)S(1)} %collective-permute-done.11), channel_id=1, source_target_pairs={{0,2},{2,4},{4,6},{6,8},{8,10},{10,12},{12,14},{14,16},{16,18},{18... | collective-permute-start | bytes 786440 | tf_op jit(solution)/shard_map/ppermute | solution.py:40
  161.4 10.8 %collective-permute-start.17 = (bf16[32,4096]{1,0:T(8,128)(2,1)S(1)}, bf16[32,4096]{1,0:T(8,128)(2,1)S(1)}, u32[]{:S(2)}, u32[]{:S(2)}) collective-permute-start(bf16[32,4096]{1,0:T(8,128)(2,1)S(1)} %get-tuple-element.19), channel_id=1, source_target_pairs={{2,0},{4,2},{6,4},{8,6},{10,8},{12,10},{14,12},{16,14},{18,16},{20... | collective-permute-start | bytes 786440 | tf_op jit(solution)/shard_map/ppermute | solution.py:44
  163.3 12.0 %collective-permute-start.25 = (bf16[32,4096]{1,0:T(8,128)(2,1)S(1)}, bf16[32,4096]{1,0:T(8,128)(2,1)S(1)}, u32[]{:S(2)}, u32[]{:S(2)}) collective-permute-start(bf16[32,4096]{1,0:T(8,128)(2,1)S(1)} %get-tuple-element.20), channel_id=1, source_target_pairs={{0,2},{2,4},{4,6},{6,8},{8,10},{10,12},{12,14},{14,16},{16,18},{18... | collective-permute-start | bytes 786440 | tf_op jit(solution)/shard_map/ppermute | solution.py:40
  175.5 10.0 %collective-permute-start.18 = (bf16[32,4096]{1,0:T(8,128)(2,1)S(1)}, bf16[32,4096]{1,0:T(8,128)(2,1)S(1)}, u32[]{:S(2)}, u32[]{:S(2)}) collective-permute-start(bf16[32,4096]{1,0:T(8,128)(2,1)S(1)} %get-tuple-element.17), channel_id=1, source_target_pairs={{2,0},{4,2},{6,4},{8,6},{10,8},{12,10},{14,12},{16,14},{18,16},{20... | collective-permute-start | bytes 786440 | tf_op jit(solution)/shard_map/ppermute | solution.py:44
  177.4 11.2 %collective-permute-start.26 = (bf16[32,4096]{1,0:T(8,128)(2,1)S(1)}, bf16[32,4096]{1,0:T(8,128)(2,1)S(1)}, u32[]{:S(2)}, u32[]{:S(2)}) collective-permute-start(bf16[32,4096]{1,0:T(8,128)(2,1)S(1)} %get-tuple-element.18), channel_id=1, source_target_pairs={{0,2},{2,4},{4,6},{6,8},{8,10},{10,12},{12,14},{14,16},{16,18},{18... | collective-permute-start | bytes 786440 | tf_op jit(solution)/shard_map/ppermute | solution.py:40
  188.7 9.1 %collective-permute-start.19 = (bf16[32,4096]{1,0:T(8,128)(2,1)S(1)}, bf16[32,4096]{1,0:T(8,128)(2,1)S(1)}, u32[]{:S(2)}, u32[]{:S(2)}) collective-permute-start(bf16[32,4096]{1,0:T(8,128)(2,1)S(1)} %get-tuple-element.15), channel_id=1, source_target_pairs={{2,0},{4,2},{6,4},{8,6},{10,8},{12,10},{14,12},{16,14},{18,16},{20... | collective-permute-start | bytes 786440 | tf_op jit(solution)/shard_map/ppermute | solution.py:44
  191.6 9.5 %collective-permute-start.27 = (bf16[32,4096]{1,0:T(8,128)(2,1)S(1)}, bf16[32,4096]{1,0:T(8,128)(2,1)S(1)}, u32[]{:S(2)}, u32[]{:S(2)}) collective-permute-start(bf16[32,4096]{1,0:T(8,128)(2,1)S(1)} %get-tuple-element.16), channel_id=1, source_target_pairs={{0,2},{2,4},{4,6},{6,8},{8,10},{10,12},{12,14},{14,16},{16,18},{18... | collective-permute-start | bytes 786440 | tf_op jit(solution)/shard_map/ppermute | solution.py:40
  201.2 12.4 %collective-permute-start.20 = (bf16[32,4096]{1,0:T(8,128)(2,1)S(1)}, bf16[32,4096]{1,0:T(8,128)(2,1)S(1)}, u32[]{:S(2)}, u32[]{:S(2)}) collective-permute-start(bf16[32,4096]{1,0:T(8,128)(2,1)S(1)} %get-tuple-element.13), channel_id=1, source_target_pairs={{2,0},{4,2},{6,4},{8,6},{10,8},{12,10},{14,12},{16,14},{18,16},{20... | collective-permute-start | bytes 786440 | tf_op jit(solution)/shard_map/ppermute | solution.py:44
  209.7 9.5 %collective-permute-start.28 = (bf16[32,4096]{1,0:T(8,128)(2,1)S(1)}, bf16[32,4096]{1,0:T(8,128)(2,1)S(1)}, u32[]{:S(2)}, u32[]{:S(2)}) collective-permute-start(bf16[32,4096]{1,0:T(8,128)(2,1)S(1)} %get-tuple-element.14), channel_id=1, source_target_pairs={{0,2},{2,4},{4,6},{6,8},{8,10},{10,12},{12,14},{14,16},{16,18},{18... | collective-permute-start | bytes 786440 | tf_op jit(solution)/shard_map/ppermute | solution.py:40
  213.7 8.3 %collective-permute-start.21 = (bf16[32,4096]{1,0:T(8,128)(2,1)S(1)}, bf16[32,4096]{1,0:T(8,128)(2,1)S(1)}, u32[]{:S(2)}, u32[]{:S(2)}) collective-permute-start(bf16[32,4096]{1,0:T(8,128)(2,1)S(1)} %add_convert_fusion.10), channel_id=1, source_target_pairs={{2,0},{4,2},{6,4},{8,6},{10,8},{12,10},{14,12},{16,14},{18,16},{20... | collective-permute-start | bytes 786440 | tf_op jit(solution)/shard_map/ppermute | solution.py:44
  222.1 11.0 %collective-permute-start.22 = (bf16[32,4096]{1,0:T(8,128)(2,1)S(1)}, bf16[32,4096]{1,0:T(8,128)(2,1)S(1)}, u32[]{:S(2)}, u32[]{:S(2)}) collective-permute-start(bf16[32,4096]{1,0:T(8,128)(2,1)S(1)} %get-tuple-element.11), channel_id=1, source_target_pairs={{2,0},{4,2},{6,4},{8,6},{10,8},{12,10},{14,12},{16,14},{18,16},{20... | collective-permute-start | bytes 786440 | tf_op jit(solution)/shard_map/ppermute | solution.py:44
  226.5 10.0 %collective-permute-start.29 = (bf16[32,4096]{1,0:T(8,128)(2,1)S(1)}, bf16[32,4096]{1,0:T(8,128)(2,1)S(1)}, u32[]{:S(2)}, u32[]{:S(2)}) collective-permute-start(bf16[32,4096]{1,0:T(8,128)(2,1)S(1)} %get-tuple-element.12), channel_id=1, source_target_pairs={{0,2},{2,4},{4,6},{6,8},{8,10},{10,12},{12,14},{14,16},{16,18},{18... | collective-permute-start | bytes 786440 | tf_op jit(solution)/shard_map/ppermute | solution.py:40
  236.6 31.4 %copy-start.4 = (f32[64,4]{0,1:T(4,128)S(1)}, f32[64,4]{0,1:T(4,128)}, u32[]{:S(2)}) copy-start(f32[64,4]{0,1:T(4,128)} %param.13) | copy-start | bytes 3076
  236.6 8.4 %collective-permute-start.23 = (bf16[32,4096]{1,0:T(8,128)(2,1)S(1)}, bf16[32,4096]{1,0:T(8,128)(2,1)S(1)}, u32[]{:S(2)}, u32[]{:S(2)}) collective-permute-start(bf16[32,4096]{1,0:T(8,128)(2,1)S(1)} %get-tuple-element.9), channel_id=1, source_target_pairs={{2,0},{4,2},{6,4},{8,6},{10,8},{12,10},{14,12},{16,14},{18,16},{20... | collective-permute-start | bytes 786440 | tf_op jit(solution)/shard_map/ppermute | solution.py:44
  238.5 9.6 %collective-permute-start.30 = (bf16[32,4096]{1,0:T(8,128)(2,1)S(1)}, bf16[32,4096]{1,0:T(8,128)(2,1)S(1)}, u32[]{:S(2)}, u32[]{:S(2)}) collective-permute-start(bf16[32,4096]{1,0:T(8,128)(2,1)S(1)} %get-tuple-element.10), channel_id=1, source_target_pairs={{0,2},{2,4},{4,6},{6,8},{8,10},{10,12},{12,14},{14,16},{16,18},{18... | collective-permute-start | bytes 786440 | tf_op jit(solution)/shard_map/ppermute | solution.py:40
  248.2 8.3 %collective-permute-start.24 = (bf16[32,4096]{1,0:T(8,128)(2,1)S(1)}, bf16[32,4096]{1,0:T(8,128)(2,1)S(1)}, u32[]{:S(2)}, u32[]{:S(2)}) collective-permute-start(bf16[32,4096]{1,0:T(8,128)(2,1)S(1)} %get-tuple-element.7), channel_id=1, source_target_pairs={{2,0},{4,2},{6,4},{8,6},{10,8},{12,10},{14,12},{16,14},{18,16},{20... | collective-permute-start | bytes 786440 | tf_op jit(solution)/shard_map/ppermute | solution.py:44
  251.9 9.5 %collective-permute-start.31 = (bf16[32,4096]{1,0:T(8,128)(2,1)S(1)}, bf16[32,4096]{1,0:T(8,128)(2,1)S(1)}, u32[]{:S(2)}, u32[]{:S(2)}) collective-permute-start(bf16[32,4096]{1,0:T(8,128)(2,1)S(1)} %get-tuple-element.8), channel_id=1, source_target_pairs={{0,2},{2,4},{4,6},{6,8},{8,10},{10,12},{12,14},{14,16},{16,18},{18... | collective-permute-start | bytes 786440 | tf_op jit(solution)/shard_map/ppermute | solution.py:40
  262.2 12.1 %all-to-all-start.1 = ((bf16[16,32,256]{2,1,0:T(8,128)(2,1)}), bf16[16,32,256]{2,1,0:T(8,128)(2,1)S(1)}, u32[]{:S(2)}, u32[]{:S(2)}) async-start(bf16[16,32,256]{2,1,0:T(8,128)(2,1)} %bitcast.72), calls=%async_computation.1 | async-start | bytes 524288 | tf_op jit(solution)/shard_map/all_to_all | solution.py:139
Sparse Core Ops, SparseCore 0:
  9.5 28.5 all-gather.2
  76.6 18.8 all-gather.4

commit v3 on v1

--- a/solution.py
+++ b/solution.py
@@ -17,15 +17,32 @@
 T = ("z", "core")
 
 
+def swap_cores(x):
+    return lax.ppermute(x, "core", [(0, 1), (1, 0)])
+
+
 def gather_kv(keys, values):
-    place = lax.axis_index(E)
-    group = place // 2
-    odd = (place % 2) == 1
+    group = lax.axis_index(E) // 2
+    core = lax.axis_index("core")
     k = lax.dynamic_slice_in_dim(keys, group * HEAD_DIM, HEAD_DIM, 1)
     v = lax.dynamic_slice_in_dim(values, group * HEAD_DIM, HEAD_DIM, 1)
-    mine = lax.all_gather(jnp.where(odd, v, k), T, axis=0, tiled=True)
-    other = lax.ppermute(mine, "y", [(0, 1), (1, 0), (2, 3), (3, 2)])
-    return jnp.where(odd, other, mine), jnp.where(odd, mine, other)
+    first = core == 0
+    came = swap_cores(jnp.where(first, v, k))
+    kept = jnp.where(first, k, v)
+    chip = jnp.concatenate([jnp.where(first, kept, came), jnp.where(first, came, kept)], axis=0)
+    mine = lax.all_gather(chip, "z", axis=0, tiled=True)
+    other = swap_cores(mine)
+    return jnp.where(first, mine, other), jnp.where(first, other, mine)
+
+
+def experts(normed, w_in, w_down):
+    w_in = lax.all_gather(w_in, "core", axis=0, tiled=True)
+    w_down = lax.all_gather(w_down, "core", axis=0, tiled=True)
+    rows = lax.all_gather(normed, "z", axis=0, tiled=True)
+    hidden = jnp.einsum("rd,cdf->rcf", rows, w_in, preferred_element_type=jnp.float32)
+    hidden = jax.nn.silu(hidden).astype(jnp.bfloat16)
+    out = jnp.einsum("rcf,cfd->rd", hidden, w_down, preferred_element_type=jnp.float32)
+    return lax.psum_scatter(out.astype(jnp.bfloat16), "z", scatter_dimension=0, tiled=True)
 
 
 def attend(query, k, v, tensor_place):
@@ -58,7 +75,6 @@
 
 def per_device(query, keys, values, resid, route_ids, route_weight, w_in, w_down):
     tensor_place = lax.axis_index(T)
-    core = lax.axis_index("core")
     block, width = query.shape
     k, v = gather_kv(keys, values)
     attended = attend(query, k, v, tensor_place)
@@ -77,20 +93,7 @@
     variance = jnp.mean((wide - center) ** 2, axis=1, keepdims=True)
     normed = ((wide - center) * lax.rsqrt(variance + 1e-05)).astype(jnp.bfloat16)
 
-    tokens = lax.all_gather(normed, T, axis=0, tiled=True)
-    hidden = jnp.dot(tokens, w_in[0], preferred_element_type=jnp.float32)
-    hidden = jax.nn.silu(hidden).astype(jnp.bfloat16)
-    hidden = hidden.reshape(-1, 2, EXP_CAP, hidden.shape[1])
-    z_count = hidden.shape[0]
-    theirs = lax.dynamic_index_in_dim(hidden, 1 - core, 1, keepdims=False)
-    ours = lax.dynamic_index_in_dim(hidden, core, 1, keepdims=False)
-    theirs = theirs.reshape(z_count * EXP_CAP, -1)
-    ours = ours.reshape(z_count * EXP_CAP, -1)
-    away = jnp.dot(theirs, w_down[0], preferred_element_type=jnp.float32).astype(jnp.bfloat16)
-    came = lax.ppermute(away, "core", [(0, 1), (1, 0)])
-    here = jnp.dot(ours, w_down[0], preferred_element_type=jnp.float32)
-    pair = (here + came.astype(jnp.float32)).astype(jnp.bfloat16)
-    summed = lax.psum_scatter(pair, "z", scatter_dimension=0, tiled=True)
+    summed = experts(normed, w_in, w_down)
 
     back = summed.reshape(EXP_CAP, EXPERTS, width).transpose(1, 0, 2)
     back = lax.all_to_all(back, E, split_axis=0, concat_axis=0, tiled=True)

time: 274 us -> 259 us (0.945)
  waiting for transfers between devices: 174 us -> 163 us
    ppermute x2, waiting for transfers between devices: 17 us -> 2.44 us  [swap_cores(): return lax.ppermute(x, 'core', [(0, 1), (1, 0)])]
    all_gather x1 -> x3, waiting for transfers between devices: 73.9 us -> 77.2 us  [the longest x1 77.2 us: experts(): rows = lax.all_gather(normed, 'z', axis=0, tiled=True)]
    dot_general x3 -> x1, matrix products: 10.8 us -> 11.3 us  [experts(): jnp.einsum('rcf,cfd->rd', hidden, w_down, preferred_element_type=jnp.floa...]
  transfers between devices with their start and end apart: 5 -> 7, of which waited for: 5 -> 5; matrix products, arithmetic and copies ran while one was open for 1% -> 2% of each run, Pallas kernels for 0% -> 0%
where the time goes in v3:
time: 259 us; the launch traced here: 258 us
  waiting for transfers between devices  163 us (63%)
  blocking collectives  52.1 us (20%)
  between operations  13.3 us (5%)
  matrix products  12.8 us (5%)
  starting transfers between devices  11.2 us (4%)
  other arithmetic  4.1 us (2%)
    all_gather x1, waiting for transfers between devices, experts(): rows = lax.all_gather(normed, 'z', axis=0, tiled=True)  77.2 us
    reduce_scatter x1, waiting for transfers between devices, experts(): lax.psum_scatter(out.astype(jnp.bfloat16), 'z', scatter_dimension=0, tile...  76.4 us
    all_gather x1, blocking collectives, gather_kv(): mine = lax.all_gather(chip, 'z', axis=0, tiled=True)  38.2 us
    all_to_all x1, blocking collectives, per_device(): lax.all_to_all(sent.reshape(EXPERTS, EXP_CAP, width), E, split_axis=0, co...  13.9 us
    dot_general x1, matrix products, experts(): jnp.einsum('rcf,cfd->rd', hidden, w_down, preferred_element_type=jnp.floa...  11.3 us
    all_to_all x1, starting transfers between devices, per_device(): back = lax.all_to_all(back, E, split_axis=0, concat_axis=0, tiled=True)  7.24 us
    all_to_all x1, waiting for transfers between devices, per_device(): back = lax.all_to_all(back, E, split_axis=0, concat_axis=0, tiled=True)  6.37 us
  transfers between devices with their start and end apart: 7, of which 5 were waited for; matrix products, arithmetic and copies ran while one was open for 2% of the time, Pallas kernels for 0%

profile of v3, /device:TPU:6, one launch (start us, length us, event | category | flops | bytes accessed | tf_op | source)
XLA Modules:
  0.0 258.4 jit_solution(14339545667302376951)
XLA Ops:
  6.5 0.0 copy-start
  6.5 0.0 copy-start.2
  6.5 0.0 all-gather.6.cloned.1.call-start
  6.5 0.7 all-gather.6.cloned.1.call-update
  7.3 0.0 all-gather.8.cloned.1.call-start
  7.3 0.7 broadcast_select_fusion.2
  8.1 1.9 collective-permute-start
  10.0 0.0 all-gather.8.cloned.1.call-update
  10.0 0.0 all-gather.4.cloned.1.call-start
  10.1 0.0 copy-done.2
  10.1 0.1 convolution_convert_fusion.1
  10.3 0.1 convert_reduce_fusion.1
  10.4 0.7 collective-permute-done
  11.1 0.7 broadcast_select_fusion.1
  11.9 38.2 %all_gather.12 = bf16[2048,128]{1,0:T(8,128)(2,1)S(1)} all-gather(bf16[128,128]{1,0:T(8,128)(2,1)S(1)} %pad_maximum_fusion), channel_id=1, replica_groups=mesh['x'=4,'y'=4,'z'=16,'core'=2] {'z'}, dimensions={0}, use_global_device_ids=true | all-gather | bytes 557056 | tf_op jit(solution)/shard_map/all_gather | solution.py:33
  50.1 1.9 collective-permute-start.1
  52.0 0.1 iota_compare_fusion.2
  52.2 0.0 copy-start.1
  52.2 1.7 collective-permute-done.1
  53.9 0.0 copy-done
  53.9 0.3 fusion.6
  54.2 0.3 fusion.30
  54.6 0.5 convolution_bitcast_fusion
  55.1 0.0 copy-done.1
  55.1 0.2 convolution_convert_fusion
  55.3 13.9 %all_to_all.10 = bf16[16,32,256]{2,1,0:T(8,128)(2,1)S(1)} all-to-all(bf16[16,32,256]{2,1,0:T(8,128)(2,1)S(1)} %bitcast.59), channel_id=1, replica_groups=mesh['x'=4,'y'=4,'z'=16,'core'=2] {'x','y'}, dimensions={0} | all-to-all | bytes 524288 | tf_op jit(solution)/shard_map/all_to_all | solution.py:87
  69.4 0.2 convert_reduce_fusion
  69.5 0.3 fusion.13
  69.8 0.8 multiply_convert_fusion.1
  70.6 0.0 all-gather.4.cloned.1.call-update
  70.6 0.0 reduce-scatter.2.cloned.1.call-start
  70.7 0.0 all-gather.6.cloned.1.call-done
  70.7 0.0 all-gather.8.cloned.1.call-done
  70.7 77.2 %all-gather.4.cloned.1.call-done = bf16[512,4096]{1,0:T(8,128)(2,1)} async-done(((bf16[32,4096]{1,0:T(8,128)(2,1)}), bf16[512,4096]{1,0:T(8,128)(2,1)}) %all-gather.4.cloned.1.call-update) | async-done | bytes 4194320 | tf_op jit(solution)/shard_map/all_gather | solution.py:41
  147.9 11.3 %bitcast_convert_fusion = bf16[512,4096]{1,0:T(8,128)(2,1)} fusion(bf16[2,256,4096]{2,1,0:T(8,128)(2,1)} %all-gather.8.cloned.1.call-done, bf16[2,4096,256]{2,1,0:T(8,128)(2,1)} %all-gather.6.cloned.1.call-done, bf16[512,4096]{1,0:T(8,128)(2,1)} %all-gather.4.cloned.1.call-done), kind=kOutput, calls=%fused_computation.1 | convolution fusion | flops 4298375168 | bytes 16777216 | tf_op jit(solution)/shard_map/rcf,cfd->rd/dot_general | solution.py:44
  159.2 0.0 copy-start.3
  159.2 0.0 reduce-scatter.2.cloned.1.call-update
  159.2 76.4 %reduce-scatter.2.cloned.1.call-done = bf16[32,4096]{1,0:T(8,128)(2,1)} async-done(((bf16[512,4096]{1,0:T(8,128)(2,1)}), bf16[32,4096]{1,0:T(8,128)(2,1)}) %reduce-scatter.2.cloned.1.call-update) | async-done | bytes 262160 | tf_op jit(solution)/shard_map/reduce_scatter | solution.py:45
  235.6 1.7 copy.43
  237.3 7.2 %all-to-all-start.1 = ((bf16[16,32,256]{2,1,0:T(8,128)(2,1)}), bf16[16,32,256]{2,1,0:T(8,128)(2,1)S(1)}, u32[]{:S(2)}, u32[]{:S(2)}) async-start(bf16[16,32,256]{2,1,0:T(8,128)(2,1)} %bitcast.57), calls=%async_computation.2 | async-start | bytes 524288 | tf_op jit(solution)/shard_map/all_to_all | solution.py:99
  244.6 0.0 copy-done.3
  244.6 6.4 %all-to-all-done.1 = bf16[16,32,256]{2,1,0:T(8,128)(2,1)S(1)} async-done(((bf16[16,32,256]{2,1,0:T(8,128)(2,1)}), bf16[16,32,256]{2,1,0:T(8,128)(2,1)S(1)}, u32[]{:S(2)}, u32[]{:S(2)}) %all-to-all-start.1) | async-done | bytes 262176 | tf_op jit(solution)/shard_map/all_to_all | solution.py:99
  251.0 0.3 fusion.7
  251.2 0.6 add_convert_fusion
  (11 shorter events, 0.2 us)
Async XLA Ops:
  6.5 47.4 %copy-start = (bf16[64,256]{1,0:T(8,128)(2,1)S(1)}, bf16[64,256]{1,0:T(8,128)(2,1)}, u32[]{:S(2)}) copy-start(bf16[64,256]{1,0:T(8,128)(2,1)} %param.8) | copy-start | bytes 98308
  6.5 3.5 %copy-start.2 = (s32[64,4]{0,1:T(4,128)S(1)}, s32[64,4]{0,1:T(4,128)}, u32[]{:S(2)}) copy-start(s32[64,4]{0,1:T(4,128)} %param.12) | copy-start | bytes 3076
  6.5 64.2 %all-gather.6.cloned.1.call-start = ((), (), s32[]{:S(2)}) async-start(), calls=%async_computation.4 | async-start | bytes 6291456 | tf_op jit(solution)/shard_map/all_gather | solution.py:39
  7.3 63.5 %all-gather.8.cloned.1.call-start = ((), (), s32[]{:S(2)}) async-start(), calls=%async_computation.5 | async-start | bytes 6291456 | tf_op jit(solution)/shard_map/all_gather | solution.py:40
  8.1 3.1 %collective-permute-start = (bf16[64,128]{1,0:T(8,128)(2,1)S(1)}, bf16[64,128]{1,0:T(8,128)(2,1)S(1)}, u32[]{:S(2)}, u32[]{:S(2)}) collective-permute-start(bf16[64,128]{1,0:T(8,128)(2,1)S(1)} %broadcast_select_fusion.2), channel_id=1, source_target_pairs={{0,1},{1,0},{2,3},{3,2},{4,5},{5,4},{6,7},{7,6},{8,9},{9,8},{10,11... | collective-permute-start | bytes 49160 | tf_op jit(solution)/shard_map/ppermute | solution.py:21
  10.0 137.9 %all-gather.4.cloned.1.call-start = ((), (), s32[]{:S(2)}) async-start(), calls=%async_computation.3 | async-start | bytes 4456448 | tf_op jit(solution)/shard_map/all_gather | solution.py:41
  50.1 3.8 %collective-permute-start.1 = (bf16[2048,128]{1,0:T(8,128)(2,1)S(1)}, bf16[2048,128]{1,0:T(8,128)(2,1)S(1)}, u32[]{:S(2)}, u32[]{:S(2)}) collective-permute-start(bf16[2048,128]{1,0:T(8,128)(2,1)S(1)} %all_gather.12), channel_id=1, source_target_pairs={{0,1},{1,0},{2,3},{3,2},{4,5},{5,4},{6,7},{7,6},{8,9},{9,8},{10,11... | collective-permute-start | bytes 1572872 | tf_op jit(solution)/shard_map/ppermute | solution.py:21
  52.2 2.9 %copy-start.1 = (bf16[64,256]{1,0:T(8,128)(2,1)S(1)}, bf16[64,256]{1,0:T(8,128)(2,1)}, u32[]{:S(2)}) copy-start(bf16[64,256]{1,0:T(8,128)(2,1)} %param.11) | copy-start | bytes 98308
  70.6 165.0 %reduce-scatter.2.cloned.1.call-start = ((), (), s32[]{:S(2)}) async-start(), calls=%async_computation.6 | async-start | bytes 4456448 | tf_op jit(solution)/shard_map/reduce_scatter | solution.py:45
  159.2 85.4 %copy-start.3 = (f32[64,4]{0,1:T(4,128)S(1)}, f32[64,4]{0,1:T(4,128)}, u32[]{:S(2)}) copy-start(f32[64,4]{0,1:T(4,128)} %param.13) | copy-start | bytes 3076
  237.3 13.6 %all-to-all-start.1 = ((bf16[16,32,256]{2,1,0:T(8,128)(2,1)}), bf16[16,32,256]{2,1,0:T(8,128)(2,1)S(1)}, u32[]{:S(2)}, u32[]{:S(2)}) async-start(bf16[16,32,256]{2,1,0:T(8,128)(2,1)} %bitcast.57), calls=%async_computation.2 | async-start | bytes 524288 | tf_op jit(solution)/shard_map/all_to_all | solution.py:99
Sparse Core Ops, SparseCore 0:
  9.5 28.5 all-gather.5
  40.2 25.4 all-gather.7
  70.8 77.1 all-gather.3
  159.3 76.2 reduce-scatter.1

commit v4 on v3

v4 whole, which is shorter than its diff:
```python
import math

import jax
import jax.numpy as jnp
from jax import lax
from jax.experimental import pallas as pl
from jax.experimental.pallas import tpu as pltpu
from jax.sharding import Mesh
from jax.sharding import PartitionSpec as P

HEADS = 32
KV_HEADS = 8
HEAD_DIM = 128
EXPERTS = 16
EXP_CAP = 32
TOPK = 4
BLOCK = 64
HALF = 128
Z = 16
MIB = 1 << 20

E = ("x", "y")
T = ("z", "core")


def swap_cores(x):
    return lax.ppermute(x, "core", [(0, 1), (1, 0)])


def gather_kv(keys, values, notes):
    group = lax.axis_index(E) // 2
    core = lax.axis_index("core")
    k = lax.dynamic_slice_in_dim(keys, group * HEAD_DIM, HEAD_DIM, 1)
    v = lax.dynamic_slice_in_dim(values, group * HEAD_DIM, HEAD_DIM, 1)
    first = core == 0
    came = swap_cores(jnp.where(first, v, k))
    kept = jnp.where(first, k, v)
    chip = jnp.concatenate([jnp.where(first, kept, came), jnp.where(first, came, kept), notes], axis=0)
    all_chips = lax.all_gather(chip, "z", axis=0)
    mine = all_chips[:, : 2 * BLOCK].reshape(-1, HEAD_DIM)
    other = swap_cores(mine)
    return jnp.where(first, mine, other), jnp.where(first, other, mine), all_chips[:, 2 * BLOCK :]


def notes_of(ids, ranks, gates):
    top = lax.reduce_precision(gates, 8, 7)
    rest = gates - top
    middle = lax.reduce_precision(rest, 8, 7)
    low = rest - middle
    parts = [ids.astype(jnp.float32), ranks.astype(jnp.float32), top, middle, low]
    rows = jnp.concatenate([p.T.reshape(2, 128) for p in parts], axis=0).astype(jnp.bfloat16)
    return jnp.pad(rows, ((0, 6), (0, 0)))


def read_notes(notes):
    rows = notes[:, :10].astype(jnp.float32).reshape(Z, 5, TOPK, BLOCK)
    return rows[:, 0] * EXP_CAP + rows[:, 1], rows[:, 2] + rows[:, 3] + rows[:, 4]


def place_kernel(slots_ref, rows_ref, out_ref):
    for z in range(slots_ref.shape[0]):
        grid = lax.broadcasted_iota(jnp.int32, (EXPERTS * EXP_CAP, BLOCK), 0).astype(jnp.float32)
        hit = grid == slots_ref[z, 0:1, :]
        for p in range(1, TOPK):
            hit = jnp.logical_or(hit, grid == slots_ref[z, p : p + 1, :])
        take = jnp.where(hit, 1.0, 0.0).astype(jnp.bfloat16)
        out = jnp.dot(take, rows_ref[z], preferred_element_type=jnp.float32).astype(jnp.bfloat16)
        out_ref[:, z] = out.reshape(EXPERTS, EXP_CAP, HALF)


def place_rows(slots, rows):
    step = 8
    return pl.pallas_call(
        place_kernel,
        grid=(Z // step,),
        in_specs=[
            pl.BlockSpec((step, TOPK, BLOCK), lambda i: (i, 0, 0)),
            pl.BlockSpec((step, BLOCK, HALF), lambda i: (i, 0, 0)),
        ],
        out_specs=pl.BlockSpec((EXPERTS, step, EXP_CAP, HALF), lambda i: (0, i, 0, 0)),
        out_shape=jax.ShapeDtypeStruct((EXPERTS, Z, EXP_CAP, HALF), jnp.bfloat16),
        cost_estimate=pl.CostEstimate(flops=2 * Z * 512 * 64 * 128, bytes_accessed=3 * MIB, transcendentals=0),
    )(slots, rows)


def mix_kernel(slots_ref, gates_ref, rows_ref, out_ref):
    for z in range(slots_ref.shape[0]):
        grid = lax.broadcasted_iota(jnp.int32, (BLOCK, EXPERTS * EXP_CAP), 1).astype(jnp.float32)
        weight = jnp.zeros((BLOCK, EXPERTS * EXP_CAP), jnp.float32)
        for p in range(TOPK):
            weight = jnp.where(grid == slots_ref[z, :, p : p + 1], gates_ref[z, :, p : p + 1], weight)
        high = weight.astype(jnp.bfloat16)
        low = (weight - high.astype(jnp.float32)).astype(jnp.bfloat16)
        rows = rows_ref[:, z].reshape(EXPERTS * EXP_CAP, HALF)
        out = jnp.dot(high, rows, preferred_element_type=jnp.float32)
        out += jnp.dot(low, rows, preferred_element_type=jnp.float32)
        out_ref[z] = out.astype(jnp.bfloat16)


def mix_rows(slots, gates, rows):
    step = 8
    return pl.pallas_call(
        mix_kernel,
        grid=(Z // step,),
        in_specs=[
            pl.BlockSpec((step, BLOCK, TOPK), lambda i: (i, 0, 0)),
            pl.BlockSpec((step, BLOCK, TOPK), lambda i: (i, 0, 0)),
            pl.BlockSpec((EXPERTS, step, EXP_CAP, HALF), lambda i: (0, i, 0, 0)),
        ],
        out_specs=pl.BlockSpec((step, BLOCK, HALF), lambda i: (i, 0, 0)),
        out_shape=jax.ShapeDtypeStruct((Z, BLOCK, HALF), jnp.bfloat16),
        cost_estimate=pl.CostEstimate(flops=4 * Z * 512 * 64 * 128, bytes_accessed=3 * MIB, transcendentals=0),
    )(slots.transpose(0, 2, 1), gates.transpose(0, 2, 1), rows)


def expert_kernel(a_ref, b_ref, in_ref, down_ref, oa_ref, ob_ref, raw, normed):
    group = a_ref.shape[0]
    rows = group * EXP_CAP
    cols = EXPERTS
    total = jnp.zeros((rows, HALF), jnp.float32)
    for c in range(cols):
        a = a_ref[:, c].reshape(rows, HALF).astype(jnp.float32)
        b = b_ref[c].reshape(rows, HALF).astype(jnp.float32)
        raw[:, 2 * c * HALF : (2 * c + 1) * HALF] = a
        raw[:, (2 * c + 1) * HALF : (2 * c + 2) * HALF] = b
        total += a + b
    width = 2 * cols * HALF
    center = jnp.sum(total, axis=1, keepdims=True) / width
    spread = jnp.zeros((rows, HALF), jnp.float32)
    for c in range(2 * cols):
        off = raw[:, c * HALF : (c + 1) * HALF] - center
        spread += off * off
    scale = lax.rsqrt(jnp.sum(spread, axis=1, keepdims=True) / width + 1e-05)
    for c in range(2 * cols):
        off = raw[:, c * HALF : (c + 1) * HALF] - center
        normed[:, c * HALF : (c + 1) * HALF] = (off * scale).astype(jnp.bfloat16)
    hidden = []
    for k in range(2):
        h = jnp.dot(normed[...], in_ref[k], preferred_element_type=jnp.float32)
        hidden.append((h * (1.0 / (1.0 + jnp.exp(-h)))).astype(jnp.bfloat16))
    chunk = 512
    for j in range(width // chunk):
        cut = slice(j * chunk, (j + 1) * chunk)
        out = jnp.dot(hidden[0], down_ref[0, :, cut], preferred_element_type=jnp.float32)
        out += jnp.dot(hidden[1], down_ref[1, :, cut], preferred_element_type=jnp.float32)
        out = out.astype(jnp.bfloat16)
        for i in range(chunk // (2 * HALF)):
            c = j * (chunk // (2 * HALF)) + i
            oa_ref[:, c] = out[:, 2 * i * HALF : (2 * i + 1) * HALF].reshape(group, EXP_CAP, HALF)
            ob_ref[c] = out[:, (2 * i + 1) * HALF : (2 * i + 2) * HALF].reshape(group, EXP_CAP, HALF)


def experts(rows_a, rows_b, w_in, w_down):
    group = 4
    rows = group * EXP_CAP
    width = w_down.shape[2]
    spec_a = pl.BlockSpec((group, EXPERTS, EXP_CAP, HALF), lambda i: (i, 0, 0, 0))
    spec_b = pl.BlockSpec((EXPERTS, group, EXP_CAP, HALF), lambda i: (0, i, 0, 0))
    return pl.pallas_call(
        expert_kernel,
        grid=(Z // group,),
        in_specs=[
            spec_a,
            spec_b,
            pl.BlockSpec(w_in.shape, lambda i: (0, 0, 0)),
            pl.BlockSpec(w_down.shape, lambda i: (0, 0, 0)),
        ],
        out_specs=[spec_a, spec_b],
        out_shape=[
            jax.ShapeDtypeStruct(rows_a.shape, jnp.bfloat16),
            jax.ShapeDtypeStruct(rows_b.shape, jnp.bfloat16),
        ],
        scratch_shapes=[pltpu.VMEM((rows, width), jnp.float32), pltpu.VMEM((rows, width), jnp.bfloat16)],
        compiler_params=pltpu.CompilerParams(vmem_limit_bytes=48 * MIB),
        cost_estimate=pl.CostEstimate(flops=4 * 512 * 512 * width, bytes_accessed=16 * MIB, transcendentals=512 * 512),
    )(rows_a, rows_b, w_in, w_down)


def attend(query, k, v, tensor_place):
    block = query.shape[0]
    heads = query.shape[1] // HEAD_DIM
    total = k.shape[0]
    q = query.reshape(block, heads, HEAD_DIM)
    scores = jnp.einsum("qhd,kd->hqk", q, k, preferred_element_type=jnp.float32)
    scores = scores / math.sqrt(HEAD_DIM)
    query_pos = tensor_place * block + jnp.arange(block)
    causal = query_pos[:, None] >= jnp.arange(total)[None, :]
    scores = jnp.where(causal[None], scores, -1e30)
    top = jnp.max(scores, axis=-1, keepdims=True)
    raised = jnp.exp(scores - top)
    probs = (raised / jnp.sum(raised, axis=-1, keepdims=True)).astype(jnp.bfloat16)
    out = jnp.einsum("hqk,kd->qhd", probs, v, preferred_element_type=jnp.float32)
    return out.reshape(block, heads * HEAD_DIM)


def ranks_of(ids):
    grid = jnp.arange(EXPERTS, dtype=jnp.int32)
    picked = ids[:, :, None] == grid[None, None, :]
    chosen = jnp.any(picked, axis=1)
    rows = ids.shape[0]
    lower = (jnp.arange(rows)[:, None] > jnp.arange(rows)[None, :]).astype(jnp.bfloat16)
    rank = jnp.dot(lower, chosen.astype(jnp.bfloat16), preferred_element_type=jnp.float32).astype(jnp.int32)
    return jnp.sum(jnp.where(picked, rank[:, None, :], 0), axis=2)


def swap_columns(x):
    return lax.all_to_all(x, E, split_axis=0, concat_axis=0, tiled=True)


def per_device(query, keys, values, resid, route_ids, route_weight, w_in, w_down):
    w_in = lax.all_gather(w_in, "core", axis=0, tiled=True)
    w_down = lax.all_gather(w_down, "core", axis=0, tiled=True)
    ranks = ranks_of(route_ids)
    gates = route_weight / jnp.sum(route_weight, axis=1, keepdims=True)
    k, v, notes = gather_kv(keys, values, notes_of(route_ids, ranks, gates))
    plane_slots, plane_gates = read_notes(notes)
    attended = attend(query, k, v, lax.axis_index(T))
    state = (resid.astype(jnp.float32) + attended).astype(jnp.bfloat16)

    slot_grid = jnp.arange(EXPERTS * EXP_CAP, dtype=jnp.int32)
    slots = route_ids * EXP_CAP + ranks
    takes = (slots[:, :, None] == slot_grid[None, None, :]).astype(jnp.bfloat16)
    sent_a = jnp.einsum("tps,td->sd", takes, state[:, :HALF], preferred_element_type=jnp.float32)
    sent_a = sent_a.astype(jnp.bfloat16).reshape(EXPERTS, EXP_CAP, HALF)
    came_a = swap_columns(sent_a)
    rows_a = lax.all_gather(came_a, "z", axis=0)

    state_b, came_a = lax.optimization_barrier((state[:, HALF:], came_a))
    plane_b = lax.all_gather(state_b, "z", axis=0)
    rows_b = swap_columns(place_rows(plane_slots, plane_b))

    out_a, out_b = experts(rows_a, rows_b, w_in, w_down)

    sum_a = lax.psum_scatter(out_a, "z", scatter_dimension=0)
    part_b = mix_rows(plane_slots, plane_gates, swap_columns(out_b))
    mix_b = lax.all_to_all(part_b, "z", split_axis=0, concat_axis=0, tiled=True)
    mix_b = jnp.sum(mix_b.astype(jnp.float32), axis=0)

    back_a = swap_columns(sum_a).reshape(EXPERTS * EXP_CAP, HALF)
    outs_a = jnp.einsum("tps,sd->tpd", takes, back_a, preferred_element_type=jnp.float32)
    mix_a = jnp.sum(gates[:, :, None] * outs_a, axis=1)
    mixture = jnp.concatenate([mix_a, mix_b], axis=1)
    return (state.astype(jnp.float32) + mixture).astype(jnp.bfloat16)


def solution(mesh):
    fine = Mesh(mesh.devices.reshape(4, 4, 16, 2), ("x", "y", "z", "core"))
    placed = (
        P(T, E),
        P(T, None),
        P(T, None),
        P(T, E),
        P(T, None),
        P(T, None),
        P(E, None, T),
        P(E, T, None),
    )
    return jax.shard_map(per_device, mesh=fine, in_specs=placed, out_specs=P(T, E), check_vma=False)
```

time: 259 us -> 253 us (0.977)
  waiting for transfers between devices: 163 us -> 54.2 us
  blocking collectives: 52.1 us -> 132 us
  Pallas kernels: 0 us -> 21 us
  matrix products: 12.8 us -> 1.45 us
  starting transfers between devices: 11.2 us -> 18.3 us
  local copies, waits for them, and re-layouts: 1.73 us -> 5.13 us
    all_gather x3, waiting for transfers between devices: 77.2 us -> 10.9 us  [the longest x1 10.9 us: per_device(): rows_a = lax.all_gather(came_a, 'z', axis=0)]
    reduce_scatter x1, waiting for transfers between devices: 76.4 us -> 18 us  [per_device(): sum_a = lax.psum_scatter(out_a, 'z', scatter_dimension=0)]
    all_to_all x1 -> x3, blocking collectives: 13.9 us -> 63.6 us  [the longest x2 38.3 us: swap_columns(): return lax.all_to_all(x, E, split_axis=0, concat_axis=0, tiled=True)]
    all_gather x1 -> x2, blocking collectives: 38.2 us -> 68.8 us  [the longest x1 38.5 us: gather_kv(): all_chips = lax.all_gather(chip, 'z', axis=0)]
    pallas_call x0 -> x3, Pallas kernels: none -> 21 us  [the longest x1 13.1 us: experts(): pl.pallas_call(expert_kernel, grid=(Z // group,), in_specs=[spec_a, spec_...]
    all_to_all x1 -> x2, waiting for transfers between devices: 6.37 us -> 21.9 us  [swap_columns(): return lax.all_to_all(x, E, split_axis=0, concat_axis=0, tiled=True)]
    dot_general x4 -> x3, matrix products: 11.9 us -> 0.62 us  [the longest x1 0.28 us: per_device(): jnp.einsum('tps,sd->tpd', takes, back_a, preferred_element_type=jnp.float32)]
    all_to_all x1 -> x2, starting transfers between devices: 7.24 us -> 14.3 us  [swap_columns(): return lax.all_to_all(x, E, split_axis=0, concat_axis=0, tiled=True)]
  transfers between devices with their start and end apart: 7 -> 8, of which waited for: 5 -> 6; matrix products, arithmetic and copies ran while one was open for 2% -> 4% of each run, Pallas kernels for 0% -> 3%
where the time goes in v4:
time: 253 us; the launch traced here: 251 us
  blocking collectives  132 us (52%)
  waiting for transfers between devices  54.2 us (21%)
  Pallas kernels  21 us (8%)
  starting transfers between devices  18.3 us (7%)
  between operations  13.3 us (5%)
  other arithmetic  5.72 us (2%)
  local copies, waits for them, and re-layouts  5.13 us (2%)
    all_gather x1, blocking collectives, gather_kv(): all_chips = lax.all_gather(chip, 'z', axis=0)  38.5 us
    all_to_all x2, blocking collectives, swap_columns(): return lax.all_to_all(x, E, split_axis=0, concat_axis=0, tiled=True)  38.3 us
    all_gather x1, blocking collectives, per_device(): plane_b = lax.all_gather(state_b, 'z', axis=0)  30.2 us
    all_to_all x1, blocking collectives, per_device(): mix_b = lax.all_to_all(part_b, 'z', split_axis=0, concat_axis=0, tiled=True)  25.2 us
    all_to_all x2, waiting for transfers between devices, swap_columns(): return lax.all_to_all(x, E, split_axis=0, concat_axis=0, tiled=True)  21.9 us
    reduce_scatter x1, waiting for transfers between devices, per_device(): sum_a = lax.psum_scatter(out_a, 'z', scatter_dimension=0)  18 us
    all_to_all x2, starting transfers between devices, swap_columns(): return lax.all_to_all(x, E, split_axis=0, concat_axis=0, tiled=True)  14.3 us
    pallas_call x1, Pallas kernels, experts(): pl.pallas_call(expert_kernel, grid=(Z // group,), in_specs=[spec_a, spec_...  13.1 us
  transfers between devices with their start and end apart: 8, of which 6 were waited for; matrix products, arithmetic and copies ran while one was open for 4% of the time, Pallas kernels for 3%

profile of v4, /device:TPU:6, one launch (start us, length us, event | category | flops | bytes accessed | tf_op | source)
XLA Modules:
  0.0 251.5 jit_solution(6255284376303133341)
XLA Ops:
  6.5 0.0 copy-start
  6.5 0.0 copy-start.4
  6.5 0.0 copy-start.3
  6.5 0.0 all-gather.7.cloned.1.call-start
  6.5 0.7 all-gather.7.cloned.1.call-update
  7.3 0.0 all-gather.9.cloned.1.call-start
  7.3 0.7 all-gather.9.cloned.1.call-update
  8.0 0.0 all-gather.11.cloned.1.call-start
  8.1 0.7 broadcast_select_fusion.2
  8.8 1.9 collective-permute-start
  10.7 0.0 copy-done.4
  10.8 0.0 copy-done.3
  10.8 0.1 convolution_convert_fusion.1
  11.0 0.1 convert_reduce_fusion.1
  11.1 0.1 reshape.78
  11.2 0.1 reshape.79
  11.3 0.1 reshape.76
  11.4 0.1 reshape.77
  11.5 0.1 reshape.80
  11.5 0.1 concatenate.10
  11.6 0.3 collective-permute-done
  11.9 0.7 broadcast_select_fusion.1
  12.7 38.5 %all-gather = bf16[2304,128]{1,0:T(8,128)(2,1)S(1)} all-gather(bf16[144,128]{1,0:T(8,128)(2,1)S(1)} %fusion.19), channel_id=2, replica_groups=mesh['x'=4,'y'=4,'z'=16,'core'=2] {'z'}, dimensions={0}, use_global_device_ids=true | all-gather | bytes 626688 | tf_op jit(solution)/shard_map/all_gather | solution.py:39
  51.3 1.9 collective-permute-start.1
  53.2 0.1 iota_compare_fusion.2
  53.3 1.7 collective-permute-done.1
  55.1 0.0 copy-done
  55.1 0.3 fusion.4
  55.4 0.3 fusion.32
  55.7 0.0 copy-start.2
  55.7 0.5 convolution_bitcast_fusion
  56.2 0.2 copy-done.2
  56.5 0.2 convolution_convert_fusion
  56.7 13.2 %all_to_all.25 = bf16[16,32,128]{2,1,0:T(8,128)(2,1)} all-to-all(bf16[16,32,128]{2,1,0:T(8,128)(2,1)S(1)} %bitcast.63), channel_id=1, replica_groups=mesh['x'=4,'y'=4,'z'=16,'core'=2] {'x','y'}, dimensions={0} | all-to-all | bytes 262144 | tf_op jit(solution)/shard_map/all_to_all | solution.py:207
  69.9 0.0 all-gather.11.cloned.1.call-update
  69.9 0.0 reduce-scatter.2.cloned.1.call-start
  70.0 0.1 reshape.89
  70.2 0.2 copy.41
  70.4 0.2 copy.42
  70.6 0.9 fusion.15
  71.6 0.8 copy.37.slots_ref
  72.4 30.2 %all-gather.2 = bf16[1024,128]{1,0:T(8,128)(2,1)} all-gather(bf16[64,128]{1,0:T(8,128)(2,1)S(1)} %slice.43), channel_id=4, replica_groups=mesh['x'=4,'y'=4,'z'=16,'core'=2] {'z'}, dimensions={0}, use_global_device_ids=true | all-gather | bytes 278528 | tf_op jit(solution)/shard_map/all_gather | solution.py:229
  102.6 3.8 %shard_map.82 = bf16[16,16,32,128]{3,2,1,0:T(8,128)(2,1)} custom-call(f32[16,4,64]{2,1,0:T(4,128)} %copy.37.slots_ref, bf16[16,64,128]{2,1,0:T(8,128)(2,1)} %bitcast.62), custom_call_target="tpu_custom_call" | custom-call | flops 134217728 | bytes 3145728 | tf_op jit(solution)/shard_map/pallas_call | solution.py:73
  106.4 25.2 %all_to_all.26.b_ref = bf16[16,16,32,128]{3,2,1,0:T(8,128)(2,1)} all-to-all(bf16[16,16,32,128]{3,2,1,0:T(8,128)(2,1)} %shard_map.82), channel_id=1, replica_groups=mesh['x'=4,'y'=4,'z'=16,'core'=2] {'x','y'}, dimensions={0} | all-to-all | bytes 4194304 | tf_op jit(solution)/shard_map/all_to_all | solution.py:207
  131.6 0.0 all-gather.7.cloned.1.call-done.in_ref
  131.6 0.0 all-gather.9.cloned.1.call-done.down_ref
  131.6 10.9 %all-gather.11.cloned.1.call-done = bf16[256,32,128]{2,1,0:T(8,128)(2,1)} async-done(((bf16[16,32,128]{2,1,0:T(8,128)(2,1)}), bf16[256,32,128]{2,1,0:T(8,128)(2,1)}) %all-gather.11.cloned.1.call-update) | async-done | bytes 2097168 | tf_op jit(solution)/shard_map/all_gather | solution.py:226
  142.5 13.1 %shard_map.83 = (bf16[16,16,32,128]{3,2,1,0:T(8,128)(2,1)}, bf16[16,16,32,128]{3,2,1,0:T(8,128)(2,1)}) custom-call(bf16[16,16,32,128]{3,2,1,0:T(8,128)(2,1)} %bitcast.66, bf16[16,16,32,128]{3,2,1,0:T(8,128)(2,1)} %all_to_all.26.b_ref, bf16[2,4096,256]{2,1,0:T(8,128)(2,1)} %all-gather.7.cloned.1.call-done.in_ref, ...), custom_call_target="tpu_custom_call" | custom-call | flops 4294967296 | bytes 16777216 | tf_op jit(solution)/shard_map/pallas_call | solution.py:159
  155.6 0.0 reduce-scatter.2.cloned.1.call-update
  155.7 7.0 %all-to-all-start.3 = ((bf16[16,16,32,128]{3,2,1,0:T(8,128)(2,1)}), bf16[16,16,32,128]{3,2,1,0:T(8,128)(2,1)S(1)}, u32[]{:S(2)}, u32[]{:S(2)}) async-start(bf16[16,16,32,128]{3,2,1,0:T(8,128)(2,1)} %get-tuple-element.10), calls=%async_computation.4 | async-start | bytes 4194304 | tf_op jit(solution)/shard_map/all_to_all | solution.py:207
  162.7 0.2 copy.43
  162.9 0.2 copy.44
  163.2 1.1 copy.45
  164.3 2.0 add_bitcast_fusion.gates_ref
  166.2 16.1 %all-to-all-done.3.rows_ref = bf16[16,16,32,128]{3,2,1,0:T(8,128)(2,1)S(1)} async-done(((bf16[16,16,32,128]{3,2,1,0:T(8,128)(2,1)}), bf16[16,16,32,128]{3,2,1,0:T(8,128)(2,1)S(1)}, u32[]{:S(2)}, u32[]{:S(2)}) %all-to-all-start.3) | async-done | bytes 2097184 | tf_op jit(solution)/shard_map/all_to_all | solution.py:207
  182.3 0.0 copy-start.1
  182.3 1.3 copy-done.1
  183.7 4.0 %shard_map.84 = bf16[16,64,128]{2,1,0:T(8,128)(2,1)} custom-call(f32[16,64,4]{2,1,0:T(8,128)} %get-tuple-element.14.slots_ref, f32[16,64,4]{2,1,0:T(8,128)} %add_bitcast_fusion.gates_ref, bf16[16,16,32,128]{3,2,1,0:T(8,128)(2,1)} %copy-done.1), custom_call_target="tpu_custom_call" | custom-call | flops 268435456 | bytes 3145728 | tf_op jit(solution)/shard_map/pallas_call | solution.py:102
  187.7 25.2 %all_to_all.27 = bf16[16,64,128]{2,1,0:T(8,128)(2,1)S(1)} all-to-all(bf16[16,64,128]{2,1,0:T(8,128)(2,1)} %shard_map.84), channel_id=1, replica_groups=mesh['x'=4,'y'=4,'z'=16,'core'=2] {'z'}, dimensions={0} | all-to-all | bytes 524288 | tf_op jit(solution)/shard_map/all_to_all | solution.py:236
  212.9 18.0 %reduce-scatter.2.cloned.1.call-done = bf16[1,16,32,128]{3,2,1,0:T(8,128)(2,1)} async-done(((bf16[16,16,32,128]{3,2,1,0:T(8,128)(2,1)}), bf16[1,16,32,128]{3,2,1,0:T(8,128)(2,1)}) %reduce-scatter.2.cloned.1.call-update) | async-done | bytes 131088 | tf_op jit(solution)/shard_map/reduce_scatter | solution.py:234
  230.9 7.3 %all-to-all-start.2 = ((bf16[16,32,128]{2,1,0:T(8,128)(2,1)}), bf16[16,32,128]{2,1,0:T(8,128)(2,1)S(1)}, u32[]{:S(2)}, u32[]{:S(2)}) async-start(bf16[16,32,128]{2,1,0:T(8,128)(2,1)} %bitcast.64), calls=%async_computation.3 | async-start | bytes 262144 | tf_op jit(solution)/shard_map/all_to_all | solution.py:207
  238.2 5.8 %all-to-all-done.2 = bf16[16,32,128]{2,1,0:T(8,128)(2,1)S(1)} async-done(((bf16[16,32,128]{2,1,0:T(8,128)(2,1)}), bf16[16,32,128]{2,1,0:T(8,128)(2,1)S(1)}, u32[]{:S(2)}, u32[]{:S(2)}) %all-to-all-start.2) | async-done | bytes 131104 | tf_op jit(solution)/shard_map/all_to_all | solution.py:207
  244.1 0.3 fusion.5
  244.3 0.6 fusion.18
  (14 shorter events, 0.2 us)
Async XLA Ops:
  6.5 48.5 %copy-start = (bf16[64,256]{1,0:T(8,128)(2,1)S(1)}, bf16[64,256]{1,0:T(8,128)(2,1)}, u32[]{:S(2)}) copy-start(bf16[64,256]{1,0:T(8,128)(2,1)} %param.8) | copy-start | bytes 98308
  6.5 4.2 %copy-start.4 = (f32[64,4]{0,1:T(4,128)S(1)}, f32[64,4]{0,1:T(4,128)}, u32[]{:S(2)}) copy-start(f32[64,4]{0,1:T(4,128)} %param.13) | copy-start | bytes 3076
  6.5 4.2 %copy-start.3 = (s32[64,4]{0,1:T(4,128)S(1)}, s32[64,4]{0,1:T(4,128)}, u32[]{:S(2)}) copy-start(s32[64,4]{0,1:T(4,128)} %param.12) | copy-start | bytes 3076
  6.5 125.1 %all-gather.7.cloned.1.call-start = ((), (), s32[]{:S(2)}) async-start(), calls=%async_computation.6 | async-start | bytes 6291456 | tf_op jit(solution)/shard_map/all_gather | solution.py:211
  7.3 124.3 %all-gather.9.cloned.1.call-start = ((), (), s32[]{:S(2)}) async-start(), calls=%async_computation.7 | async-start | bytes 6291456 | tf_op jit(solution)/shard_map/all_gather | solution.py:212
  8.0 134.5 %all-gather.11.cloned.1.call-start = ((), (), s32[]{:S(2)}) async-start(), calls=%async_computation.9 | async-start | bytes 2228224 | tf_op jit(solution)/shard_map/all_gather | solution.py:226
  8.8 3.1 %collective-permute-start = (bf16[64,128]{1,0:T(8,128)(2,1)S(1)}, bf16[64,128]{1,0:T(8,128)(2,1)S(1)}, u32[]{:S(2)}, u32[]{:S(2)}) collective-permute-start(bf16[64,128]{1,0:T(8,128)(2,1)S(1)} %broadcast_select_fusion.2), channel_id=1, source_target_pairs={{0,1},{1,0},{2,3},{3,2},{4,5},{5,4},{6,7},{7,6},{8,9},{9,8},{10,11... | collective-permute-start | bytes 49160 | tf_op jit(solution)/shard_map/ppermute | solution.py:27
  51.3 3.8 %collective-permute-start.1 = (bf16[2048,128]{1,0:T(8,128)(2,1)S(1)}, bf16[2048,128]{1,0:T(8,128)(2,1)S(1)}, u32[]{:S(2)}, u32[]{:S(2)}) collective-permute-start(bf16[2048,128]{1,0:T(8,128)(2,1)S(1)} %bitcast.59), channel_id=1, source_target_pairs={{0,1},{1,0},{2,3},{3,2},{4,5},{5,4},{6,7},{7,6},{8,9},{9,8},{10,11... | collective-permute-start | bytes 1572872 | tf_op jit(solution)/shard_map/ppermute | solution.py:27
  55.7 0.8 copy-start.2
  69.9 161.0 %reduce-scatter.2.cloned.1.call-start = ((), (), s32[]{:S(2)}) async-start(), calls=%async_computation.8 | async-start | bytes 2228224 | tf_op jit(solution)/shard_map/reduce_scatter | solution.py:234
  155.7 26.7 %all-to-all-start.3 = ((bf16[16,16,32,128]{3,2,1,0:T(8,128)(2,1)}), bf16[16,16,32,128]{3,2,1,0:T(8,128)(2,1)S(1)}, u32[]{:S(2)}, u32[]{:S(2)}) async-start(bf16[16,16,32,128]{3,2,1,0:T(8,128)(2,1)} %get-tuple-element.10), calls=%async_computation.4 | async-start | bytes 4194304 | tf_op jit(solution)/shard_map/all_to_all | solution.py:207
  182.3 1.3 copy-start.1
  230.9 13.2 %all-to-all-start.2 = ((bf16[16,32,128]{2,1,0:T(8,128)(2,1)}), bf16[16,32,128]{2,1,0:T(8,128)(2,1)S(1)}, u32[]{:S(2)}, u32[]{:S(2)}) async-start(bf16[16,32,128]{2,1,0:T(8,128)(2,1)} %bitcast.64), calls=%async_computation.3 | async-start | bytes 262144 | tf_op jit(solution)/shard_map/all_to_all | solution.py:207
Sparse Core Ops, SparseCore 0:
  9.5 28.5 all-gather.6
  40.1 25.4 all-gather.8
  70.0 72.3 all-gather.10
  155.8 75.0 reduce-scatter.1

commit v5 on v4

v5 whole, which is shorter than its diff:
```python
import math

import jax
import jax.numpy as jnp
from jax import lax
from jax.experimental import pallas as pl
from jax.experimental.pallas import tpu as pltpu
from jax.sharding import Mesh
from jax.sharding import PartitionSpec as P

HEADS = 32
KV_HEADS = 8
HEAD_DIM = 128
EXPERTS = 16
EXP_CAP = 32
TOPK = 4
BLOCK = 64
HALF = 128
Z = 16
MIB = 1 << 20

E = ("x", "y")
T = ("z", "core")


def swap_cores(x):
    return lax.ppermute(x, "core", [(0, 1), (1, 0)])


def gather_kv(keys, values, notes):
    group = lax.axis_index(E) // 2
    core = lax.axis_index("core")
    k = lax.dynamic_slice_in_dim(keys, group * HEAD_DIM, HEAD_DIM, 1)
    v = lax.dynamic_slice_in_dim(values, group * HEAD_DIM, HEAD_DIM, 1)
    first = core == 0
    came = swap_cores(jnp.where(first, v, k))
    kept = jnp.where(first, k, v)
    chip = jnp.concatenate([jnp.where(first, kept, came), jnp.where(first, came, kept), notes], axis=0)
    all_chips = lax.all_gather(chip, "z", axis=0)
    mine = all_chips[:, : 2 * BLOCK].reshape(-1, HEAD_DIM)
    other = swap_cores(mine)
    return jnp.where(first, mine, other), jnp.where(first, other, mine), all_chips[:, 2 * BLOCK :]


def notes_of(ids, ranks, gates):
    top = lax.reduce_precision(gates, 8, 7)
    rest = gates - top
    middle = lax.reduce_precision(rest, 8, 7)
    low = rest - middle
    parts = [ids.astype(jnp.float32), ranks.astype(jnp.float32), top, middle, low]
    rows = jnp.concatenate([p.T.reshape(2, 128) for p in parts], axis=0).astype(jnp.bfloat16)
    return jnp.pad(rows, ((0, 6), (0, 0)))


def read_notes(notes):
    rows = notes[:, :10].astype(jnp.float32).reshape(Z, 5, TOPK, BLOCK)
    return rows[:, 0] * EXP_CAP + rows[:, 1], rows[:, 2] + rows[:, 3] + rows[:, 4]


def grids_kernel(slots_ref, slots_t_ref, gates_ref, take_ref, high_ref, low_ref):
    slots = EXPERTS * EXP_CAP
    for z in range(slots_ref.shape[0]):
        grid = lax.broadcasted_iota(jnp.int32, (slots, BLOCK), 0).astype(jnp.float32)
        hit = grid == slots_t_ref[z, 0:1, :]
        for p in range(1, TOPK):
            hit = jnp.logical_or(hit, grid == slots_t_ref[z, p : p + 1, :])
        take_ref[z] = jnp.where(hit, 1.0, 0.0).astype(jnp.bfloat16)
        grid = lax.broadcasted_iota(jnp.int32, (BLOCK, slots), 1).astype(jnp.float32)
        weight = jnp.zeros((BLOCK, slots), jnp.float32)
        for p in range(TOPK):
            weight = jnp.where(grid == slots_ref[z, :, p : p + 1], gates_ref[z, :, p : p + 1], weight)
        high = weight.astype(jnp.bfloat16)
        high_ref[z] = high
        low_ref[z] = (weight - high.astype(jnp.float32)).astype(jnp.bfloat16)


def grids(slots, gates):
    step = 4
    total = EXPERTS * EXP_CAP
    return pl.pallas_call(
        grids_kernel,
        grid=(Z // step,),
        in_specs=[
            pl.BlockSpec((step, BLOCK, TOPK), lambda i: (i, 0, 0)),
            pl.BlockSpec((step, TOPK, BLOCK), lambda i: (i, 0, 0)),
            pl.BlockSpec((step, BLOCK, TOPK), lambda i: (i, 0, 0)),
        ],
        out_specs=[
            pl.BlockSpec((step, total, BLOCK), lambda i: (i, 0, 0)),
            pl.BlockSpec((step, BLOCK, total), lambda i: (i, 0, 0)),
            pl.BlockSpec((step, BLOCK, total), lambda i: (i, 0, 0)),
        ],
        out_shape=[
            jax.ShapeDtypeStruct((Z, total, BLOCK), jnp.bfloat16),
            jax.ShapeDtypeStruct((Z, BLOCK, total), jnp.bfloat16),
            jax.ShapeDtypeStruct((Z, BLOCK, total), jnp.bfloat16),
        ],
        cost_estimate=pl.CostEstimate(flops=16 * MIB, bytes_accessed=4 * MIB, transcendentals=0),
    )(slots.transpose(0, 2, 1), slots, gates.transpose(0, 2, 1))


def place_kernel(take_ref, rows_ref, out_ref):
    for z in range(take_ref.shape[0]):
        out = jnp.dot(take_ref[z], rows_ref[z], preferred_element_type=jnp.float32).astype(jnp.bfloat16)
        out_ref[:, z] = out.reshape(EXPERTS, EXP_CAP, HALF)


def place_rows(take, rows):
    step = 4
    return pl.pallas_call(
        place_kernel,
        grid=(Z // step,),
        in_specs=[
            pl.BlockSpec((step, EXPERTS * EXP_CAP, BLOCK), lambda i: (i, 0, 0)),
            pl.BlockSpec((step, BLOCK, HALF), lambda i: (i, 0, 0)),
        ],
        out_specs=pl.BlockSpec((EXPERTS, step, EXP_CAP, HALF), lambda i: (0, i, 0, 0)),
        out_shape=jax.ShapeDtypeStruct((EXPERTS, Z, EXP_CAP, HALF), jnp.bfloat16),
        cost_estimate=pl.CostEstimate(flops=2 * Z * 512 * 64 * 128, bytes_accessed=5 * MIB, transcendentals=0),
    )(take, rows)


def mix_kernel(high_ref, low_ref, rows_ref, out_ref):
    for z in range(high_ref.shape[0]):
        rows = rows_ref[:, z].reshape(EXPERTS * EXP_CAP, HALF)
        out = jnp.dot(high_ref[z], rows, preferred_element_type=jnp.float32)
        out += jnp.dot(low_ref[z], rows, preferred_element_type=jnp.float32)
        out_ref[z] = out.astype(jnp.bfloat16)


def mix_rows(high, low, rows):
    step = 4
    weights = pl.BlockSpec((step, BLOCK, EXPERTS * EXP_CAP), lambda i: (i, 0, 0))
    return pl.pallas_call(
        mix_kernel,
        grid=(Z // step,),
        in_specs=[
            weights,
            weights,
            pl.BlockSpec((EXPERTS, step, EXP_CAP, HALF), lambda i: (0, i, 0, 0)),
        ],
        out_specs=pl.BlockSpec((step, BLOCK, HALF), lambda i: (i, 0, 0)),
        out_shape=jax.ShapeDtypeStruct((Z, BLOCK, HALF), jnp.bfloat16),
        cost_estimate=pl.CostEstimate(flops=4 * Z * 512 * 64 * 128, bytes_accessed=5 * MIB, transcendentals=0),
    )(high, low, rows)


def expert_kernel(a_ref, b_ref, in_ref, down_ref, oa_ref, ob_ref, raw, normed):
    group = a_ref.shape[1]
    rows = group * EXP_CAP
    cols = EXPERTS
    width = 2 * cols * HALF
    hidden = []
    for k in range(2):
        h = jnp.dot(normed[...], in_ref[k], preferred_element_type=jnp.float32)
        hidden.append((h * (1.0 / (1.0 + jnp.exp(-h)))).astype(jnp.bfloat16))
    chunk = 512
    for j in range(width // chunk):
        cut = slice(j * chunk, (j + 1) * chunk)
        out = jnp.dot(hidden[0], down_ref[0, :, cut], preferred_element_type=jnp.float32)
        out += jnp.dot(hidden[1], down_ref[1, :, cut], preferred_element_type=jnp.float32)
        out = out.astype(jnp.bfloat16)
        for i in range(chunk // (2 * HALF)):
            c = j * (chunk // (2 * HALF)) + i
            oa_ref[c] = out[:, 2 * i * HALF : (2 * i + 1) * HALF].reshape(group, EXP_CAP, HALF)
            ob_ref[c] = out[:, (2 * i + 1) * HALF : (2 * i + 2) * HALF].reshape(group, EXP_CAP, HALF)
    total = jnp.zeros((rows, HALF), jnp.float32)
    for c in range(cols):
        a = a_ref[c].reshape(rows, HALF).astype(jnp.float32)
        b = b_ref[c].reshape(rows, HALF).astype(jnp.float32)
        raw[:, 2 * c * HALF : (2 * c + 1) * HALF] = a
        raw[:, (2 * c + 1) * HALF : (2 * c + 2) * HALF] = b
        total += a + b
    center = jnp.sum(total, axis=1, keepdims=True) / width
    spread = jnp.zeros((rows, HALF), jnp.float32)
    for c in range(2 * cols):
        off = raw[:, c * HALF : (c + 1) * HALF] - center
        spread += off * off
    scale = lax.rsqrt(jnp.sum(spread, axis=1, keepdims=True) / width + 1e-05)
    for c in range(2 * cols):
        off = raw[:, c * HALF : (c + 1) * HALF] - center
        normed[:, c * HALF : (c + 1) * HALF] = (off * scale).astype(jnp.bfloat16)


def experts(rows_a, rows_b, w_in, w_down):
    group = 4
    rows = group * EXP_CAP
    steps = Z // group
    width = w_down.shape[2]
    block = (EXPERTS, group, EXP_CAP, HALF)
    spec_in = pl.BlockSpec(block, lambda i: (0, jnp.minimum(i, steps - 1), 0, 0))
    spec_out = pl.BlockSpec(block, lambda i: (0, jnp.maximum(i - 1, 0), 0, 0))
    return pl.pallas_call(
        expert_kernel,
        grid=(steps + 1,),
        in_specs=[
            spec_in,
            spec_in,
            pl.BlockSpec(w_in.shape, lambda i: (0, 0, 0)),
            pl.BlockSpec(w_down.shape, lambda i: (0, 0, 0)),
        ],
        out_specs=[spec_out, spec_out],
        out_shape=[jax.ShapeDtypeStruct(rows_a.shape, jnp.bfloat16)] * 2,
        scratch_shapes=[pltpu.VMEM((rows, width), jnp.float32), pltpu.VMEM((rows, width), jnp.bfloat16)],
        compiler_params=pltpu.CompilerParams(vmem_limit_bytes=48 * MIB),
        cost_estimate=pl.CostEstimate(flops=4 * 512 * 512 * width, bytes_accessed=16 * MIB, transcendentals=512 * 512),
    )(rows_a, rows_b, w_in, w_down)


def attend(query, k, v, tensor_place):
    block = query.shape[0]
    heads = query.shape[1] // HEAD_DIM
    total = k.shape[0]
    q = query.reshape(block, heads, HEAD_DIM)
    scores = jnp.einsum("qhd,kd->hqk", q, k, preferred_element_type=jnp.float32)
    scores = scores / math.sqrt(HEAD_DIM)
    query_pos = tensor_place * block + jnp.arange(block)
    causal = query_pos[:, None] >= jnp.arange(total)[None, :]
    scores = jnp.where(causal[None], scores, -1e30)
    top = jnp.max(scores, axis=-1, keepdims=True)
    raised = jnp.exp(scores - top)
    probs = (raised / jnp.sum(raised, axis=-1, keepdims=True)).astype(jnp.bfloat16)
    out = jnp.einsum("hqk,kd->qhd", probs, v, preferred_element_type=jnp.float32)
    return out.reshape(block, heads * HEAD_DIM)


def ranks_of(ids):
    grid = jnp.arange(EXPERTS, dtype=jnp.int32)
    picked = ids[:, :, None] == grid[None, None, :]
    chosen = jnp.any(picked, axis=1)
    rows = ids.shape[0]
    lower = (jnp.arange(rows)[:, None] > jnp.arange(rows)[None, :]).astype(jnp.bfloat16)
    rank = jnp.dot(lower, chosen.astype(jnp.bfloat16), preferred_element_type=jnp.float32).astype(jnp.int32)
    return jnp.sum(jnp.where(picked, rank[:, None, :], 0), axis=2)


def swap_columns(x):
    return lax.all_to_all(x, E, split_axis=0, concat_axis=0, tiled=True)


def swap_chips(x):
    return lax.all_to_all(x, "z", split_axis=0, concat_axis=0, tiled=True)


def per_device(query, keys, values, resid, route_ids, route_weight, w_in, w_down):
    w_in = lax.all_gather(w_in, "core", axis=0, tiled=True)
    w_down = lax.all_gather(w_down, "core", axis=0, tiled=True)
    ranks = ranks_of(route_ids)
    gates = route_weight / jnp.sum(route_weight, axis=1, keepdims=True)
    k, v, notes = gather_kv(keys, values, notes_of(route_ids, ranks, gates))
    plane_slots, plane_gates = read_notes(notes)
    attended = attend(query, k, v, lax.axis_index(T))
    state = (resid.astype(jnp.float32) + attended).astype(jnp.bfloat16)

    take, high, low = grids(plane_slots, plane_gates)
    rows = []
    for cut in (state[:, :HALF], state[:, HALF:]):
        plane = swap_chips(jnp.broadcast_to(cut[None], (Z, BLOCK, HALF)))
        rows.append(swap_columns(place_rows(take, plane)))
    mixes = []
    for part in experts(*rows, w_in, w_down):
        mix = swap_chips(mix_rows(high, low, swap_columns(part)))
        mixes.append(jnp.sum(mix.astype(jnp.float32), axis=0))
    mixture = jnp.concatenate(mixes, axis=1)
    return (state.astype(jnp.float32) + mixture).astype(jnp.bfloat16)


def solution(mesh):
    fine = Mesh(mesh.devices.reshape(4, 4, 16, 2), ("x", "y", "z", "core"))
    placed = (
        P(T, E),
        P(T, None),
        P(T, None),
        P(T, E),
        P(T, None),
        P(T, None),
        P(E, None, T),
        P(E, T, None),
    )
    return jax.shard_map(per_device, mesh=fine, in_specs=placed, out_specs=P(T, E), check_vma=False)
```

time: 253 us -> 297 us (1.17)
  starting transfers between devices: 18.3 us -> 38.2 us
  waiting for transfers between devices: 54.2 us -> 73.2 us
  Pallas kernels: 21 us -> 37.6 us
  blocking collectives: 132 us -> 123 us
    all_to_all x0 -> x3, waiting for transfers between devices: none -> 31.4 us  [swap_chips(): return lax.all_to_all(x, 'z', split_axis=0, concat_axis=0, tiled=True)]
    all_gather x1 -> x0, blocking collectives: 30.2 us -> none  [per_device(): plane_b = lax.all_gather(state_b, 'z', axis=0)]
    all_to_all x0 -> x3, starting transfers between devices: none -> 21.2 us  [swap_chips(): return lax.all_to_all(x, 'z', split_axis=0, concat_axis=0, tiled=True)]
    all_to_all x2, blocking collectives: 38.3 us -> 58.4 us  [swap_columns(): return lax.all_to_all(x, E, split_axis=0, concat_axis=0, tiled=True)]
    reduce_scatter x1 -> x0, waiting for transfers between devices: 18 us -> none  [per_device(): sum_a = lax.psum_scatter(out_a, 'z', scatter_dimension=0)]
    all_to_all x2, waiting for transfers between devices: 21.9 us -> 38.3 us  [swap_columns(): return lax.all_to_all(x, E, split_axis=0, concat_axis=0, tiled=True)]
    pallas_call x2 -> x4, Pallas kernels: 17.2 us -> 29 us  [the longest x1 14.8 us: experts(): pl.pallas_call(expert_kernel, grid=(steps + 1,), in_specs=[spec_in, spec_...]
    all_gather x1 -> x0, waiting for transfers between devices: 10.9 us -> none  [per_device(): rows_a = lax.all_gather(came_a, 'z', axis=0)]
  transfers between devices with their start and end apart: 8 -> 9, of which waited for: 6 -> 7; matrix products, arithmetic and copies ran while one was open for 4% -> 3% of each run, Pallas kernels for 3% -> 8%
where the time goes in v5:
time: 297 us; the launch traced here: 294 us
  blocking collectives  123 us (41%)
  waiting for transfers between devices  73.2 us (25%)
  starting transfers between devices  38.2 us (13%)
  Pallas kernels  37.6 us (13%)
  between operations  13.7 us (5%)
  other arithmetic  4.3 us (1%)
  local copies, waits for them, and re-layouts  3.51 us (1%)
    all_to_all x2, blocking collectives, swap_columns(): return lax.all_to_all(x, E, split_axis=0, concat_axis=0, tiled=True)  58.4 us
    all_gather x1, blocking collectives, gather_kv(): all_chips = lax.all_gather(chip, 'z', axis=0)  38.5 us
    all_to_all x2, waiting for transfers between devices, swap_columns(): return lax.all_to_all(x, E, split_axis=0, concat_axis=0, tiled=True)  38.3 us
    all_to_all x3, waiting for transfers between devices, swap_chips(): return lax.all_to_all(x, 'z', split_axis=0, concat_axis=0, tiled=True)  31.4 us
    all_to_all x1, blocking collectives, swap_chips(): return lax.all_to_all(x, 'z', split_axis=0, concat_axis=0, tiled=True)  25.7 us
    all_to_all x3, starting transfers between devices, swap_chips(): return lax.all_to_all(x, 'z', split_axis=0, concat_axis=0, tiled=True)  21.2 us
    pallas_call x1, Pallas kernels, experts(): pl.pallas_call(expert_kernel, grid=(steps + 1,), in_specs=[spec_in, spec_...  14.8 us
    all_to_all x2, starting transfers between devices, swap_columns(): return lax.all_to_all(x, E, split_axis=0, concat_axis=0, tiled=True)  13.1 us
  transfers between devices with their start and end apart: 9, of which 7 were waited for; matrix products, arithmetic and copies ran while one was open for 3% of the time, Pallas kernels for 8%

profile of v5, /device:TPU:6, one launch (start us, length us, event | category | flops | bytes accessed | tf_op | source)
XLA Modules:
  0.0 294.0 jit_solution(14051962355632629742)
XLA Ops:
  6.5 0.0 copy-start
  6.5 0.0 copy-start.5
  6.5 0.0 copy-start.6
  6.5 0.0 all-gather.4.cloned.1.call-start
  6.5 0.7 all-gather.4.cloned.1.call-update
  7.3 0.7 broadcast_select_fusion.2
  8.0 1.9 collective-permute-start
  10.0 0.0 copy-done.5
  10.0 0.1 convolution_convert_fusion
  10.1 0.0 copy-done.6
  10.2 0.1 reshape.70
  10.3 0.1 reshape.74
  10.4 0.1 reshape.73
  10.5 0.1 reshape.72
  10.6 0.1 reshape.71
  10.6 0.1 concatenate.10
  10.7 0.4 collective-permute-done
  11.1 0.7 broadcast_select_fusion.1
  11.9 38.5 %all-gather = bf16[2304,128]{1,0:T(8,128)(2,1)S(1)} all-gather(bf16[144,128]{1,0:T(8,128)(2,1)S(1)} %fusion.14), channel_id=2, replica_groups=mesh['x'=4,'y'=4,'z'=16,'core'=2] {'z'}, dimensions={0}, use_global_device_ids=true | all-gather | bytes 626688 | tf_op jit(solution)/shard_map/all_gather | solution.py:39
  50.5 1.9 collective-permute-start.1
  52.4 0.1 iota_compare_fusion
  52.6 1.7 collective-permute-done.1
  54.3 0.0 copy-done
  54.3 0.3 fusion.4
  54.6 0.3 fusion.31
  54.9 0.0 copy-start.4
  54.9 0.5 convolution_bitcast_fusion
  55.4 0.2 copy-done.4
  55.8 25.7 %all_to_all.40.rows_ref = bf16[16,64,128]{2,1,0:T(8,128)(2,1)} all-to-all(bf16[16,64,128]{2,1,0:T(8,128)(2,1)S(1)} %broadcast_in_dim.32), channel_id=1, replica_groups=mesh['x'=4,'y'=4,'z'=16,'core'=2] {'z'}, dimensions={0} | all-to-all | bytes 524288 | tf_op jit(solution)/shard_map/all_to_all | solution.py:242
  81.5 0.8 broadcast_in_dim.33
  82.3 5.9 %all-to-all-start.2 = ((bf16[16,64,128]{2,1,0:T(8,128)(2,1)}), bf16[16,64,128]{2,1,0:T(8,128)(2,1)S(1)}, u32[]{:S(2)}, u32[]{:S(2)}) async-start(bf16[16,64,128]{2,1,0:T(8,128)(2,1)} %broadcast_in_dim.33), calls=%async_computation.2 | async-start | bytes 524288 | tf_op jit(solution)/shard_map/all_to_all | solution.py:242
  88.2 0.0 all-gather.6.cloned.1.call-start
  88.3 0.7 all-gather.6.cloned.1.call-update
  89.0 0.1 reshape.81
  89.1 0.2 copy.44
  89.4 0.6 fusion.27
  90.0 1.1 copy.40.slots_ref
  91.1 0.2 copy.43
  91.3 0.2 copy.45
  91.6 0.9 add_bitcast_fusion.gates_ref
  92.5 5.6 %shard_map.82 = (bf16[16,512,64]{2,1,0:T(8,128)(2,1)}, bf16[16,64,512]{2,1,0:T(8,128)(2,1)}, bf16[16,64,512]{2,1,0:T(8,128)(2,1)}) custom-call(f32[16,64,4]{2,1,0:T(8,128)} %copy.40.slots_ref, f32[16,4,64]{2,1,0:T(4,128)} %get-tuple-element.22.slots_t_ref, f32[16,64,4]{2,1,0:T(8,128)} %add_bitcast_fusion.gates_ref), custom_call_target="tpu_custom_call" | custom-call | flops 16777216 | bytes 4194304 | tf_op jit(solution)/shard_map/pallas_call | solution.py:80
  98.1 4.3 %shard_map.83 = bf16[16,16,32,128]{3,2,1,0:T(8,128)(2,1)} custom-call(bf16[16,512,64]{2,1,0:T(8,128)(2,1)} %get-tuple-element.12.take_ref, bf16[16,64,128]{2,1,0:T(8,128)(2,1)} %all_to_all.40.rows_ref), custom_call_target="tpu_custom_call" | custom-call | flops 134217728 | bytes 5242880 | tf_op jit(solution)/shard_map/pallas_call | solution.py:110
  102.4 4.2 %all-to-all-done.2.rows_ref = bf16[16,64,128]{2,1,0:T(8,128)(2,1)S(1)} async-done(((bf16[16,64,128]{2,1,0:T(8,128)(2,1)}), bf16[16,64,128]{2,1,0:T(8,128)(2,1)S(1)}, u32[]{:S(2)}, u32[]{:S(2)}) %all-to-all-start.2) | async-done | bytes 262176 | tf_op jit(solution)/shard_map/all_to_all | solution.py:242
  106.5 0.0 copy-start.3
  106.5 7.4 %all-to-all-start.1 = ((bf16[16,16,32,128]{3,2,1,0:T(8,128)(2,1)}), bf16[16,16,32,128]{3,2,1,0:T(8,128)(2,1)S(1)}, u32[]{:S(2)}, u32[]{:S(2)}) async-start(bf16[16,16,32,128]{3,2,1,0:T(8,128)(2,1)} %shard_map.83), calls=%async_computation.1 | async-start | bytes 4194304 | tf_op jit(solution)/shard_map/all_to_all | solution.py:238
  114.0 0.0 copy-done.3
  114.0 4.2 %shard_map.84 = bf16[16,16,32,128]{3,2,1,0:T(8,128)(2,1)} custom-call(bf16[16,512,64]{2,1,0:T(8,128)(2,1)} %get-tuple-element.12.take_ref, bf16[16,64,128]{2,1,0:T(8,128)(2,1)} %copy-done.3), custom_call_target="tpu_custom_call" | custom-call | flops 134217728 | bytes 5242880 | tf_op jit(solution)/shard_map/pallas_call | solution.py:110
  118.2 19.2 %all-to-all-done.1.a_ref = bf16[16,16,32,128]{3,2,1,0:T(8,128)(2,1)S(1)} async-done(((bf16[16,16,32,128]{3,2,1,0:T(8,128)(2,1)}), bf16[16,16,32,128]{3,2,1,0:T(8,128)(2,1)S(1)}, u32[]{:S(2)}, u32[]{:S(2)}) %all-to-all-start.1) | async-done | bytes 2097184 | tf_op jit(solution)/shard_map/all_to_all | solution.py:238
  137.4 0.0 copy-start.2
  137.4 30.0 %all_to_all.41.b_ref = bf16[16,16,32,128]{3,2,1,0:T(8,128)(2,1)} all-to-all(bf16[16,16,32,128]{3,2,1,0:T(8,128)(2,1)} %shard_map.84), channel_id=1, replica_groups=mesh['x'=4,'y'=4,'z'=16,'core'=2] {'x','y'}, dimensions={0} | all-to-all | bytes 4194304 | tf_op jit(solution)/shard_map/all_to_all | solution.py:238
  167.4 0.0 copy-done.2
  167.4 0.0 all-gather.4.cloned.1.call-done.in_ref
  167.4 14.8 %shard_map.85 = (bf16[16,16,32,128]{3,2,1,0:T(8,128)(2,1)S(1)}, bf16[16,16,32,128]{3,2,1,0:T(8,128)(2,1)}) custom-call(bf16[16,16,32,128]{3,2,1,0:T(8,128)(2,1)} %copy-done.2, bf16[16,16,32,128]{3,2,1,0:T(8,128)(2,1)} %all_to_all.41.b_ref, bf16[2,4096,256]{2,1,0:T(8,128)(2,1)} %all-gather.4.cloned.1.call-done.in_ref, ...), custom_call_target="tpu_custom_call" | custom-call | flops 4294967296 | bytes 16777216 | tf_op jit(solution)/shard_map/pallas_call | solution.py:193
  182.2 28.4 %all_to_all.42.rows_ref = bf16[16,16,32,128]{3,2,1,0:T(8,128)(2,1)} all-to-all(bf16[16,16,32,128]{3,2,1,0:T(8,128)(2,1)S(1)} %get-tuple-element.13), channel_id=1, replica_groups=mesh['x'=4,'y'=4,'z'=16,'core'=2] {'x','y'}, dimensions={0} | all-to-all | bytes 4194304 | tf_op jit(solution)/shard_map/all_to_all | solution.py:238
  210.5 5.7 %all-to-all-start.6 = ((bf16[16,16,32,128]{3,2,1,0:T(8,128)(2,1)}), bf16[16,16,32,128]{3,2,1,0:T(8,128)(2,1)S(1)}, u32[]{:S(2)}, u32[]{:S(2)}) async-start(bf16[16,16,32,128]{3,2,1,0:T(8,128)(2,1)} %get-tuple-element.14), calls=%async_computation.6 | async-start | bytes 4194304 | tf_op jit(solution)/shard_map/all_to_all | solution.py:238
  216.2 4.3 %shard_map.86 = bf16[16,64,128]{2,1,0:T(8,128)(2,1)} custom-call(bf16[16,64,512]{2,1,0:T(8,128)(2,1)} %get-tuple-element.10.high_ref, bf16[16,64,512]{2,1,0:T(8,128)(2,1)} %get-tuple-element.11.low_ref, bf16[16,16,32,128]{3,2,1,0:T(8,128)(2,1)} %all_to_all.42.rows_ref), custom_call_target="tpu_custom_call" | custom-call | flops 268435456 | bytes 5242880 | tf_op jit(solution)/shard_map/pallas_call | solution.py:134
  220.6 19.1 %all-to-all-done.6.rows_ref = bf16[16,16,32,128]{3,2,1,0:T(8,128)(2,1)S(1)} async-done(((bf16[16,16,32,128]{3,2,1,0:T(8,128)(2,1)}), bf16[16,16,32,128]{3,2,1,0:T(8,128)(2,1)S(1)}, u32[]{:S(2)}, u32[]{:S(2)}) %all-to-all-start.6) | async-done | bytes 2097184 | tf_op jit(solution)/shard_map/all_to_all | solution.py:238
  239.7 10.0 %all-to-all-start.5 = ((bf16[16,64,128]{2,1,0:T(8,128)(2,1)}), bf16[16,64,128]{2,1,0:T(8,128)(2,1)S(1)}, u32[]{:S(2)}, u32[]{:S(2)}) async-start(bf16[16,64,128]{2,1,0:T(8,128)(2,1)} %shard_map.86), calls=%async_computation.5 | async-start | bytes 524288 | tf_op jit(solution)/shard_map/all_to_all | solution.py:242
  249.6 0.0 copy-done.1
  249.6 4.3 %shard_map.87 = bf16[16,64,128]{2,1,0:T(8,128)(2,1)} custom-call(bf16[16,64,512]{2,1,0:T(8,128)(2,1)} %get-tuple-element.10.high_ref, bf16[16,64,512]{2,1,0:T(8,128)(2,1)} %get-tuple-element.11.low_ref, bf16[16,16,32,128]{3,2,1,0:T(8,128)(2,1)} %copy-done.1), custom_call_target="tpu_custom_call" | custom-call | flops 268435456 | bytes 5242880 | tf_op jit(solution)/shard_map/pallas_call | solution.py:134
  254.0 11.4 %all-to-all-done.5 = bf16[16,64,128]{2,1,0:T(8,128)(2,1)S(1)} async-done(((bf16[16,64,128]{2,1,0:T(8,128)(2,1)}), bf16[16,64,128]{2,1,0:T(8,128)(2,1)S(1)}, u32[]{:S(2)}, u32[]{:S(2)}) %all-to-all-start.5) | async-done | bytes 262176 | tf_op jit(solution)/shard_map/all_to_all | solution.py:242
  265.3 5.3 %all-to-all-start.7 = ((bf16[16,64,128]{2,1,0:T(8,128)(2,1)}), bf16[16,64,128]{2,1,0:T(8,128)(2,1)S(1)}, u32[]{:S(2)}, u32[]{:S(2)}) async-start(bf16[16,64,128]{2,1,0:T(8,128)(2,1)} %shard_map.87), calls=%async_computation.7 | async-start | bytes 524288 | tf_op jit(solution)/shard_map/all_to_all | solution.py:242
  270.7 15.8 %all-to-all-done.7 = bf16[16,64,128]{2,1,0:T(8,128)(2,1)S(1)} async-done(((bf16[16,64,128]{2,1,0:T(8,128)(2,1)}), bf16[16,64,128]{2,1,0:T(8,128)(2,1)S(1)}, u32[]{:S(2)}, u32[]{:S(2)}) %all-to-all-start.7) | async-done | bytes 262176 | tf_op jit(solution)/shard_map/all_to_all | solution.py:242
  286.6 0.6 fusion.13
  (19 shorter events, 0.3 us)
Async XLA Ops:
  6.5 47.7 %copy-start = (bf16[64,256]{1,0:T(8,128)(2,1)S(1)}, bf16[64,256]{1,0:T(8,128)(2,1)}, u32[]{:S(2)}) copy-start(bf16[64,256]{1,0:T(8,128)(2,1)} %param.8) | copy-start | bytes 98308
  6.5 3.4 %copy-start.5 = (s32[64,4]{0,1:T(4,128)S(1)}, s32[64,4]{0,1:T(4,128)}, u32[]{:S(2)}) copy-start(s32[64,4]{0,1:T(4,128)} %param.12) | copy-start | bytes 3076
  6.5 3.6 %copy-start.6 = (f32[64,4]{0,1:T(4,128)S(1)}, f32[64,4]{0,1:T(4,128)}, u32[]{:S(2)}) copy-start(f32[64,4]{0,1:T(4,128)} %param.13) | copy-start | bytes 3076
  6.5 160.9 %all-gather.4.cloned.1.call-start = ((), (), s32[]{:S(2)}) async-start(), calls=%async_computation.8 | async-start | bytes 6291456 | tf_op jit(solution)/shard_map/all_gather | solution.py:246
  8.0 3.1 %collective-permute-start = (bf16[64,128]{1,0:T(8,128)(2,1)S(1)}, bf16[64,128]{1,0:T(8,128)(2,1)S(1)}, u32[]{:S(2)}, u32[]{:S(2)}) collective-permute-start(bf16[64,128]{1,0:T(8,128)(2,1)S(1)} %broadcast_select_fusion.2), channel_id=1, source_target_pairs={{0,1},{1,0},{2,3},{3,2},{4,5},{5,4},{6,7},{7,6},{8,9},{9,8},{10,11... | collective-permute-start | bytes 49160 | tf_op jit(solution)/shard_map/ppermute | solution.py:27
  50.5 3.8 %collective-permute-start.1 = (bf16[2048,128]{1,0:T(8,128)(2,1)S(1)}, bf16[2048,128]{1,0:T(8,128)(2,1)S(1)}, u32[]{:S(2)}, u32[]{:S(2)}) collective-permute-start(bf16[2048,128]{1,0:T(8,128)(2,1)S(1)} %bitcast.68), channel_id=1, source_target_pairs={{0,1},{1,0},{2,3},{3,2},{4,5},{5,4},{6,7},{7,6},{8,9},{9,8},{10,11... | collective-permute-start | bytes 1572872 | tf_op jit(solution)/shard_map/ppermute | solution.py:27
  54.9 0.8 copy-start.4
  82.3 24.3 %all-to-all-start.2 = ((bf16[16,64,128]{2,1,0:T(8,128)(2,1)}), bf16[16,64,128]{2,1,0:T(8,128)(2,1)S(1)}, u32[]{:S(2)}, u32[]{:S(2)}) async-start(bf16[16,64,128]{2,1,0:T(8,128)(2,1)} %broadcast_in_dim.33), calls=%async_computation.2 | async-start | bytes 524288 | tf_op jit(solution)/shard_map/all_to_all | solution.py:242
  88.2 79.2 %all-gather.6.cloned.1.call-start = ((), (), s32[]{:S(2)}) async-start(), calls=%async_computation.9 | async-start | bytes 6291456 | tf_op jit(solution)/shard_map/all_gather | solution.py:247
  106.5 7.4 %copy-start.3 = (bf16[16,64,128]{2,1,0:T(8,128)(2,1)}, bf16[16,64,128]{2,1,0:T(8,128)(2,1)S(1)}, u32[]{:S(2)}) copy-start(bf16[16,64,128]{2,1,0:T(8,128)(2,1)S(1)} %all-to-all-done.2.rows_ref) | copy-start | bytes 786436
  106.5 30.9 %all-to-all-start.1 = ((bf16[16,16,32,128]{3,2,1,0:T(8,128)(2,1)}), bf16[16,16,32,128]{3,2,1,0:T(8,128)(2,1)S(1)}, u32[]{:S(2)}, u32[]{:S(2)}) async-start(bf16[16,16,32,128]{3,2,1,0:T(8,128)(2,1)} %shard_map.83), calls=%async_computation.1 | async-start | bytes 4194304 | tf_op jit(solution)/shard_map/all_to_all | solution.py:238
  137.4 30.0 %copy-start.2 = (bf16[16,16,32,128]{3,2,1,0:T(8,128)(2,1)}, bf16[16,16,32,128]{3,2,1,0:T(8,128)(2,1)S(1)}, u32[]{:S(2)}) copy-start(bf16[16,16,32,128]{3,2,1,0:T(8,128)(2,1)S(1)} %all-to-all-done.1.a_ref) | copy-start | bytes 6291460
  210.5 29.1 %all-to-all-start.6 = ((bf16[16,16,32,128]{3,2,1,0:T(8,128)(2,1)}), bf16[16,16,32,128]{3,2,1,0:T(8,128)(2,1)S(1)}, u32[]{:S(2)}, u32[]{:S(2)}) async-start(bf16[16,16,32,128]{3,2,1,0:T(8,128)(2,1)} %get-tuple-element.14), calls=%async_computation.6 | async-start | bytes 4194304 | tf_op jit(solution)/shard_map/all_to_all | solution.py:238
  239.7 10.0 %copy-start.1 = (bf16[16,16,32,128]{3,2,1,0:T(8,128)(2,1)}, bf16[16,16,32,128]{3,2,1,0:T(8,128)(2,1)S(1)}, u32[]{:S(2)}) copy-start(bf16[16,16,32,128]{3,2,1,0:T(8,128)(2,1)S(1)} %all-to-all-done.6.rows_ref) | copy-start | bytes 6291460
  239.7 25.7 %all-to-all-start.5 = ((bf16[16,64,128]{2,1,0:T(8,128)(2,1)}), bf16[16,64,128]{2,1,0:T(8,128)(2,1)S(1)}, u32[]{:S(2)}, u32[]{:S(2)}) async-start(bf16[16,64,128]{2,1,0:T(8,128)(2,1)} %shard_map.86), calls=%async_computation.5 | async-start | bytes 524288 | tf_op jit(solution)/shard_map/all_to_all | solution.py:242
  265.3 21.2 %all-to-all-start.7 = ((bf16[16,64,128]{2,1,0:T(8,128)(2,1)}), bf16[16,64,128]{2,1,0:T(8,128)(2,1)S(1)}, u32[]{:S(2)}, u32[]{:S(2)}) async-start(bf16[16,64,128]{2,1,0:T(8,128)(2,1)} %shard_map.87), calls=%async_computation.7 | async-start | bytes 524288 | tf_op jit(solution)/shard_map/all_to_all | solution.py:242
Sparse Core Ops, SparseCore 0:
  9.5 28.5 all-gather.3
  91.2 25.3 all-gather.5

commit v6 on v4

v6 whole, which is shorter than its diff:
```python
import math

import jax
import jax.numpy as jnp
from jax import lax
from jax.experimental import pallas as pl
from jax.experimental.pallas import tpu as pltpu
from jax.sharding import Mesh
from jax.sharding import PartitionSpec as P

HEADS = 32
KV_HEADS = 8
HEAD_DIM = 128
EXPERTS = 16
EXP_CAP = 32
TOPK = 4
BLOCK = 64
WIDTH = 256
Z = 16
PARTS = 2
MIB = 1 << 20

E = ("x", "y")
T = ("z", "core")


def swap_cores(x):
    return lax.ppermute(x, "core", [(0, 1), (1, 0)])


def gather_kv(keys, values, notes):
    group = lax.axis_index(E) // 2
    core = lax.axis_index("core")
    k = lax.dynamic_slice_in_dim(keys, group * HEAD_DIM, HEAD_DIM, 1)
    v = lax.dynamic_slice_in_dim(values, group * HEAD_DIM, HEAD_DIM, 1)
    first = core == 0
    came = swap_cores(jnp.where(first, v, k))
    kept = jnp.where(first, k, v)
    chip = jnp.concatenate([jnp.where(first, kept, came), jnp.where(first, came, kept), notes], axis=0)
    all_chips = lax.all_gather(chip, "z", axis=0)
    mine = all_chips[:, : 2 * BLOCK].reshape(-1, HEAD_DIM)
    other = swap_cores(mine)
    return jnp.where(first, mine, other), jnp.where(first, other, mine), all_chips[:, 2 * BLOCK :]


def notes_of(ids, ranks, gates):
    top = lax.reduce_precision(gates, 8, 7)
    rest = gates - top
    middle = lax.reduce_precision(rest, 8, 7)
    low = rest - middle
    parts = [ids.astype(jnp.float32), ranks.astype(jnp.float32), top, middle, low]
    rows = jnp.concatenate([p.T.reshape(2, 128) for p in parts], axis=0).astype(jnp.bfloat16)
    return jnp.pad(rows, ((0, 6), (0, 0)))


def read_notes(notes):
    rows = notes[:, :10].astype(jnp.float32).reshape(Z, 5, TOPK, BLOCK)
    return rows[:, 0] * EXP_CAP + rows[:, 1], rows[:, 2] + rows[:, 3] + rows[:, 4]


def place_kernel(slots_ref, rows_ref, out_ref):
    for z in range(slots_ref.shape[0]):
        grid = lax.broadcasted_iota(jnp.int32, (EXPERTS * EXP_CAP, BLOCK), 0).astype(jnp.float32)
        hit = grid == slots_ref[z, 0:1, :]
        for p in range(1, TOPK):
            hit = jnp.logical_or(hit, grid == slots_ref[z, p : p + 1, :])
        take = jnp.where(hit, 1.0, 0.0).astype(jnp.bfloat16)
        out = jnp.dot(take, rows_ref[z], preferred_element_type=jnp.float32).astype(jnp.bfloat16)
        out_ref[:, z] = out.reshape(EXPERTS, EXP_CAP, WIDTH)


def place_rows(slots, rows, part):
    step = 4
    count = Z // PARTS
    first = part * count // step
    return pl.pallas_call(
        place_kernel,
        grid=(count // step,),
        in_specs=[
            pl.BlockSpec((step, TOPK, BLOCK), lambda i: (first + i, 0, 0)),
            pl.BlockSpec((step, BLOCK, WIDTH), lambda i: (first + i, 0, 0)),
        ],
        out_specs=pl.BlockSpec((EXPERTS, step, EXP_CAP, WIDTH), lambda i: (0, i, 0, 0)),
        out_shape=jax.ShapeDtypeStruct((EXPERTS, count, EXP_CAP, WIDTH), jnp.bfloat16),
        compiler_params=pltpu.CompilerParams(vmem_limit_bytes=32 * MIB),
        cost_estimate=pl.CostEstimate(flops=2 * Z * 512 * 64 * 128, bytes_accessed=3 * MIB, transcendentals=0),
    )(slots, rows)


def mix_kernel(slots_ref, gates_ref, rows_ref, out_ref):
    for z in range(slots_ref.shape[0]):
        grid = lax.broadcasted_iota(jnp.int32, (BLOCK, EXPERTS * EXP_CAP), 1).astype(jnp.float32)
        weight = jnp.zeros((BLOCK, EXPERTS * EXP_CAP), jnp.float32)
        for p in range(TOPK):
            weight = jnp.where(grid == slots_ref[z, :, p : p + 1], gates_ref[z, :, p : p + 1], weight)
        high = weight.astype(jnp.bfloat16)
        low = (weight - high.astype(jnp.float32)).astype(jnp.bfloat16)
        rows = rows_ref[:, z].reshape(EXPERTS * EXP_CAP, WIDTH)
        out = jnp.dot(high, rows, preferred_element_type=jnp.float32)
        out += jnp.dot(low, rows, preferred_element_type=jnp.float32)
        out_ref[z] = out.astype(jnp.bfloat16)


def mix_rows(slots, gates, rows, part):
    step = 4
    count = Z // PARTS
    first = part * count // step
    return pl.pallas_call(
        mix_kernel,
        grid=(count // step,),
        in_specs=[
            pl.BlockSpec((step, BLOCK, TOPK), lambda i: (first + i, 0, 0)),
            pl.BlockSpec((step, BLOCK, TOPK), lambda i: (first + i, 0, 0)),
            pl.BlockSpec((EXPERTS, step, EXP_CAP, WIDTH), lambda i: (0, i, 0, 0)),
        ],
        out_specs=pl.BlockSpec((step, BLOCK, WIDTH), lambda i: (i, 0, 0)),
        out_shape=jax.ShapeDtypeStruct((count, BLOCK, WIDTH), jnp.bfloat16),
        compiler_params=pltpu.CompilerParams(vmem_limit_bytes=32 * MIB),
        cost_estimate=pl.CostEstimate(flops=4 * Z * 512 * 64 * 128, bytes_accessed=3 * MIB, transcendentals=0),
    )(slots, gates, rows)


def expert_kernel(rows_ref, in_ref, down_ref, out_ref, raw, normed):
    group = rows_ref.shape[1]
    rows = group * EXP_CAP
    width = EXPERTS * WIDTH
    total = jnp.zeros((rows, WIDTH), jnp.float32)
    for c in range(EXPERTS):
        part = rows_ref[c].reshape(rows, WIDTH).astype(jnp.float32)
        raw[:, c * WIDTH : (c + 1) * WIDTH] = part
        total += part
    center = jnp.sum(total, axis=1, keepdims=True) / width
    spread = jnp.zeros((rows, WIDTH), jnp.float32)
    for c in range(EXPERTS):
        off = raw[:, c * WIDTH : (c + 1) * WIDTH] - center
        spread += off * off
    scale = lax.rsqrt(jnp.sum(spread, axis=1, keepdims=True) / width + 1e-05)
    for c in range(EXPERTS):
        off = raw[:, c * WIDTH : (c + 1) * WIDTH] - center
        normed[:, c * WIDTH : (c + 1) * WIDTH] = (off * scale).astype(jnp.bfloat16)
    hidden = []
    for k in range(2):
        h = jnp.dot(normed[...], in_ref[k], preferred_element_type=jnp.float32)
        hidden.append((h * (1.0 / (1.0 + jnp.exp(-h)))).astype(jnp.bfloat16))
    for c in range(EXPERTS):
        cut = slice(c * WIDTH, (c + 1) * WIDTH)
        out = jnp.dot(hidden[0], down_ref[0, :, cut], preferred_element_type=jnp.float32)
        out += jnp.dot(hidden[1], down_ref[1, :, cut], preferred_element_type=jnp.float32)
        out_ref[c] = out.astype(jnp.bfloat16).reshape(group, EXP_CAP, WIDTH)


def experts(rows, w_in, w_down):
    group = 4
    width = w_down.shape[2]
    count = rows.shape[1]
    spec = pl.BlockSpec((EXPERTS, group, EXP_CAP, WIDTH), lambda i: (0, i, 0, 0))
    return pl.pallas_call(
        expert_kernel,
        grid=(count // group,),
        in_specs=[
            spec,
            pl.BlockSpec(w_in.shape, lambda i: (0, 0, 0)),
            pl.BlockSpec(w_down.shape, lambda i: (0, 0, 0)),
        ],
        out_specs=spec,
        out_shape=jax.ShapeDtypeStruct(rows.shape, jnp.bfloat16),
        scratch_shapes=[
            pltpu.VMEM((group * EXP_CAP, width), jnp.float32),
            pltpu.VMEM((group * EXP_CAP, width), jnp.bfloat16),
        ],
        compiler_params=pltpu.CompilerParams(vmem_limit_bytes=48 * MIB),
        cost_estimate=pl.CostEstimate(flops=2 * 512 * 512 * width, bytes_accessed=12 * MIB, transcendentals=256 * 512),
    )(rows, w_in, w_down)


def attend(query, k, v, tensor_place):
    block = query.shape[0]
    heads = query.shape[1] // HEAD_DIM
    total = k.shape[0]
    q = query.reshape(block, heads, HEAD_DIM)
    scores = jnp.einsum("qhd,kd->hqk", q, k, preferred_element_type=jnp.float32)
    scores = scores / math.sqrt(HEAD_DIM)
    query_pos = tensor_place * block + jnp.arange(block)
    causal = query_pos[:, None] >= jnp.arange(total)[None, :]
    scores = jnp.where(causal[None], scores, -1e30)
    top = jnp.max(scores, axis=-1, keepdims=True)
    raised = jnp.exp(scores - top)
    probs = (raised / jnp.sum(raised, axis=-1, keepdims=True)).astype(jnp.bfloat16)
    out = jnp.einsum("hqk,kd->qhd", probs, v, preferred_element_type=jnp.float32)
    return out.reshape(block, heads * HEAD_DIM)


def ranks_of(ids):
    grid = jnp.arange(EXPERTS, dtype=jnp.int32)
    picked = ids[:, :, None] == grid[None, None, :]
    chosen = jnp.any(picked, axis=1)
    rows = ids.shape[0]
    lower = (jnp.arange(rows)[:, None] > jnp.arange(rows)[None, :]).astype(jnp.bfloat16)
    rank = jnp.dot(lower, chosen.astype(jnp.bfloat16), preferred_element_type=jnp.float32).astype(jnp.int32)
    return jnp.sum(jnp.where(picked, rank[:, None, :], 0), axis=2)


def swap_columns(x):
    return lax.all_to_all(x, E, split_axis=0, concat_axis=0, tiled=True)


def swap_chips(x):
    return lax.all_to_all(x, "z", split_axis=0, concat_axis=0, tiled=True)


def per_device(query, keys, values, resid, route_ids, route_weight, w_in, w_down):
    w_in = lax.all_gather(w_in, "core", axis=0, tiled=True)
    w_down = lax.all_gather(w_down, "core", axis=0, tiled=True)
    ranks = ranks_of(route_ids)
    gates = route_weight / jnp.sum(route_weight, axis=1, keepdims=True)
    k, v, notes = gather_kv(keys, values, notes_of(route_ids, ranks, gates))
    plane_slots, plane_gates = read_notes(notes)
    attended = attend(query, k, v, lax.axis_index(T))
    state = (resid.astype(jnp.float32) + attended).astype(jnp.bfloat16)

    slots_t, gates_t = plane_slots.transpose(0, 2, 1), plane_gates.transpose(0, 2, 1)
    plane = lax.all_gather(state, "z", axis=0)
    rows = [swap_columns(place_rows(plane_slots, plane, part)) for part in range(PARTS)]
    outs = [experts(part, w_in, w_down) for part in rows]
    outs[0], rows[1] = lax.optimization_barrier((outs[0], rows[1]))
    mixes = [mix_rows(slots_t, gates_t, swap_columns(out), part) for part, out in enumerate(outs)]
    mix = swap_chips(jnp.concatenate(mixes, axis=0))
    mixture = jnp.sum(mix.astype(jnp.float32), axis=0)
    return (state.astype(jnp.float32) + mixture).astype(jnp.bfloat16)


def solution(mesh):
    fine = Mesh(mesh.devices.reshape(4, 4, 16, 2), ("x", "y", "z", "core"))
    placed = (
        P(T, E),
        P(T, None),
        P(T, None),
        P(T, E),
        P(T, None),
        P(T, None),
        P(E, None, T),
        P(E, T, None),
    )
    return jax.shard_map(per_device, mesh=fine, in_specs=placed, out_specs=P(T, E), check_vma=False)
```

time: 253 us -> 236 us (0.933)
  blocking collectives: 132 us -> 92.8 us
  starting transfers between devices: 18.3 us -> 34 us
  local copies, waits for them, and re-layouts: 5.13 us -> 13.3 us
  waiting for transfers between devices: 54.2 us -> 50.4 us
    all_to_all x3 -> x1, blocking collectives: 63.6 us -> 25 us  [swap_chips(): return lax.all_to_all(x, 'z', split_axis=0, concat_axis=0, tiled=True)]
    all_to_all x2 -> x4, waiting for transfers between devices: 21.9 us -> 48.5 us  [swap_columns(): return lax.all_to_all(x, E, split_axis=0, concat_axis=0, tiled=True)]
    reduce_scatter x1 -> x0, waiting for transfers between devices: 18 us -> none  [per_device(): sum_a = lax.psum_scatter(out_a, 'z', scatter_dimension=0)]
    all_to_all x2 -> x4, starting transfers between devices: 14.3 us -> 30.1 us  [swap_columns(): return lax.all_to_all(x, E, split_axis=0, concat_axis=0, tiled=True)]
    all_gather x1 -> x0, waiting for transfers between devices: 10.9 us -> none  [per_device(): rows_a = lax.all_gather(came_a, 'z', axis=0)]
    unnamed x15 -> x25, local copies, waits for them, and re-layouts: 3.64 us -> 12.5 us
    pallas_call x3 -> x6, Pallas kernels: 21 us -> 23.5 us  [the longest x2 15 us: experts(): pl.pallas_call(expert_kernel, grid=(count // group,), in_specs=[spec, pl....]
  transfers between devices with their start and end apart: 8 -> 8, of which waited for: 6 -> 6; matrix products, arithmetic and copies ran while one was open for 4% -> 4% of each run, Pallas kernels for 3% -> 9%
where the time goes in v6:
time: 236 us; the launch traced here: 233 us
  blocking collectives  92.8 us (39%)
  waiting for transfers between devices  50.4 us (21%)
  starting transfers between devices  34 us (14%)
  Pallas kernels  23.5 us (10%)
  between operations  13.7 us (6%)
  local copies, waits for them, and re-layouts  13.3 us (6%)
  other arithmetic  4.45 us (2%)
    all_to_all x4, waiting for transfers between devices, swap_columns(): return lax.all_to_all(x, E, split_axis=0, concat_axis=0, tiled=True)  48.5 us
    all_gather x1, blocking collectives, gather_kv(): all_chips = lax.all_gather(chip, 'z', axis=0)  38.6 us
    all_to_all x4, starting transfers between devices, swap_columns(): return lax.all_to_all(x, E, split_axis=0, concat_axis=0, tiled=True)  30.1 us
    all_gather x1, blocking collectives, per_device(): plane = lax.all_gather(state, 'z', axis=0)  29.3 us
    all_to_all x1, blocking collectives, swap_chips(): return lax.all_to_all(x, 'z', split_axis=0, concat_axis=0, tiled=True)  25 us
    pallas_call x2, Pallas kernels, experts(): pl.pallas_call(expert_kernel, grid=(count // group,), in_specs=[spec, pl....  15 us
    unnamed x25, local copies, waits for them, and re-layouts  12.5 us
  transfers between devices with their start and end apart: 8, of which 6 were waited for; matrix products, arithmetic and copies ran while one was open for 4% of the time, Pallas kernels for 9%

profile of v6, /device:TPU:6, one launch (start us, length us, event | category | flops | bytes accessed | tf_op | source)
XLA Modules:
  0.0 233.1 jit_solution(3847970979063398002)
XLA Ops:
  6.5 0.0 copy-start
  6.5 0.0 all-gather.5.cloned.1.call-start
  6.5 0.7 all-gather.5.cloned.1.call-update
  7.3 0.0 all-gather.7.cloned.1.call-start
  7.3 0.8 broadcast_select_fusion.2
  8.1 1.9 collective-permute-start
  10.0 0.0 all-gather.7.cloned.1.call-update
  10.0 0.0 copy-done.8
  10.1 0.0 copy-done.9
  10.1 0.1 convolution_convert_fusion
  10.3 0.1 iota_compare_fusion
  10.5 0.1 reshape.70
  10.6 0.1 reshape.71
  10.6 0.1 reshape.72
  10.7 0.1 reshape.69
  10.8 0.1 reshape.68
  10.9 0.1 concatenate.10
  11.0 0.2 collective-permute-done
  11.2 0.8 broadcast_select_fusion.1
  12.0 38.6 %all-gather = bf16[2304,128]{1,0:T(8,128)(2,1)S(1)} all-gather(bf16[144,128]{1,0:T(8,128)(2,1)S(1)} %fusion.15), channel_id=2, replica_groups=mesh['x'=4,'y'=4,'z'=16,'core'=2] {'z'}, dimensions={0}, use_global_device_ids=true | all-gather | bytes 626688 | tf_op jit(solution)/shard_map/all_gather | solution.py:40
  50.6 1.9 collective-permute-start.1
  52.5 0.1 reshape.79
  52.7 0.2 copy.45
  53.0 0.2 copy.46
  53.2 0.1 fusion.12
  53.3 0.2 copy.43.slots_ref
  53.5 0.9 collective-permute-done.1
  54.4 0.0 copy-done
  54.4 0.3 fusion.4
  54.7 0.3 fusion.27
  55.1 0.5 convolution_bitcast_fusion
  55.6 0.2 copy-done.7
  55.8 29.3 %all-gather.1 = bf16[1024,256]{1,0:T(8,128)(2,1)S(1)} all-gather(bf16[64,256]{1,0:T(8,128)(2,1)S(1)} %fusion.14), channel_id=3, replica_groups=mesh['x'=4,'y'=4,'z'=16,'core'=2] {'z'}, dimensions={0}, use_global_device_ids=true | all-gather | bytes 557056 | tf_op jit(solution)/shard_map/all_gather | solution.py:222
  85.1 2.1 shard_map.82
  87.2 7.4 %all-to-all-start = ((bf16[16,8,32,256]{3,2,1,0:T(8,128)(2,1)}), bf16[16,8,32,256]{3,2,1,0:T(8,128)(2,1)S(1)}, u32[]{:S(2)}, u32[]{:S(2)}) async-start(bf16[16,8,32,256]{3,2,1,0:T(8,128)(2,1)} %shard_map.82), calls=%async_computation | async-start | bytes 4194304 | tf_op jit(solution)/shard_map/all_to_all | solution.py:204
  94.6 2.2 shard_map.84
  96.8 18.8 %all-to-all-done.rows_ref = bf16[16,8,32,256]{3,2,1,0:T(8,128)(2,1)S(1)} async-done(((bf16[16,8,32,256]{3,2,1,0:T(8,128)(2,1)}), bf16[16,8,32,256]{3,2,1,0:T(8,128)(2,1)S(1)}, u32[]{:S(2)}, u32[]{:S(2)}) %all-to-all-start) | async-done | bytes 2097184 | tf_op jit(solution)/shard_map/all_to_all | solution.py:204
  115.6 1.4 copy-done.4
  117.0 6.7 %all-to-all-start.1 = ((bf16[16,8,32,256]{3,2,1,0:T(8,128)(2,1)}), bf16[16,8,32,256]{3,2,1,0:T(8,128)(2,1)S(1)}, u32[]{:S(2)}, u32[]{:S(2)}) async-start(bf16[16,8,32,256]{3,2,1,0:T(8,128)(2,1)} %shard_map.84), calls=%async_computation.1 | async-start | bytes 4194304 | tf_op jit(solution)/shard_map/all_to_all | solution.py:204
  123.7 0.0 all-gather.5.cloned.1.call-done.in_ref
  123.7 0.0 all-gather.7.cloned.1.call-done.down_ref
  123.7 0.0 copy-start.5
  123.7 1.6 copy-done.5
  125.3 7.5 %shard_map.83 = bf16[16,8,32,256]{3,2,1,0:T(8,128)(2,1)S(1)} custom-call(bf16[16,8,32,256]{3,2,1,0:T(8,128)(2,1)S(1)} %copy-done.5, bf16[2,4096,256]{2,1,0:T(8,128)(2,1)} %all-gather.5.cloned.1.call-done.in_ref, bf16[2,256,4096]{2,1,0:T(8,128)(2,1)} %all-gather.7.cloned.1.call-done.down_ref), custom_call_target="tpu_custom_call" | custom-call | flops 2147483648 | bytes 12582912 | tf_op jit(solution)/shard_map/pallas_call | solution.py:157
  132.8 0.0 copy-start.6
  132.8 1.3 copy-done.6
  134.2 9.1 %all-to-all-done.1.rows_ref = bf16[16,8,32,256]{3,2,1,0:T(8,128)(2,1)S(1)} async-done(((bf16[16,8,32,256]{3,2,1,0:T(8,128)(2,1)}), bf16[16,8,32,256]{3,2,1,0:T(8,128)(2,1)S(1)}, u32[]{:S(2)}, u32[]{:S(2)}) %all-to-all-start.1) | async-done | bytes 2097184 | tf_op jit(solution)/shard_map/all_to_all | solution.py:204
  143.3 1.3 copy-done.2
  144.6 6.5 %all-to-all-start.2 = ((bf16[16,8,32,256]{3,2,1,0:T(8,128)(2,1)}), bf16[16,8,32,256]{3,2,1,0:T(8,128)(2,1)S(1)}, u32[]{:S(2)}, u32[]{:S(2)}) async-start(bf16[16,8,32,256]{3,2,1,0:T(8,128)(2,1)} %copy-done.6), calls=%async_computation.2 | async-start | bytes 4194304 | tf_op jit(solution)/shard_map/all_to_all | solution.py:204
  151.1 1.6 copy-done.3
  152.7 7.5 %shard_map.86 = bf16[16,8,32,256]{3,2,1,0:T(8,128)(2,1)S(1)} custom-call(bf16[16,8,32,256]{3,2,1,0:T(8,128)(2,1)S(1)} %copy-done.3, bf16[2,4096,256]{2,1,0:T(8,128)(2,1)} %all-gather.5.cloned.1.call-done.in_ref, bf16[2,256,4096]{2,1,0:T(8,128)(2,1)} %all-gather.7.cloned.1.call-done.down_ref), custom_call_target="tpu_custom_call" | custom-call | flops 2147483648 | bytes 12582912 | tf_op jit(solution)/shard_map/pallas_call | solution.py:157
  160.2 1.3 copy-done.1
  161.6 8.8 %all-to-all-done.2.rows_ref = bf16[16,8,32,256]{3,2,1,0:T(8,128)(2,1)S(1)} async-done(((bf16[16,8,32,256]{3,2,1,0:T(8,128)(2,1)}), bf16[16,8,32,256]{3,2,1,0:T(8,128)(2,1)S(1)}, u32[]{:S(2)}, u32[]{:S(2)}) %all-to-all-start.2) | async-done | bytes 2097184 | tf_op jit(solution)/shard_map/all_to_all | solution.py:204
  170.4 9.5 %all-to-all-start.3 = ((bf16[16,8,32,256]{3,2,1,0:T(8,128)(2,1)}), bf16[16,8,32,256]{3,2,1,0:T(8,128)(2,1)}, u32[]{:S(2)}, u32[]{:S(2)}) async-start(bf16[16,8,32,256]{3,2,1,0:T(8,128)(2,1)} %copy-done.1), calls=%async_computation.3 | async-start | bytes 4194304 | tf_op jit(solution)/shard_map/all_to_all | solution.py:204
  179.9 1.0 copy.47
  180.9 1.1 copy.48
  182.0 1.1 copy.49
  183.0 1.4 add_bitcast_fusion.gates_ref
  184.5 1.5 shard_map.85
  186.0 11.8 %all-to-all-done.3.rows_ref = bf16[16,8,32,256]{3,2,1,0:T(8,128)(2,1)} async-done(((bf16[16,8,32,256]{3,2,1,0:T(8,128)(2,1)}), bf16[16,8,32,256]{3,2,1,0:T(8,128)(2,1)}, u32[]{:S(2)}, u32[]{:S(2)}) %all-to-all-start.3) | async-done | bytes 2097184 | tf_op jit(solution)/shard_map/all_to_all | solution.py:204
  197.9 2.6 %shard_map.87 = bf16[8,64,256]{2,1,0:T(8,128)(2,1)S(1)} custom-call(f32[16,64,4]{2,1,0:T(8,128)S(1)} %get-tuple-element.10.slots_ref, f32[16,64,4]{2,1,0:T(8,128)S(1)} %add_bitcast_fusion.gates_ref, bf16[16,8,32,256]{3,2,1,0:T(8,128)(2,1)} %all-to-all-done.3.rows_ref), custom_call_target="tpu_custom_call" | custom-call | flops 268435456 | bytes 3145728 | tf_op jit(solution)/shard_map/pallas_call | solution.py:108
  200.6 25.0 %all_to_all.25 = bf16[16,64,256]{2,1,0:T(8,128)(2,1)S(1)} all-to-all(bf16[16,64,256]{2,1,0:T(8,128)(2,1)S(1)} %pad_maximum_fusion), channel_id=1, replica_groups=mesh['x'=4,'y'=4,'z'=16,'core'=2] {'z'}, dimensions={0} | all-to-all | bytes 1048576 | tf_op jit(solution)/shard_map/all_to_all | solution.py:208
  225.5 0.1 convert_reduce_fusion
  225.6 0.6 add_convert_fusion
  (21 shorter events, 0.3 us)
Async XLA Ops:
  6.5 47.9 %copy-start = (bf16[64,256]{1,0:T(8,128)(2,1)S(1)}, bf16[64,256]{1,0:T(8,128)(2,1)}, u32[]{:S(2)}) copy-start(bf16[64,256]{1,0:T(8,128)(2,1)} %param.8) | copy-start | bytes 98308
  6.5 3.5 %copy-start.8 = (s32[64,4]{0,1:T(4,128)S(1)}, s32[64,4]{0,1:T(4,128)}, u32[]{:S(2)}) copy-start(s32[64,4]{0,1:T(4,128)} %param.12) | copy-start | bytes 3076
  6.5 3.5 %copy-start.9 = (f32[64,4]{0,1:T(4,128)S(1)}, f32[64,4]{0,1:T(4,128)}, u32[]{:S(2)}) copy-start(f32[64,4]{0,1:T(4,128)} %param.13) | copy-start | bytes 3076
  6.5 117.1 %all-gather.5.cloned.1.call-start = ((), (), s32[]{:S(2)}) async-start(), calls=%async_computation.5 | async-start | bytes 6291456 | tf_op jit(solution)/shard_map/all_gather | solution.py:212
  7.3 116.4 %all-gather.7.cloned.1.call-start = ((), (), s32[]{:S(2)}) async-start(), calls=%async_computation.6 | async-start | bytes 6291456 | tf_op jit(solution)/shard_map/all_gather | solution.py:213
  8.1 3.1 %collective-permute-start = (bf16[64,128]{1,0:T(8,128)(2,1)S(1)}, bf16[64,128]{1,0:T(8,128)(2,1)S(1)}, u32[]{:S(2)}, u32[]{:S(2)}) collective-permute-start(bf16[64,128]{1,0:T(8,128)(2,1)S(1)} %broadcast_select_fusion.2), channel_id=1, source_target_pairs={{0,1},{1,0},{2,3},{3,2},{4,5},{5,4},{6,7},{7,6},{8,9},{9,8},{10,11... | collective-permute-start | bytes 49160 | tf_op jit(solution)/shard_map/ppermute | solution.py:28
  50.6 3.8 %collective-permute-start.1 = (bf16[2048,128]{1,0:T(8,128)(2,1)S(1)}, bf16[2048,128]{1,0:T(8,128)(2,1)S(1)}, u32[]{:S(2)}, u32[]{:S(2)}) collective-permute-start(bf16[2048,128]{1,0:T(8,128)(2,1)S(1)} %bitcast.53), channel_id=1, source_target_pairs={{0,1},{1,0},{2,3},{3,2},{4,5},{5,4},{6,7},{7,6},{8,9},{9,8},{10,11... | collective-permute-start | bytes 1572872 | tf_op jit(solution)/shard_map/ppermute | solution.py:28
  55.1 0.8 copy-start.7
  87.2 28.4 %all-to-all-start = ((bf16[16,8,32,256]{3,2,1,0:T(8,128)(2,1)}), bf16[16,8,32,256]{3,2,1,0:T(8,128)(2,1)S(1)}, u32[]{:S(2)}, u32[]{:S(2)}) async-start(bf16[16,8,32,256]{3,2,1,0:T(8,128)(2,1)} %shard_map.82), calls=%async_computation | async-start | bytes 4194304 | tf_op jit(solution)/shard_map/all_to_all | solution.py:204
  115.6 1.4 copy-start.4
  117.0 26.3 %all-to-all-start.1 = ((bf16[16,8,32,256]{3,2,1,0:T(8,128)(2,1)}), bf16[16,8,32,256]{3,2,1,0:T(8,128)(2,1)S(1)}, u32[]{:S(2)}, u32[]{:S(2)}) async-start(bf16[16,8,32,256]{3,2,1,0:T(8,128)(2,1)} %shard_map.84), calls=%async_computation.1 | async-start | bytes 4194304 | tf_op jit(solution)/shard_map/all_to_all | solution.py:204
  123.7 1.6 copy-start.5
  132.8 1.4 copy-start.6
  143.2 1.3 copy-start.2
  144.6 25.8 %all-to-all-start.2 = ((bf16[16,8,32,256]{3,2,1,0:T(8,128)(2,1)}), bf16[16,8,32,256]{3,2,1,0:T(8,128)(2,1)S(1)}, u32[]{:S(2)}, u32[]{:S(2)}) async-start(bf16[16,8,32,256]{3,2,1,0:T(8,128)(2,1)} %copy-done.6), calls=%async_computation.2 | async-start | bytes 4194304 | tf_op jit(solution)/shard_map/all_to_all | solution.py:204
  151.1 1.6 copy-start.3
  160.2 1.3 copy-start.1
  170.4 27.5 %all-to-all-start.3 = ((bf16[16,8,32,256]{3,2,1,0:T(8,128)(2,1)}), bf16[16,8,32,256]{3,2,1,0:T(8,128)(2,1)}, u32[]{:S(2)}, u32[]{:S(2)}) async-start(bf16[16,8,32,256]{3,2,1,0:T(8,128)(2,1)} %copy-done.1), calls=%async_computation.3 | async-start | bytes 4194304 | tf_op jit(solution)/shard_map/all_to_all | solution.py:204
Sparse Core Ops, SparseCore 0:
  9.5 28.5 all-gather.4
  40.2 25.4 all-gather.6

commit v7 on v6

--- a/solution.py
+++ b/solution.py
@@ -28,19 +28,23 @@
     return lax.ppermute(x, "core", [(0, 1), (1, 0)])
 
 
+def swap_chips(x):
+    return lax.all_to_all(x, "z", split_axis=0, concat_axis=0, tiled=True)
+
+
+def gather_chips(x):
+    return swap_chips(jnp.broadcast_to(x[None], (Z,) + x.shape))
+
+
 def gather_kv(keys, values, notes):
-    group = lax.axis_index(E) // 2
-    core = lax.axis_index("core")
-    k = lax.dynamic_slice_in_dim(keys, group * HEAD_DIM, HEAD_DIM, 1)
-    v = lax.dynamic_slice_in_dim(values, group * HEAD_DIM, HEAD_DIM, 1)
-    first = core == 0
-    came = swap_cores(jnp.where(first, v, k))
-    kept = jnp.where(first, k, v)
-    chip = jnp.concatenate([jnp.where(first, kept, came), jnp.where(first, came, kept), notes], axis=0)
-    all_chips = lax.all_gather(chip, "z", axis=0)
-    mine = all_chips[:, : 2 * BLOCK].reshape(-1, HEAD_DIM)
-    other = swap_cores(mine)
-    return jnp.where(first, mine, other), jnp.where(first, other, mine), all_chips[:, 2 * BLOCK :]
+    first = lax.axis_index(E) // 2 * HEAD_DIM
+    k = lax.dynamic_slice_in_dim(keys, first, HEAD_DIM, 1)
+    v = lax.dynamic_slice_in_dim(values, first, HEAD_DIM, 1)
+    sent = jnp.concatenate([jnp.concatenate([k, v], axis=1), notes], axis=0)
+    came = gather_chips(sent)
+    mine = came[:, :BLOCK]
+    both = jnp.stack([mine, swap_cores(mine)])
+    return both[..., :HEAD_DIM], both[..., HEAD_DIM:], came[:, BLOCK:]
 
 
 def notes_of(ids, ranks, gates):
@@ -49,13 +53,17 @@
     middle = lax.reduce_precision(rest, 8, 7)
     low = rest - middle
     parts = [ids.astype(jnp.float32), ranks.astype(jnp.float32), top, middle, low]
-    rows = jnp.concatenate([p.T.reshape(2, 128) for p in parts], axis=0).astype(jnp.bfloat16)
-    return jnp.pad(rows, ((0, 6), (0, 0)))
+    rows = jnp.concatenate([p.T.reshape(1, TOPK * BLOCK) for p in parts], axis=0).astype(jnp.bfloat16)
+    return jnp.pad(rows, ((0, 11), (0, 0)))
 
 
 def read_notes(notes):
-    rows = notes[:, :10].astype(jnp.float32).reshape(Z, 5, TOPK, BLOCK)
+    rows = notes[:, :5].astype(jnp.float32).reshape(Z, 5, TOPK, BLOCK)
     return rows[:, 0] * EXP_CAP + rows[:, 1], rows[:, 2] + rows[:, 3] + rows[:, 4]
+
+
+def in_hbm(x):
+    return pltpu.with_memory_space_constraint(x, pltpu.MemorySpace.HBM)
 
 
 def place_kernel(slots_ref, rows_ref, out_ref):
@@ -81,10 +89,10 @@
             pl.BlockSpec((step, BLOCK, WIDTH), lambda i: (first + i, 0, 0)),
         ],
         out_specs=pl.BlockSpec((EXPERTS, step, EXP_CAP, WIDTH), lambda i: (0, i, 0, 0)),
-        out_shape=jax.ShapeDtypeStruct((EXPERTS, count, EXP_CAP, WIDTH), jnp.bfloat16),
-        compiler_params=pltpu.CompilerParams(vmem_limit_bytes=32 * MIB),
+        out_shape=pltpu.MemorySpace.HBM((EXPERTS, count, EXP_CAP, WIDTH), jnp.bfloat16),
+        compiler_params=pltpu.CompilerParams(vmem_limit_bytes=63 * MIB),
         cost_estimate=pl.CostEstimate(flops=2 * Z * 512 * 64 * 128, bytes_accessed=3 * MIB, transcendentals=0),
-    )(slots, rows)
+    )(slots, in_hbm(rows))
 
 
 def mix_kernel(slots_ref, gates_ref, rows_ref, out_ref):
@@ -114,10 +122,10 @@
             pl.BlockSpec((EXPERTS, step, EXP_CAP, WIDTH), lambda i: (0, i, 0, 0)),
         ],
         out_specs=pl.BlockSpec((step, BLOCK, WIDTH), lambda i: (i, 0, 0)),
-        out_shape=jax.ShapeDtypeStruct((count, BLOCK, WIDTH), jnp.bfloat16),
-        compiler_params=pltpu.CompilerParams(vmem_limit_bytes=32 * MIB),
+        out_shape=pltpu.MemorySpace.HBM((count, BLOCK, WIDTH), jnp.bfloat16),
+        compiler_params=pltpu.CompilerParams(vmem_limit_bytes=63 * MIB),
         cost_estimate=pl.CostEstimate(flops=4 * Z * 512 * 64 * 128, bytes_accessed=3 * MIB, transcendentals=0),
-    )(slots, gates, rows)
+    )(slots, gates, in_hbm(rows))
 
 
 def expert_kernel(rows_ref, in_ref, down_ref, out_ref, raw, normed):
@@ -159,35 +167,39 @@
         grid=(count // group,),
         in_specs=[
             spec,
-            pl.BlockSpec(w_in.shape, lambda i: (0, 0, 0)),
-            pl.BlockSpec(w_down.shape, lambda i: (0, 0, 0)),
+            pl.BlockSpec(w_in.shape, lambda i: (0, 0, 0), pipeline_mode=pl.Buffered(1)),
+            pl.BlockSpec(w_down.shape, lambda i: (0, 0, 0), pipeline_mode=pl.Buffered(1)),
         ],
         out_specs=spec,
-        out_shape=jax.ShapeDtypeStruct(rows.shape, jnp.bfloat16),
+        out_shape=pltpu.MemorySpace.HBM(rows.shape, jnp.bfloat16),
         scratch_shapes=[
             pltpu.VMEM((group * EXP_CAP, width), jnp.float32),
             pltpu.VMEM((group * EXP_CAP, width), jnp.bfloat16),
         ],
-        compiler_params=pltpu.CompilerParams(vmem_limit_bytes=48 * MIB),
+        compiler_params=pltpu.CompilerParams(vmem_limit_bytes=63 * MIB),
         cost_estimate=pl.CostEstimate(flops=2 * 512 * 512 * width, bytes_accessed=12 * MIB, transcendentals=256 * 512),
-    )(rows, w_in, w_down)
-
-
-def attend(query, k, v, tensor_place):
-    block = query.shape[0]
+    )(in_hbm(rows), in_hbm(w_in), in_hbm(w_down))
+
+
+def attend(query, k, v):
     heads = query.shape[1] // HEAD_DIM
-    total = k.shape[0]
-    q = query.reshape(block, heads, HEAD_DIM)
+    chip, core = lax.axis_index("z"), lax.axis_index("core")
+    q = query.reshape(BLOCK, heads, HEAD_DIM)
+    k = k.reshape(-1, HEAD_DIM)
+    v = v.reshape(-1, HEAD_DIM)
     scores = jnp.einsum("qhd,kd->hqk", q, k, preferred_element_type=jnp.float32)
     scores = scores / math.sqrt(HEAD_DIM)
-    query_pos = tensor_place * block + jnp.arange(block)
-    causal = query_pos[:, None] >= jnp.arange(total)[None, :]
+    place = jnp.arange(k.shape[0])
+    key_core = jnp.where(place < Z * BLOCK, core, 1 - core)
+    key_pos = (place // BLOCK % Z * 2 + key_core) * BLOCK + place % BLOCK
+    query_pos = (chip * 2 + core) * BLOCK + jnp.arange(BLOCK)
+    causal = query_pos[:, None] >= key_pos[None, :]
     scores = jnp.where(causal[None], scores, -1e30)
     top = jnp.max(scores, axis=-1, keepdims=True)
     raised = jnp.exp(scores - top)
     probs = (raised / jnp.sum(raised, axis=-1, keepdims=True)).astype(jnp.bfloat16)
     out = jnp.einsum("hqk,kd->qhd", probs, v, preferred_element_type=jnp.float32)
-    return out.reshape(block, heads * HEAD_DIM)
+    return out.reshape(BLOCK, heads * HEAD_DIM)
 
 
 def ranks_of(ids):
@@ -204,10 +216,6 @@
     return lax.all_to_all(x, E, split_axis=0, concat_axis=0, tiled=True)
 
 
-def swap_chips(x):
-    return lax.all_to_all(x, "z", split_axis=0, concat_axis=0, tiled=True)
-
-
 def per_device(query, keys, values, resid, route_ids, route_weight, w_in, w_down):
     w_in = lax.all_gather(w_in, "core", axis=0, tiled=True)
     w_down = lax.all_gather(w_down, "core", axis=0, tiled=True)
@@ -215,11 +223,11 @@
     gates = route_weight / jnp.sum(route_weight, axis=1, keepdims=True)
     k, v, notes = gather_kv(keys, values, notes_of(route_ids, ranks, gates))
     plane_slots, plane_gates = read_notes(notes)
-    attended = attend(query, k, v, lax.axis_index(T))
+    attended = attend(query, k, v)
     state = (resid.astype(jnp.float32) + attended).astype(jnp.bfloat16)
 
     slots_t, gates_t = plane_slots.transpose(0, 2, 1), plane_gates.transpose(0, 2, 1)
-    plane = lax.all_gather(state, "z", axis=0)
+    plane = gather_chips(state)
     rows = [swap_columns(place_rows(plane_slots, plane, part)) for part in range(PARTS)]
     outs = [experts(part, w_in, w_down) for part in rows]
     outs[0], rows[1] = lax.optimization_barrier((outs[0], rows[1]))

time: 236 us -> 285 us (1.21)
  waiting for transfers between devices: 50.4 us -> 126 us
  blocking collectives: 92.8 us -> 46.7 us
  starting transfers between devices: 34 us -> 52.6 us
  local copies, waits for them, and re-layouts: 13.3 us -> 6.43 us
  Pallas kernels: 23.5 us -> 30.1 us
  other arithmetic: 4.45 us -> 7.51 us
    all_gather x2 -> x0, blocking collectives: 67.8 us -> none  [the longest x1 38.6 us: gather_kv(): all_chips = lax.all_gather(chip, 'z', axis=0)]
    all_to_all x0 -> x2, waiting for transfers between devices: none -> 58.8 us  [swap_chips(): return lax.all_to_all(x, 'z', split_axis=0, concat_axis=0, tiled=True)]
    all_to_all x0 -> x2, starting transfers between devices: none -> 22.7 us  [swap_chips(): return lax.all_to_all(x, 'z', split_axis=0, concat_axis=0, tiled=True)]
    all_to_all x1, blocking collectives: 25 us -> 46.7 us  [swap_chips(): return lax.all_to_all(x, 'z', split_axis=0, concat_axis=0, tiled=True)]
    all_to_all x4, waiting for transfers between devices: 48.5 us -> 63.7 us  [swap_columns(): return lax.all_to_all(x, E, split_axis=0, concat_axis=0, tiled=True)]
    unnamed x25 -> x13, local copies, waits for them, and re-layouts: 12.5 us -> 2.4 us
  transfers between devices with their start and end apart: 8 -> 9, of which waited for: 6 -> 7; matrix products, arithmetic and copies ran while one was open for 4% -> 2% of each run, Pallas kernels for 9% -> 9%
where the time goes in v7:
time: 285 us; the launch traced here: 284 us
  waiting for transfers between devices  126 us (44%)
  starting transfers between devices  52.6 us (18%)
  blocking collectives  46.7 us (16%)
  Pallas kernels  30.1 us (11%)
  between operations  13.6 us (5%)
  other arithmetic  7.51 us (3%)
  local copies, waits for them, and re-layouts  6.43 us (2%)
    all_to_all x4, waiting for transfers between devices, swap_columns(): return lax.all_to_all(x, E, split_axis=0, concat_axis=0, tiled=True)  63.7 us
    all_to_all x2, waiting for transfers between devices, swap_chips(): return lax.all_to_all(x, 'z', split_axis=0, concat_axis=0, tiled=True)  58.8 us
    all_to_all x1, blocking collectives, swap_chips(): return lax.all_to_all(x, 'z', split_axis=0, concat_axis=0, tiled=True)  46.7 us
    all_to_all x4, starting transfers between devices, swap_columns(): return lax.all_to_all(x, E, split_axis=0, concat_axis=0, tiled=True)  27.9 us
    all_to_all x2, starting transfers between devices, swap_chips(): return lax.all_to_all(x, 'z', split_axis=0, concat_axis=0, tiled=True)  22.7 us
    pallas_call x2, Pallas kernels, experts(): pl.pallas_call(expert_kernel, grid=(count // group,), in_specs=[spec, pl....  17.3 us
    pallas_call x2, Pallas kernels, mix_rows(): pl.pallas_call(mix_kernel, grid=(count // step,), in_specs=[pl.BlockSpec(...  6.81 us
    pallas_call x2, Pallas kernels, place_rows(): pl.pallas_call(place_kernel, grid=(count // step,), in_specs=[pl.BlockSpe...  6.02 us
  transfers between devices with their start and end apart: 9, of which 7 were waited for; matrix products, arithmetic and copies ran while one was open for 2% of the time, Pallas kernels for 9%

profile of v7, /device:TPU:6, one launch (start us, length us, event | category | flops | bytes accessed | tf_op | source)
XLA Modules:
  0.0 283.7 jit_solution(10695855138613364598)
XLA Ops:
  6.5 0.0 copy-start
  6.5 0.7 fusion.17
  7.2 0.7 fusion.34
  7.9 0.7 reduce_sum.37
  8.6 0.7 fusion.36
  9.3 0.1 reshape.121
  9.4 0.1 reshape.122
  9.5 0.1 reshape.123
  9.6 0.1 convolution_convert_fusion
  9.7 0.7 select_reduce_fusion
  10.4 0.1 reshape.120
  10.5 0.1 reshape.119
  10.6 0.7 constant_dynamic-slice_fusion
  11.4 0.9 broadcast_in_dim.38
  12.3 15.2 %all-to-all-start = ((bf16[16,80,256]{2,1,0:T(8,128)(2,1)}), bf16[16,80,256]{2,1,0:T(8,128)(2,1)S(1)}, u32[]{:S(2)}, u32[]{:S(2)}) async-start(bf16[16,80,256]{2,1,0:T(8,128)(2,1)} %broadcast_in_dim.38), calls=%async_computation | async-start | bytes 1310720 | tf_op jit(solution)/shard_map/all_to_all | solution.py:32
  27.5 0.0 all-gather.3.cloned.1.call-start
  27.5 0.7 all-gather.3.cloned.1.call-update
  28.2 32.8 %all-to-all-done = bf16[16,80,256]{2,1,0:T(8,128)(2,1)S(1)} async-done(((bf16[16,80,256]{2,1,0:T(8,128)(2,1)}), bf16[16,80,256]{2,1,0:T(8,128)(2,1)S(1)}, u32[]{:S(2)}, u32[]{:S(2)}) %all-to-all-start) | async-done | bytes 655392 | tf_op jit(solution)/shard_map/all_to_all | solution.py:32
  61.0 0.1 fusion.41
  61.1 1.9 collective-permute-start
  63.1 0.1 broadcast_compare_fusion
  63.2 1.7 collective-permute-done
  64.9 0.3 pad_maximum_fusion
  65.2 0.0 copy-done
  65.2 0.6 fusion.43
  65.8 0.0 copy-start.3
  65.8 0.4 convolution_bitcast_fusion
  66.2 0.4 copy-done.3
  66.6 0.9 broadcast_in_dim.62
  67.5 7.5 %all-to-all-start.1 = ((bf16[16,64,256]{2,1,0:T(8,128)(2,1)}), bf16[16,64,256]{2,1,0:T(8,128)(2,1)S(1)}, u32[]{:S(2)}, u32[]{:S(2)}) async-start(bf16[16,64,256]{2,1,0:T(8,128)(2,1)} %broadcast_in_dim.62), calls=%async_computation.1 | async-start | bytes 1048576 | tf_op jit(solution)/shard_map/all_to_all | solution.py:32
  75.0 0.0 all-gather.5.cloned.1.call-start
  75.0 0.7 all-gather.5.cloned.1.call-update
  75.8 0.1 reshape.131
  75.9 0.2 copy.60
  76.2 0.2 copy.61
  76.4 0.9 fusion.7
  77.3 0.8 copy.57.slots_ref
  78.2 26.1 %all-to-all-done.1.rows_ref = bf16[16,64,256]{2,1,0:T(8,128)(2,1)S(1)} async-done(((bf16[16,64,256]{2,1,0:T(8,128)(2,1)}), bf16[16,64,256]{2,1,0:T(8,128)(2,1)S(1)}, u32[]{:S(2)}, u32[]{:S(2)}) %all-to-all-start.1) | async-done | bytes 524320 | tf_op jit(solution)/shard_map/all_to_all | solution.py:32
  104.2 0.8 copy-done.1
  105.0 3.0 %shard_map.82 = bf16[16,8,32,256]{3,2,1,0:T(8,128)(2,1)} custom-call(f32[16,4,64]{2,1,0:T(4,128)} %copy.57.slots_ref, bf16[16,64,256]{2,1,0:T(8,128)(2,1)} %copy-done.1), custom_call_target="tpu_custom_call" | custom-call | flops 134217728 | bytes 3145728 | tf_op jit(solution)/shard_map/pallas_call | solution.py:84
  108.0 7.4 %all-to-all-start.2 = ((bf16[16,8,32,256]{3,2,1,0:T(8,128)(2,1)}), bf16[16,8,32,256]{3,2,1,0:T(8,128)(2,1)}, u32[]{:S(2)}, u32[]{:S(2)}) async-start(bf16[16,8,32,256]{3,2,1,0:T(8,128)(2,1)} %shard_map.82), calls=%async_computation.2 | async-start | bytes 4194304 | tf_op jit(solution)/shard_map/all_to_all | solution.py:216
  115.5 3.0 %shard_map.84 = bf16[16,8,32,256]{3,2,1,0:T(8,128)(2,1)} custom-call(f32[16,4,64]{2,1,0:T(4,128)} %copy.57.slots_ref, bf16[16,64,256]{2,1,0:T(8,128)(2,1)} %copy-done.1), custom_call_target="tpu_custom_call" | custom-call | flops 134217728 | bytes 3145728 | tf_op jit(solution)/shard_map/pallas_call | solution.py:84
  118.5 18.3 %all-to-all-done.2.rows_ref = bf16[16,8,32,256]{3,2,1,0:T(8,128)(2,1)} async-done(((bf16[16,8,32,256]{3,2,1,0:T(8,128)(2,1)}), bf16[16,8,32,256]{3,2,1,0:T(8,128)(2,1)}, u32[]{:S(2)}, u32[]{:S(2)}) %all-to-all-start.2) | async-done | bytes 2097184 | tf_op jit(solution)/shard_map/all_to_all | solution.py:216
  136.8 6.7 %all-to-all-start.3 = ((bf16[16,8,32,256]{3,2,1,0:T(8,128)(2,1)}), bf16[16,8,32,256]{3,2,1,0:T(8,128)(2,1)}, u32[]{:S(2)}, u32[]{:S(2)}) async-start(bf16[16,8,32,256]{3,2,1,0:T(8,128)(2,1)} %shard_map.84), calls=%async_computation.3 | async-start | bytes 4194304 | tf_op jit(solution)/shard_map/all_to_all | solution.py:216
  143.5 0.0 all-gather.3.cloned.1.call-done.in_ref
  143.5 0.0 all-gather.5.cloned.1.call-done.down_ref
  143.5 8.6 %shard_map.83 = bf16[16,8,32,256]{3,2,1,0:T(8,128)(2,1)} custom-call(bf16[16,8,32,256]{3,2,1,0:T(8,128)(2,1)} %all-to-all-done.2.rows_ref, bf16[2,4096,256]{2,1,0:T(8,128)(2,1)} %all-gather.3.cloned.1.call-done.in_ref, bf16[2,256,4096]{2,1,0:T(8,128)(2,1)} %all-gather.5.cloned.1.call-done.down_ref), custom_call_target="tpu_custom_call" | custom-call | flops 2147483648 | bytes 12582912 | tf_op jit(solution)/shard_map/pallas_call | solution.py:165
  152.1 11.9 %all-to-all-done.3.rows_ref = bf16[16,8,32,256]{3,2,1,0:T(8,128)(2,1)} async-done(((bf16[16,8,32,256]{3,2,1,0:T(8,128)(2,1)}), bf16[16,8,32,256]{3,2,1,0:T(8,128)(2,1)}, u32[]{:S(2)}, u32[]{:S(2)}) %all-to-all-start.3) | async-done | bytes 2097184 | tf_op jit(solution)/shard_map/all_to_all | solution.py:216
  164.0 6.6 %all-to-all-start.4 = ((bf16[16,8,32,256]{3,2,1,0:T(8,128)(2,1)}), bf16[16,8,32,256]{3,2,1,0:T(8,128)(2,1)}, u32[]{:S(2)}, u32[]{:S(2)}) async-start(bf16[16,8,32,256]{3,2,1,0:T(8,128)(2,1)} %shard_map.83), calls=%async_computation.4 | async-start | bytes 4194304 | tf_op jit(solution)/shard_map/all_to_all | solution.py:216
  170.6 8.6 %shard_map.86 = bf16[16,8,32,256]{3,2,1,0:T(8,128)(2,1)} custom-call(bf16[16,8,32,256]{3,2,1,0:T(8,128)(2,1)} %all-to-all-done.3.rows_ref, bf16[2,4096,256]{2,1,0:T(8,128)(2,1)} %all-gather.3.cloned.1.call-done.in_ref, bf16[2,256,4096]{2,1,0:T(8,128)(2,1)} %all-gather.5.cloned.1.call-done.down_ref), custom_call_target="tpu_custom_call" | custom-call | flops 2147483648 | bytes 12582912 | tf_op jit(solution)/shard_map/pallas_call | solution.py:165
  179.2 15.3 %all-to-all-done.4.rows_ref = bf16[16,8,32,256]{3,2,1,0:T(8,128)(2,1)} async-done(((bf16[16,8,32,256]{3,2,1,0:T(8,128)(2,1)}), bf16[16,8,32,256]{3,2,1,0:T(8,128)(2,1)}, u32[]{:S(2)}, u32[]{:S(2)}) %all-to-all-start.4) | async-done | bytes 2097184 | tf_op jit(solution)/shard_map/all_to_all | solution.py:216
  194.5 7.3 %all-to-all-start.5 = ((bf16[16,8,32,256]{3,2,1,0:T(8,128)(2,1)}), bf16[16,8,32,256]{3,2,1,0:T(8,128)(2,1)}, u32[]{:S(2)}, u32[]{:S(2)}) async-start(bf16[16,8,32,256]{3,2,1,0:T(8,128)(2,1)} %shard_map.86), calls=%async_computation.5 | async-start | bytes 4194304 | tf_op jit(solution)/shard_map/all_to_all | solution.py:216
  201.8 0.2 copy.62
  202.0 0.2 copy.63
  202.3 0.2 copy.64
  202.5 0.9 add_bitcast_fusion.gates_ref
  203.4 3.4 %shard_map.85 = bf16[8,64,256]{2,1,0:T(8,128)(2,1)} custom-call(f32[16,64,4]{2,1,0:T(8,128)} %get-tuple-element.12.slots_ref, f32[16,64,4]{2,1,0:T(8,128)} %add_bitcast_fusion.gates_ref, bf16[16,8,32,256]{3,2,1,0:T(8,128)(2,1)} %all-to-all-done.4.rows_ref), custom_call_target="tpu_custom_call" | custom-call | flops 268435456 | bytes 3145728 | tf_op jit(solution)/shard_map/pallas_call | solution.py:116
  206.8 18.2 %all-to-all-done.5.rows_ref = bf16[16,8,32,256]{3,2,1,0:T(8,128)(2,1)} async-done(((bf16[16,8,32,256]{3,2,1,0:T(8,128)(2,1)}), bf16[16,8,32,256]{3,2,1,0:T(8,128)(2,1)}, u32[]{:S(2)}, u32[]{:S(2)}) %all-to-all-start.5) | async-done | bytes 2097184 | tf_op jit(solution)/shard_map/all_to_all | solution.py:216
  225.1 3.4 %shard_map.87 = bf16[8,64,256]{2,1,0:T(8,128)(2,1)} custom-call(f32[16,64,4]{2,1,0:T(8,128)} %get-tuple-element.12.slots_ref, f32[16,64,4]{2,1,0:T(8,128)} %add_bitcast_fusion.gates_ref, bf16[16,8,32,256]{3,2,1,0:T(8,128)(2,1)} %all-to-all-done.5.rows_ref), custom_call_target="tpu_custom_call" | custom-call | flops 268435456 | bytes 3145728 | tf_op jit(solution)/shard_map/pallas_call | solution.py:116
  228.5 0.0 copy-done.2
  228.5 1.0 pad_maximum_fusion.1
  229.5 46.7 %all_to_all.35 = bf16[16,64,256]{2,1,0:T(8,128)(2,1)S(1)} all-to-all(bf16[16,64,256]{2,1,0:T(8,128)(2,1)S(1)} %pad_maximum_fusion.1), channel_id=1, replica_groups=mesh['x'=4,'y'=4,'z'=16,'core'=2] {'z'}, dimensions={0} | all-to-all | bytes 1048576 | tf_op jit(solution)/shard_map/all_to_all | solution.py:32
  276.1 0.1 convert_reduce_fusion
  276.2 0.6 add_convert_fusion
  (12 shorter events, 0.1 us)
Async XLA Ops:
  6.5 58.7 %copy-start = (bf16[64,256]{1,0:T(8,128)(2,1)S(1)}, bf16[64,256]{1,0:T(8,128)(2,1)}, u32[]{:S(2)}) copy-start(bf16[64,256]{1,0:T(8,128)(2,1)} %param.8) | copy-start | bytes 98308
  12.3 48.7 %all-to-all-start = ((bf16[16,80,256]{2,1,0:T(8,128)(2,1)}), bf16[16,80,256]{2,1,0:T(8,128)(2,1)S(1)}, u32[]{:S(2)}, u32[]{:S(2)}) async-start(bf16[16,80,256]{2,1,0:T(8,128)(2,1)} %broadcast_in_dim.38), calls=%async_computation | async-start | bytes 1310720 | tf_op jit(solution)/shard_map/all_to_all | solution.py:32
  27.5 116.0 %all-gather.3.cloned.1.call-start = ((), (), s32[]{:S(2)}) async-start(), calls=%async_computation.7 | async-start | bytes 6291456 | tf_op jit(solution)/shard_map/all_gather | solution.py:220
  61.1 3.8 %collective-permute-start = (bf16[16,64,256]{2,1,0:T(8,128)(2,1)S(1)}, bf16[16,64,256]{2,1,0:T(8,128)(2,1)S(1)}, u32[]{:S(2)}, u32[]{:S(2)}) collective-permute-start(bf16[16,64,256]{2,1,0:T(8,128)(2,1)S(1)} %get-tuple-element.13), channel_id=1, source_target_pairs={{0,1},{1,0},{2,3},{3,2},{4,5},{5,4},{6,7},{7,6},{8,9},{9,8},{10,11... | collective-permute-start | bytes 1572872 | tf_op jit(solution)/shard_map/ppermute | solution.py:28
  65.8 0.8 copy-start.3
  67.5 36.7 %all-to-all-start.1 = ((bf16[16,64,256]{2,1,0:T(8,128)(2,1)}), bf16[16,64,256]{2,1,0:T(8,128)(2,1)S(1)}, u32[]{:S(2)}, u32[]{:S(2)}) async-start(bf16[16,64,256]{2,1,0:T(8,128)(2,1)} %broadcast_in_dim.62), calls=%async_computation.1 | async-start | bytes 1048576 | tf_op jit(solution)/shard_map/all_to_all | solution.py:32
  75.0 68.5 %all-gather.5.cloned.1.call-start = ((), (), s32[]{:S(2)}) async-start(), calls=%async_computation.8 | async-start | bytes 6291456 | tf_op jit(solution)/shard_map/all_gather | solution.py:221
  104.2 0.8 copy-start.1
  108.0 28.8 %all-to-all-start.2 = ((bf16[16,8,32,256]{3,2,1,0:T(8,128)(2,1)}), bf16[16,8,32,256]{3,2,1,0:T(8,128)(2,1)}, u32[]{:S(2)}, u32[]{:S(2)}) async-start(bf16[16,8,32,256]{3,2,1,0:T(8,128)(2,1)} %shard_map.82), calls=%async_computation.2 | async-start | bytes 4194304 | tf_op jit(solution)/shard_map/all_to_all | solution.py:216
  136.8 27.2 %all-to-all-start.3 = ((bf16[16,8,32,256]{3,2,1,0:T(8,128)(2,1)}), bf16[16,8,32,256]{3,2,1,0:T(8,128)(2,1)}, u32[]{:S(2)}, u32[]{:S(2)}) async-start(bf16[16,8,32,256]{3,2,1,0:T(8,128)(2,1)} %shard_map.84), calls=%async_computation.3 | async-start | bytes 4194304 | tf_op jit(solution)/shard_map/all_to_all | solution.py:216
  164.0 30.5 %all-to-all-start.4 = ((bf16[16,8,32,256]{3,2,1,0:T(8,128)(2,1)}), bf16[16,8,32,256]{3,2,1,0:T(8,128)(2,1)}, u32[]{:S(2)}, u32[]{:S(2)}) async-start(bf16[16,8,32,256]{3,2,1,0:T(8,128)(2,1)} %shard_map.83), calls=%async_computation.4 | async-start | bytes 4194304 | tf_op jit(solution)/shard_map/all_to_all | solution.py:216
  194.5 30.6 %all-to-all-start.5 = ((bf16[16,8,32,256]{3,2,1,0:T(8,128)(2,1)}), bf16[16,8,32,256]{3,2,1,0:T(8,128)(2,1)}, u32[]{:S(2)}, u32[]{:S(2)}) async-start(bf16[16,8,32,256]{3,2,1,0:T(8,128)(2,1)} %shard_map.86), calls=%async_computation.5 | async-start | bytes 4194304 | tf_op jit(solution)/shard_map/all_to_all | solution.py:216
  206.8 21.6 %copy-start.2 = (bf16[8,64,256]{2,1,0:T(8,128)(2,1)S(1)}, bf16[8,64,256]{2,1,0:T(8,128)(2,1)}, u32[]{:S(2)}) copy-start(bf16[8,64,256]{2,1,0:T(8,128)(2,1)} %shard_map.85) | copy-start | bytes 786436
Sparse Core Ops, SparseCore 0:
  30.4 25.3 all-gather.2
  77.9 25.3 all-gather.4

commit v8 on v7

--- a/solution.py
+++ b/solution.py
@@ -32,19 +32,13 @@
     return lax.all_to_all(x, "z", split_axis=0, concat_axis=0, tiled=True)
 
 
-def gather_chips(x):
-    return swap_chips(jnp.broadcast_to(x[None], (Z,) + x.shape))
-
-
-def gather_kv(keys, values, notes):
+def gather_kv(keys, values):
     first = lax.axis_index(E) // 2 * HEAD_DIM
     k = lax.dynamic_slice_in_dim(keys, first, HEAD_DIM, 1)
     v = lax.dynamic_slice_in_dim(values, first, HEAD_DIM, 1)
-    sent = jnp.concatenate([jnp.concatenate([k, v], axis=1), notes], axis=0)
-    came = gather_chips(sent)
-    mine = came[:, :BLOCK]
+    mine = lax.all_gather(jnp.concatenate([k, v], axis=1), "z", axis=0)
     both = jnp.stack([mine, swap_cores(mine)])
-    return both[..., :HEAD_DIM], both[..., HEAD_DIM:], came[:, BLOCK:]
+    return both[..., :HEAD_DIM], both[..., HEAD_DIM:]
 
 
 def notes_of(ids, ranks, gates):
@@ -219,15 +213,16 @@
 def per_device(query, keys, values, resid, route_ids, route_weight, w_in, w_down):
     w_in = lax.all_gather(w_in, "core", axis=0, tiled=True)
     w_down = lax.all_gather(w_down, "core", axis=0, tiled=True)
+    k, v = gather_kv(keys, values)
+    attended = attend(query, k, v)
+    state = (resid.astype(jnp.float32) + attended).astype(jnp.bfloat16)
+
     ranks = ranks_of(route_ids)
     gates = route_weight / jnp.sum(route_weight, axis=1, keepdims=True)
-    k, v, notes = gather_kv(keys, values, notes_of(route_ids, ranks, gates))
-    plane_slots, plane_gates = read_notes(notes)
-    attended = attend(query, k, v)
-    state = (resid.astype(jnp.float32) + attended).astype(jnp.bfloat16)
-
+    sent = jnp.concatenate([state, notes_of(route_ids, ranks, gates)], axis=0)
+    plane = lax.all_gather(sent, "z", axis=0)
+    plane_slots, plane_gates = read_notes(plane[:, BLOCK:])
     slots_t, gates_t = plane_slots.transpose(0, 2, 1), plane_gates.transpose(0, 2, 1)
-    plane = gather_chips(state)
     rows = [swap_columns(place_rows(plane_slots, plane, part)) for part in range(PARTS)]
     outs = [experts(part, w_in, w_down) for part in rows]
     outs[0], rows[1] = lax.optimization_barrier((outs[0], rows[1]))

time: 285 us -> 250 us (0.88)
  waiting for transfers between devices: 126 us -> 54.5 us
  blocking collectives: 46.7 us -> 113 us
  starting transfers between devices: 52.6 us -> 29.2 us
  other arithmetic: 7.51 us -> 4.09 us
    all_gather x0 -> x2, blocking collectives: none -> 68.4 us  [the longest x1 38.5 us: gather_kv(): mine = lax.all_gather(jnp.concatenate([k, v], axis=1), 'z', axis=0)]
    all_to_all x2 -> x0, waiting for transfers between devices: 58.8 us -> none  [swap_chips(): return lax.all_to_all(x, 'z', split_axis=0, concat_axis=0, tiled=True)]
    all_to_all x2 -> x0, starting transfers between devices: 22.7 us -> none  [swap_chips(): return lax.all_to_all(x, 'z', split_axis=0, concat_axis=0, tiled=True)]
    all_to_all x4, waiting for transfers between devices: 63.7 us -> 52.9 us  [swap_columns(): return lax.all_to_all(x, E, split_axis=0, concat_axis=0, tiled=True)]
  transfers between devices with their start and end apart: 9 -> 7, of which waited for: 7 -> 5; matrix products, arithmetic and copies ran while one was open for 2% -> 3% of each run, Pallas kernels for 9% -> 11%
where the time goes in v8:
time: 250 us; the launch traced here: 249 us
  blocking collectives  113 us (45%)
  waiting for transfers between devices  54.5 us (22%)
  Pallas kernels  30.4 us (12%)
  starting transfers between devices  29.2 us (12%)
  between operations  13.6 us (5%)
  other arithmetic  4.09 us (2%)
  local copies, waits for them, and re-layouts  3.79 us (2%)
    all_to_all x4, waiting for transfers between devices, swap_columns(): return lax.all_to_all(x, E, split_axis=0, concat_axis=0, tiled=True)  52.9 us
    all_to_all x1, blocking collectives, swap_chips(): return lax.all_to_all(x, 'z', split_axis=0, concat_axis=0, tiled=True)  44.2 us
    all_gather x1, blocking collectives, gather_kv(): mine = lax.all_gather(jnp.concatenate([k, v], axis=1), 'z', axis=0)  38.5 us
    all_gather x1, blocking collectives, per_device(): plane = lax.all_gather(sent, 'z', axis=0)  29.8 us
    all_to_all x4, starting transfers between devices, swap_columns(): return lax.all_to_all(x, E, split_axis=0, concat_axis=0, tiled=True)  27.3 us
    pallas_call x2, Pallas kernels, experts(): pl.pallas_call(expert_kernel, grid=(count // group,), in_specs=[spec, pl....  17.4 us
    pallas_call x2, Pallas kernels, mix_rows(): pl.pallas_call(mix_kernel, grid=(count // step,), in_specs=[pl.BlockSpec(...  6.83 us
    pallas_call x2, Pallas kernels, place_rows(): pl.pallas_call(place_kernel, grid=(count // step,), in_specs=[pl.BlockSpe...  6.16 us
  transfers between devices with their start and end apart: 7, of which 5 were waited for; matrix products, arithmetic and copies ran while one was open for 3% of the time, Pallas kernels for 11%

profile of v8, /device:TPU:6, one launch (start us, length us, event | category | flops | bytes accessed | tf_op | source)
XLA Modules:
  0.0 249.3 jit_solution(3185299589645881177)
XLA Ops:
  6.5 0.0 copy-start
  6.5 0.0 copy-start.4
  6.5 0.0 copy-start.5
  6.5 0.0 all-gather.5.cloned.1.call-start
  6.5 0.7 all-gather.5.cloned.1.call-update
  7.3 0.0 all-gather.7.cloned.1.call-start
  7.3 0.7 constant_dynamic-slice_fusion
  8.1 38.5 %all-gather = bf16[1024,256]{1,0:T(8,128)(2,1)S(1)} all-gather(bf16[64,256]{1,0:T(8,128)(2,1)S(1)} %pad_maximum_fusion.2), channel_id=2, replica_groups=mesh['x'=4,'y'=4,'z'=16,'core'=2] {'z'}, dimensions={0}, use_global_device_ids=true | all-gather | bytes 557056 | tf_op jit(solution)/shard_map/all_gather | solution.py:39
  46.6 1.9 collective-permute-start
  48.5 0.0 all-gather.7.cloned.1.call-update
  48.6 0.0 copy-done.4
  48.6 0.0 copy-done.5
  48.7 0.1 reshape.123
  48.8 0.1 reshape.124
  48.8 0.1 reshape.125
  48.9 0.1 convolution_convert_fusion
  49.1 0.1 reshape.122
  49.2 0.1 reshape.121
  49.3 0.1 broadcast_compare_fusion
  49.5 0.9 collective-permute-done
  50.4 0.3 pad_maximum_fusion
  50.7 0.0 copy-done
  50.7 0.6 fusion.42
  51.3 0.0 copy-start.3
  51.3 0.4 convolution_bitcast_fusion
  51.7 0.4 copy-done.3
  52.1 29.8 %all-gather.1 = bf16[1280,256]{1,0:T(8,128)(2,1)S(1)} all-gather(bf16[80,256]{1,0:T(8,128)(2,1)S(1)} %fusion.10), channel_id=3, replica_groups=mesh['x'=4,'y'=4,'z'=16,'core'=2] {'z'}, dimensions={0}, use_global_device_ids=true | all-gather | bytes 696320 | tf_op jit(solution)/shard_map/all_gather | solution.py:223
  82.0 0.0 copy-start.1
  82.0 0.1 reshape.135
  82.1 0.2 copy.60
  82.4 0.2 copy.61
  82.6 0.9 fusion.7
  83.5 0.8 copy.56.slots_ref
  84.4 0.0 copy-done.1
  84.4 3.1 %shard_map.82 = bf16[16,8,32,256]{3,2,1,0:T(8,128)(2,1)} custom-call(f32[16,4,64]{2,1,0:T(4,128)} %copy.56.slots_ref, bf16[16,80,256]{2,1,0:T(8,128)(2,1)} %bitcast.65), custom_call_target="tpu_custom_call" | custom-call | flops 134217728 | bytes 3145728 | tf_op jit(solution)/shard_map/pallas_call | solution.py:78
  87.4 7.4 %all-to-all-start = ((bf16[16,8,32,256]{3,2,1,0:T(8,128)(2,1)}), bf16[16,8,32,256]{3,2,1,0:T(8,128)(2,1)}, u32[]{:S(2)}, u32[]{:S(2)}) async-start(bf16[16,8,32,256]{3,2,1,0:T(8,128)(2,1)} %shard_map.82), calls=%async_computation | async-start | bytes 4194304 | tf_op jit(solution)/shard_map/all_to_all | solution.py:210
  94.9 3.1 %shard_map.84 = bf16[16,8,32,256]{3,2,1,0:T(8,128)(2,1)} custom-call(f32[16,4,64]{2,1,0:T(4,128)} %copy.56.slots_ref, bf16[16,80,256]{2,1,0:T(8,128)(2,1)} %bitcast.66), custom_call_target="tpu_custom_call" | custom-call | flops 134217728 | bytes 3145728 | tf_op jit(solution)/shard_map/pallas_call | solution.py:78
  98.0 18.1 %all-to-all-done.rows_ref = bf16[16,8,32,256]{3,2,1,0:T(8,128)(2,1)} async-done(((bf16[16,8,32,256]{3,2,1,0:T(8,128)(2,1)}), bf16[16,8,32,256]{3,2,1,0:T(8,128)(2,1)}, u32[]{:S(2)}, u32[]{:S(2)}) %all-to-all-start) | async-done | bytes 2097184 | tf_op jit(solution)/shard_map/all_to_all | solution.py:210
  116.1 6.7 %all-to-all-start.1 = ((bf16[16,8,32,256]{3,2,1,0:T(8,128)(2,1)}), bf16[16,8,32,256]{3,2,1,0:T(8,128)(2,1)}, u32[]{:S(2)}, u32[]{:S(2)}) async-start(bf16[16,8,32,256]{3,2,1,0:T(8,128)(2,1)} %shard_map.84), calls=%async_computation.1 | async-start | bytes 4194304 | tf_op jit(solution)/shard_map/all_to_all | solution.py:210
  122.8 0.0 all-gather.5.cloned.1.call-done.in_ref
  122.8 0.0 all-gather.7.cloned.1.call-done.down_ref
  122.8 8.7 %shard_map.83 = bf16[16,8,32,256]{3,2,1,0:T(8,128)(2,1)} custom-call(bf16[16,8,32,256]{3,2,1,0:T(8,128)(2,1)} %all-to-all-done.rows_ref, bf16[2,4096,256]{2,1,0:T(8,128)(2,1)} %all-gather.5.cloned.1.call-done.in_ref, bf16[2,256,4096]{2,1,0:T(8,128)(2,1)} %all-gather.7.cloned.1.call-done.down_ref), custom_call_target="tpu_custom_call" | custom-call | flops 2147483648 | bytes 12582912 | tf_op jit(solution)/shard_map/pallas_call | solution.py:159
  131.5 11.0 %all-to-all-done.1.rows_ref = bf16[16,8,32,256]{3,2,1,0:T(8,128)(2,1)} async-done(((bf16[16,8,32,256]{3,2,1,0:T(8,128)(2,1)}), bf16[16,8,32,256]{3,2,1,0:T(8,128)(2,1)}, u32[]{:S(2)}, u32[]{:S(2)}) %all-to-all-start.1) | async-done | bytes 2097184 | tf_op jit(solution)/shard_map/all_to_all | solution.py:210
  142.5 6.6 %all-to-all-start.2 = ((bf16[16,8,32,256]{3,2,1,0:T(8,128)(2,1)}), bf16[16,8,32,256]{3,2,1,0:T(8,128)(2,1)}, u32[]{:S(2)}, u32[]{:S(2)}) async-start(bf16[16,8,32,256]{3,2,1,0:T(8,128)(2,1)} %shard_map.83), calls=%async_computation.2 | async-start | bytes 4194304 | tf_op jit(solution)/shard_map/all_to_all | solution.py:210
  149.1 8.7 %shard_map.86 = bf16[16,8,32,256]{3,2,1,0:T(8,128)(2,1)} custom-call(bf16[16,8,32,256]{3,2,1,0:T(8,128)(2,1)} %all-to-all-done.1.rows_ref, bf16[2,4096,256]{2,1,0:T(8,128)(2,1)} %all-gather.5.cloned.1.call-done.in_ref, bf16[2,256,4096]{2,1,0:T(8,128)(2,1)} %all-gather.7.cloned.1.call-done.down_ref), custom_call_target="tpu_custom_call" | custom-call | flops 2147483648 | bytes 12582912 | tf_op jit(solution)/shard_map/pallas_call | solution.py:159
  157.7 10.2 %all-to-all-done.2.rows_ref = bf16[16,8,32,256]{3,2,1,0:T(8,128)(2,1)} async-done(((bf16[16,8,32,256]{3,2,1,0:T(8,128)(2,1)}), bf16[16,8,32,256]{3,2,1,0:T(8,128)(2,1)}, u32[]{:S(2)}, u32[]{:S(2)}) %all-to-all-start.2) | async-done | bytes 2097184 | tf_op jit(solution)/shard_map/all_to_all | solution.py:210
  168.0 6.6 %all-to-all-start.3 = ((bf16[16,8,32,256]{3,2,1,0:T(8,128)(2,1)}), bf16[16,8,32,256]{3,2,1,0:T(8,128)(2,1)}, u32[]{:S(2)}, u32[]{:S(2)}) async-start(bf16[16,8,32,256]{3,2,1,0:T(8,128)(2,1)} %shard_map.86), calls=%async_computation.3 | async-start | bytes 4194304 | tf_op jit(solution)/shard_map/all_to_all | solution.py:210
  174.5 0.2 copy.62
  174.7 0.2 copy.63
  175.0 0.2 copy.64
  175.2 0.9 add_bitcast_fusion.gates_ref
  176.2 3.4 %shard_map.85 = bf16[8,64,256]{2,1,0:T(8,128)(2,1)} custom-call(f32[16,64,4]{2,1,0:T(8,128)} %get-tuple-element.10.slots_ref, f32[16,64,4]{2,1,0:T(8,128)} %add_bitcast_fusion.gates_ref, bf16[16,8,32,256]{3,2,1,0:T(8,128)(2,1)} %all-to-all-done.2.rows_ref), custom_call_target="tpu_custom_call" | custom-call | flops 268435456 | bytes 3145728 | tf_op jit(solution)/shard_map/pallas_call | solution.py:110
  179.6 0.0 copy-start.2
  179.6 13.6 %all-to-all-done.3.rows_ref = bf16[16,8,32,256]{3,2,1,0:T(8,128)(2,1)} async-done(((bf16[16,8,32,256]{3,2,1,0:T(8,128)(2,1)}), bf16[16,8,32,256]{3,2,1,0:T(8,128)(2,1)}, u32[]{:S(2)}, u32[]{:S(2)}) %all-to-all-start.3) | async-done | bytes 2097184 | tf_op jit(solution)/shard_map/all_to_all | solution.py:210
  193.1 3.4 %shard_map.87 = bf16[8,64,256]{2,1,0:T(8,128)(2,1)} custom-call(f32[16,64,4]{2,1,0:T(8,128)} %get-tuple-element.10.slots_ref, f32[16,64,4]{2,1,0:T(8,128)} %add_bitcast_fusion.gates_ref, bf16[16,8,32,256]{3,2,1,0:T(8,128)(2,1)} %all-to-all-done.3.rows_ref), custom_call_target="tpu_custom_call" | custom-call | flops 268435456 | bytes 3145728 | tf_op jit(solution)/shard_map/pallas_call | solution.py:110
  196.6 0.0 copy-done.2
  196.6 1.0 pad_maximum_fusion.1
  197.6 44.2 %all_to_all.25 = bf16[16,64,256]{2,1,0:T(8,128)(2,1)S(1)} all-to-all(bf16[16,64,256]{2,1,0:T(8,128)(2,1)S(1)} %pad_maximum_fusion.1), channel_id=1, replica_groups=mesh['x'=4,'y'=4,'z'=16,'core'=2] {'z'}, dimensions={0} | all-to-all | bytes 1048576 | tf_op jit(solution)/shard_map/all_to_all | solution.py:32
  241.8 0.1 convert_reduce_fusion
  241.8 0.6 add_convert_fusion
  (15 shorter events, 0.2 us)
Async XLA Ops:
  6.5 44.2 %copy-start = (bf16[64,256]{1,0:T(8,128)(2,1)S(1)}, bf16[64,256]{1,0:T(8,128)(2,1)}, u32[]{:S(2)}) copy-start(bf16[64,256]{1,0:T(8,128)(2,1)} %param.8) | copy-start | bytes 98308
  6.5 42.0 %copy-start.4 = (s32[64,4]{0,1:T(4,128)S(1)}, s32[64,4]{0,1:T(4,128)}, u32[]{:S(2)}) copy-start(s32[64,4]{0,1:T(4,128)} %param.12) | copy-start | bytes 3076
  6.5 42.1 %copy-start.5 = (f32[64,4]{0,1:T(4,128)S(1)}, f32[64,4]{0,1:T(4,128)}, u32[]{:S(2)}) copy-start(f32[64,4]{0,1:T(4,128)} %param.13) | copy-start | bytes 3076
  6.5 116.2 %all-gather.5.cloned.1.call-start = ((), (), s32[]{:S(2)}) async-start(), calls=%async_computation.5 | async-start | bytes 6291456 | tf_op jit(solution)/shard_map/all_gather | solution.py:214
  7.3 115.5 %all-gather.7.cloned.1.call-start = ((), (), s32[]{:S(2)}) async-start(), calls=%async_computation.6 | async-start | bytes 6291456 | tf_op jit(solution)/shard_map/all_gather | solution.py:215
  46.6 3.8 %collective-permute-start = (bf16[16,64,256]{2,1,0:T(8,128)(2,1)S(1)}, bf16[16,64,256]{2,1,0:T(8,128)(2,1)S(1)}, u32[]{:S(2)}, u32[]{:S(2)}) collective-permute-start(bf16[16,64,256]{2,1,0:T(8,128)(2,1)S(1)} %bitcast.67), channel_id=1, source_target_pairs={{0,1},{1,0},{2,3},{3,2},{4,5},{5,4},{6,7},{7,6},{8,9},{9,8},{10,11... | collective-permute-start | bytes 1572872 | tf_op jit(solution)/shard_map/ppermute | solution.py:28
  51.3 0.8 copy-start.3
  82.0 2.4 copy-start.1
  87.4 28.6 %all-to-all-start = ((bf16[16,8,32,256]{3,2,1,0:T(8,128)(2,1)}), bf16[16,8,32,256]{3,2,1,0:T(8,128)(2,1)}, u32[]{:S(2)}, u32[]{:S(2)}) async-start(bf16[16,8,32,256]{3,2,1,0:T(8,128)(2,1)} %shard_map.82), calls=%async_computation | async-start | bytes 4194304 | tf_op jit(solution)/shard_map/all_to_all | solution.py:210
  116.1 26.4 %all-to-all-start.1 = ((bf16[16,8,32,256]{3,2,1,0:T(8,128)(2,1)}), bf16[16,8,32,256]{3,2,1,0:T(8,128)(2,1)}, u32[]{:S(2)}, u32[]{:S(2)}) async-start(bf16[16,8,32,256]{3,2,1,0:T(8,128)(2,1)} %shard_map.84), calls=%async_computation.1 | async-start | bytes 4194304 | tf_op jit(solution)/shard_map/all_to_all | solution.py:210
  142.5 25.5 %all-to-all-start.2 = ((bf16[16,8,32,256]{3,2,1,0:T(8,128)(2,1)}), bf16[16,8,32,256]{3,2,1,0:T(8,128)(2,1)}, u32[]{:S(2)}, u32[]{:S(2)}) async-start(bf16[16,8,32,256]{3,2,1,0:T(8,128)(2,1)} %shard_map.83), calls=%async_computation.2 | async-start | bytes 4194304 | tf_op jit(solution)/shard_map/all_to_all | solution.py:210
  168.0 25.2 %all-to-all-start.3 = ((bf16[16,8,32,256]{3,2,1,0:T(8,128)(2,1)}), bf16[16,8,32,256]{3,2,1,0:T(8,128)(2,1)}, u32[]{:S(2)}, u32[]{:S(2)}) async-start(bf16[16,8,32,256]{3,2,1,0:T(8,128)(2,1)} %shard_map.86), calls=%async_computation.3 | async-start | bytes 4194304 | tf_op jit(solution)/shard_map/all_to_all | solution.py:210
  179.6 17.0 %copy-start.2 = (bf16[8,64,256]{2,1,0:T(8,128)(2,1)S(1)}, bf16[8,64,256]{2,1,0:T(8,128)(2,1)}, u32[]{:S(2)}) copy-start(bf16[8,64,256]{2,1,0:T(8,128)(2,1)} %shard_map.85) | copy-start | bytes 786436
Sparse Core Ops, SparseCore 0:
  9.5 28.5 all-gather.4
  48.7 19.8 all-gather.6

commit v9 on v8

--- a/solution.py
+++ b/solution.py
@@ -60,33 +60,32 @@
     return pltpu.with_memory_space_constraint(x, pltpu.MemorySpace.HBM)
 
 
-def place_kernel(slots_ref, rows_ref, out_ref):
-    for z in range(slots_ref.shape[0]):
+def place_kernel(rows_ref, out_ref):
+    for z in range(rows_ref.shape[0]):
+        notes = rows_ref[z, BLOCK : BLOCK + 16, :].astype(jnp.float32)
+        slots = notes[0:1] * EXP_CAP + notes[1:2]
         grid = lax.broadcasted_iota(jnp.int32, (EXPERTS * EXP_CAP, BLOCK), 0).astype(jnp.float32)
-        hit = grid == slots_ref[z, 0:1, :]
+        hit = grid == slots[:, :BLOCK]
         for p in range(1, TOPK):
-            hit = jnp.logical_or(hit, grid == slots_ref[z, p : p + 1, :])
+            hit = jnp.logical_or(hit, grid == slots[:, p * BLOCK : (p + 1) * BLOCK])
         take = jnp.where(hit, 1.0, 0.0).astype(jnp.bfloat16)
-        out = jnp.dot(take, rows_ref[z], preferred_element_type=jnp.float32).astype(jnp.bfloat16)
+        out = jnp.dot(take, rows_ref[z, :BLOCK, :], preferred_element_type=jnp.float32).astype(jnp.bfloat16)
         out_ref[:, z] = out.reshape(EXPERTS, EXP_CAP, WIDTH)
 
 
-def place_rows(slots, rows, part):
+def place_rows(rows, part):
     step = 4
     count = Z // PARTS
     first = part * count // step
     return pl.pallas_call(
         place_kernel,
         grid=(count // step,),
-        in_specs=[
-            pl.BlockSpec((step, TOPK, BLOCK), lambda i: (first + i, 0, 0)),
-            pl.BlockSpec((step, BLOCK, WIDTH), lambda i: (first + i, 0, 0)),
-        ],
+        in_specs=[pl.BlockSpec((step,) + rows.shape[1:], lambda i: (first + i, 0, 0))],
         out_specs=pl.BlockSpec((EXPERTS, step, EXP_CAP, WIDTH), lambda i: (0, i, 0, 0)),
         out_shape=pltpu.MemorySpace.HBM((EXPERTS, count, EXP_CAP, WIDTH), jnp.bfloat16),
-        compiler_params=pltpu.CompilerParams(vmem_limit_bytes=63 * MIB),
+        compiler_params=pltpu.CompilerParams(vmem_limit_bytes=(16 if part == 0 else 63) * MIB),
         cost_estimate=pl.CostEstimate(flops=2 * Z * 512 * 64 * 128, bytes_accessed=3 * MIB, transcendentals=0),
-    )(slots, in_hbm(rows))
+    )(rows)
 
 
 def mix_kernel(slots_ref, gates_ref, rows_ref, out_ref):
@@ -116,10 +115,10 @@
             pl.BlockSpec((EXPERTS, step, EXP_CAP, WIDTH), lambda i: (0, i, 0, 0)),
         ],
         out_specs=pl.BlockSpec((step, BLOCK, WIDTH), lambda i: (i, 0, 0)),
-        out_shape=pltpu.MemorySpace.HBM((count, BLOCK, WIDTH), jnp.bfloat16),
-        compiler_params=pltpu.CompilerParams(vmem_limit_bytes=63 * MIB),
+        out_shape=jax.ShapeDtypeStruct((count, BLOCK, WIDTH), jnp.bfloat16),
+        compiler_params=pltpu.CompilerParams(vmem_limit_bytes=16 * MIB),
         cost_estimate=pl.CostEstimate(flops=4 * Z * 512 * 64 * 128, bytes_accessed=3 * MIB, transcendentals=0),
-    )(slots, gates, in_hbm(rows))
+    )(slots, gates, rows)
 
 
 def expert_kernel(rows_ref, in_ref, down_ref, out_ref, raw, normed):
@@ -223,7 +222,7 @@
     plane = lax.all_gather(sent, "z", axis=0)
     plane_slots, plane_gates = read_notes(plane[:, BLOCK:])
     slots_t, gates_t = plane_slots.transpose(0, 2, 1), plane_gates.transpose(0, 2, 1)
-    rows = [swap_columns(place_rows(plane_slots, plane, part)) for part in range(PARTS)]
+    rows = [swap_columns(place_rows(plane, part)) for part in range(PARTS)]
     outs = [experts(part, w_in, w_down) for part in rows]
     outs[0], rows[1] = lax.optimization_barrier((outs[0], rows[1]))
     mixes = [mix_rows(slots_t, gates_t, swap_columns(out), part) for part, out in enumerate(outs)]

time: 250 us -> 245 us (0.980)
  waiting for transfers between devices: 54.5 us -> 47.6 us
  local copies, waits for them, and re-layouts: 3.79 us -> 8.03 us
  Pallas kernels: 30.4 us -> 27.6 us
    all_to_all x4, waiting for transfers between devices: 52.9 us -> 46 us  [swap_columns(): return lax.all_to_all(x, E, split_axis=0, concat_axis=0, tiled=True)]
    unnamed x17 -> x19, local copies, waits for them, and re-layouts: 1.62 us -> 6.69 us
    pallas_call x2, Pallas kernels: 6.83 us -> 4.15 us  [mix_rows(): pl.pallas_call(mix_kernel, grid=(count // step,), in_specs=[pl.BlockSpec(...]
  transfers between devices with their start and end apart: 7 -> 7, of which waited for: 5 -> 5; matrix products, arithmetic and copies ran while one was open for 3% -> 4% of each run, Pallas kernels for 11% -> 11%
where the time goes in v9:
time: 245 us; the launch traced here: 244 us
  blocking collectives  113 us (46%)
  waiting for transfers between devices  47.6 us (19%)
  starting transfers between devices  29.2 us (12%)
  Pallas kernels  27.6 us (11%)
  between operations  13.6 us (6%)
  local copies, waits for them, and re-layouts  8.03 us (3%)
  other arithmetic  4.71 us (2%)
    all_to_all x4, waiting for transfers between devices, swap_columns(): return lax.all_to_all(x, E, split_axis=0, concat_axis=0, tiled=True)  46 us
    all_to_all x1, blocking collectives, swap_chips(): return lax.all_to_all(x, 'z', split_axis=0, concat_axis=0, tiled=True)  44.2 us
    all_gather x1, blocking collectives, gather_kv(): mine = lax.all_gather(jnp.concatenate([k, v], axis=1), 'z', axis=0)  38.5 us
    all_gather x1, blocking collectives, per_device(): plane = lax.all_gather(sent, 'z', axis=0)  29.8 us
    all_to_all x4, starting transfers between devices, swap_columns(): return lax.all_to_all(x, E, split_axis=0, concat_axis=0, tiled=True)  27.3 us
    pallas_call x2, Pallas kernels, experts(): pl.pallas_call(expert_kernel, grid=(count // group,), in_specs=[spec, pl....  17.4 us
    unnamed x19, local copies, waits for them, and re-layouts  6.69 us
    pallas_call x2, Pallas kernels, place_rows(): pl.pallas_call(place_kernel, grid=(count // step,), in_specs=[pl.BlockSpe...  6.07 us
  transfers between devices with their start and end apart: 7, of which 5 were waited for; matrix products, arithmetic and copies ran while one was open for 4% of the time, Pallas kernels for 11%

profile of v9, /device:TPU:6, one launch (start us, length us, event | category | flops | bytes accessed | tf_op | source)
XLA Modules:
  0.0 244.5 jit_solution(8166949331649010322)
XLA Ops:
  6.5 0.0 copy-start
  6.5 0.0 copy-start.5
  6.5 0.0 copy-start.6
  6.5 0.0 all-gather.5.cloned.1.call-start
  6.5 0.7 all-gather.5.cloned.1.call-update
  7.3 0.0 all-gather.7.cloned.1.call-start
  7.3 0.7 constant_dynamic-slice_fusion
  8.1 38.5 %all-gather = bf16[1024,256]{1,0:T(8,128)(2,1)S(1)} all-gather(bf16[64,256]{1,0:T(8,128)(2,1)S(1)} %pad_maximum_fusion.2), channel_id=2, replica_groups=mesh['x'=4,'y'=4,'z'=16,'core'=2] {'z'}, dimensions={0}, use_global_device_ids=true | all-gather | bytes 557056 | tf_op jit(solution)/shard_map/all_gather | solution.py:39
  46.6 1.9 collective-permute-start
  48.5 0.0 all-gather.7.cloned.1.call-update
  48.6 0.0 copy-done.5
  48.6 0.0 copy-done.6
  48.7 0.1 reshape.123
  48.8 0.1 reshape.124
  48.8 0.1 reshape.125
  48.9 0.1 convolution_convert_fusion
  49.1 0.1 reshape.122
  49.2 0.1 reshape.121
  49.3 0.1 broadcast_compare_fusion
  49.5 0.9 collective-permute-done
  50.4 0.3 pad_maximum_fusion
  50.7 0.0 copy-done
  50.7 0.6 fusion.40
  51.3 0.0 copy-start.4
  51.3 0.4 convolution_bitcast_fusion
  51.7 0.4 copy-done.4
  52.1 29.8 %all-gather.1 = bf16[1280,256]{1,0:T(8,128)(2,1)S(1)} all-gather(bf16[80,256]{1,0:T(8,128)(2,1)S(1)} %fusion.8), channel_id=3, replica_groups=mesh['x'=4,'y'=4,'z'=16,'core'=2] {'z'}, dimensions={0}, use_global_device_ids=true | all-gather | bytes 696320 | tf_op jit(solution)/shard_map/all_gather | solution.py:222
  82.0 0.0 copy-start.1
  82.0 2.6 %shard_map.82 = bf16[16,8,32,256]{3,2,1,0:T(8,128)(2,1)} custom-call(bf16[16,80,256]{2,1,0:T(8,128)(2,1)S(1)} %bitcast.63), custom_call_target="tpu_custom_call" | custom-call | flops 134217728 | bytes 3145728 | tf_op jit(solution)/shard_map/pallas_call | solution.py:80
  84.5 0.0 copy-done.1
  84.5 7.4 %all-to-all-start = ((bf16[16,8,32,256]{3,2,1,0:T(8,128)(2,1)}), bf16[16,8,32,256]{3,2,1,0:T(8,128)(2,1)}, u32[]{:S(2)}, u32[]{:S(2)}) async-start(bf16[16,8,32,256]{3,2,1,0:T(8,128)(2,1)} %shard_map.82), calls=%async_computation | async-start | bytes 4194304 | tf_op jit(solution)/shard_map/all_to_all | solution.py:209
  92.0 3.5 %shard_map.84 = bf16[16,8,32,256]{3,2,1,0:T(8,128)(2,1)} custom-call(bf16[16,80,256]{2,1,0:T(8,128)(2,1)} %bitcast.64), custom_call_target="tpu_custom_call" | custom-call | flops 134217728 | bytes 3145728 | tf_op jit(solution)/shard_map/pallas_call | solution.py:80
  95.5 17.7 %all-to-all-done.rows_ref = bf16[16,8,32,256]{3,2,1,0:T(8,128)(2,1)} async-done(((bf16[16,8,32,256]{3,2,1,0:T(8,128)(2,1)}), bf16[16,8,32,256]{3,2,1,0:T(8,128)(2,1)}, u32[]{:S(2)}, u32[]{:S(2)}) %all-to-all-start) | async-done | bytes 2097184 | tf_op jit(solution)/shard_map/all_to_all | solution.py:209
  113.2 6.7 %all-to-all-start.1 = ((bf16[16,8,32,256]{3,2,1,0:T(8,128)(2,1)}), bf16[16,8,32,256]{3,2,1,0:T(8,128)(2,1)}, u32[]{:S(2)}, u32[]{:S(2)}) async-start(bf16[16,8,32,256]{3,2,1,0:T(8,128)(2,1)} %shard_map.84), calls=%async_computation.1 | async-start | bytes 4194304 | tf_op jit(solution)/shard_map/all_to_all | solution.py:209
  119.8 0.0 all-gather.5.cloned.1.call-done.in_ref
  119.9 0.0 all-gather.7.cloned.1.call-done.down_ref
  119.9 8.7 %shard_map.83 = bf16[16,8,32,256]{3,2,1,0:T(8,128)(2,1)} custom-call(bf16[16,8,32,256]{3,2,1,0:T(8,128)(2,1)} %all-to-all-done.rows_ref, bf16[2,4096,256]{2,1,0:T(8,128)(2,1)} %all-gather.5.cloned.1.call-done.in_ref, bf16[2,256,4096]{2,1,0:T(8,128)(2,1)} %all-gather.7.cloned.1.call-done.down_ref), custom_call_target="tpu_custom_call" | custom-call | flops 2147483648 | bytes 12582912 | tf_op jit(solution)/shard_map/pallas_call | solution.py:158
  128.6 11.0 %all-to-all-done.1.rows_ref = bf16[16,8,32,256]{3,2,1,0:T(8,128)(2,1)} async-done(((bf16[16,8,32,256]{3,2,1,0:T(8,128)(2,1)}), bf16[16,8,32,256]{3,2,1,0:T(8,128)(2,1)}, u32[]{:S(2)}, u32[]{:S(2)}) %all-to-all-start.1) | async-done | bytes 2097184 | tf_op jit(solution)/shard_map/all_to_all | solution.py:209
  139.5 6.6 %all-to-all-start.2 = ((bf16[16,8,32,256]{3,2,1,0:T(8,128)(2,1)}), bf16[16,8,32,256]{3,2,1,0:T(8,128)(2,1)}, u32[]{:S(2)}, u32[]{:S(2)}) async-start(bf16[16,8,32,256]{3,2,1,0:T(8,128)(2,1)} %shard_map.83), calls=%async_computation.2 | async-start | bytes 4194304 | tf_op jit(solution)/shard_map/all_to_all | solution.py:209
  146.1 8.7 %shard_map.86 = bf16[16,8,32,256]{3,2,1,0:T(8,128)(2,1)} custom-call(bf16[16,8,32,256]{3,2,1,0:T(8,128)(2,1)} %all-to-all-done.1.rows_ref, bf16[2,4096,256]{2,1,0:T(8,128)(2,1)} %all-gather.5.cloned.1.call-done.in_ref, bf16[2,256,4096]{2,1,0:T(8,128)(2,1)} %all-gather.7.cloned.1.call-done.down_ref), custom_call_target="tpu_custom_call" | custom-call | flops 2147483648 | bytes 12582912 | tf_op jit(solution)/shard_map/pallas_call | solution.py:158
  154.8 10.2 %all-to-all-done.2.rows_ref = bf16[16,8,32,256]{3,2,1,0:T(8,128)(2,1)} async-done(((bf16[16,8,32,256]{3,2,1,0:T(8,128)(2,1)}), bf16[16,8,32,256]{3,2,1,0:T(8,128)(2,1)}, u32[]{:S(2)}, u32[]{:S(2)}) %all-to-all-start.2) | async-done | bytes 2097184 | tf_op jit(solution)/shard_map/all_to_all | solution.py:209
  165.0 6.6 %all-to-all-start.3 = ((bf16[16,8,32,256]{3,2,1,0:T(8,128)(2,1)}), bf16[16,8,32,256]{3,2,1,0:T(8,128)(2,1)S(1)}, u32[]{:S(2)}, u32[]{:S(2)}) async-start(bf16[16,8,32,256]{3,2,1,0:T(8,128)(2,1)} %shard_map.86), calls=%async_computation.3 | async-start | bytes 4194304 | tf_op jit(solution)/shard_map/all_to_all | solution.py:209
  171.6 0.8 slice_convert_fusion
  172.4 0.1 reshape.135
  172.6 1.0 copy.52
  173.6 1.1 copy.53
  174.7 1.0 copy.54
  175.8 0.2 copy.50
  176.0 1.1 copy.51
  177.1 1.1 add_bitcast_fusion.1.slots_ref
  178.2 1.5 add_bitcast_fusion.gates_ref
  179.6 2.6 %shard_map.85 = bf16[8,64,256]{2,1,0:T(8,128)(2,1)S(1)} custom-call(f32[16,64,4]{2,1,0:T(8,128)S(1)} %add_bitcast_fusion.1.slots_ref, f32[16,64,4]{2,1,0:T(8,128)S(1)} %add_bitcast_fusion.gates_ref, bf16[16,8,32,256]{3,2,1,0:T(8,128)(2,1)} %all-to-all-done.2.rows_ref), custom_call_target="tpu_custom_call" | custom-call | flops 268435456 | bytes 3145728 | tf_op jit(solution)/shard_map/pallas_call | solution.py:109
  182.3 0.0 copy-start.2
  182.3 0.8 copy-done.2
  183.1 7.1 %all-to-all-done.3.rows_ref = bf16[16,8,32,256]{3,2,1,0:T(8,128)(2,1)S(1)} async-done(((bf16[16,8,32,256]{3,2,1,0:T(8,128)(2,1)}), bf16[16,8,32,256]{3,2,1,0:T(8,128)(2,1)S(1)}, u32[]{:S(2)}, u32[]{:S(2)}) %all-to-all-start.3) | async-done | bytes 2097184 | tf_op jit(solution)/shard_map/all_to_all | solution.py:209
  190.1 0.0 copy-start.3
  190.1 1.0 copy-done.3
  191.2 1.5 shard_map.87
  192.8 44.2 %all_to_all.25 = bf16[16,64,256]{2,1,0:T(8,128)(2,1)S(1)} all-to-all(bf16[16,64,256]{2,1,0:T(8,128)(2,1)S(1)} %pad_maximum_fusion.1), channel_id=1, replica_groups=mesh['x'=4,'y'=4,'z'=16,'core'=2] {'z'}, dimensions={0} | all-to-all | bytes 1048576 | tf_op jit(solution)/shard_map/all_to_all | solution.py:32
  237.0 0.1 convert_reduce_fusion
  237.0 0.6 add_convert_fusion
  (15 shorter events, 0.2 us)
Async XLA Ops:
  6.5 44.2 %copy-start = (bf16[64,256]{1,0:T(8,128)(2,1)S(1)}, bf16[64,256]{1,0:T(8,128)(2,1)}, u32[]{:S(2)}) copy-start(bf16[64,256]{1,0:T(8,128)(2,1)} %param.8) | copy-start | bytes 98308
  6.5 42.0 %copy-start.5 = (s32[64,4]{0,1:T(4,128)S(1)}, s32[64,4]{0,1:T(4,128)}, u32[]{:S(2)}) copy-start(s32[64,4]{0,1:T(4,128)} %param.12) | copy-start | bytes 3076
  6.5 42.1 %copy-start.6 = (f32[64,4]{0,1:T(4,128)S(1)}, f32[64,4]{0,1:T(4,128)}, u32[]{:S(2)}) copy-start(f32[64,4]{0,1:T(4,128)} %param.13) | copy-start | bytes 3076
  6.5 113.3 %all-gather.5.cloned.1.call-start = ((), (), s32[]{:S(2)}) async-start(), calls=%async_computation.5 | async-start | bytes 6291456 | tf_op jit(solution)/shard_map/all_gather | solution.py:213
  7.3 112.6 %all-gather.7.cloned.1.call-start = ((), (), s32[]{:S(2)}) async-start(), calls=%async_computation.6 | async-start | bytes 6291456 | tf_op jit(solution)/shard_map/all_gather | solution.py:214
  46.6 3.8 %collective-permute-start = (bf16[16,64,256]{2,1,0:T(8,128)(2,1)S(1)}, bf16[16,64,256]{2,1,0:T(8,128)(2,1)S(1)}, u32[]{:S(2)}, u32[]{:S(2)}) collective-permute-start(bf16[16,64,256]{2,1,0:T(8,128)(2,1)S(1)} %bitcast.66), channel_id=1, source_target_pairs={{0,1},{1,0},{2,3},{3,2},{4,5},{5,4},{6,7},{7,6},{8,9},{9,8},{10,11... | collective-permute-start | bytes 1572872 | tf_op jit(solution)/shard_map/ppermute | solution.py:28
  51.3 0.8 copy-start.4
  82.0 2.6 %copy-start.1 = (bf16[1280,256]{1,0:T(8,128)(2,1)}, bf16[1280,256]{1,0:T(8,128)(2,1)S(1)}, u32[]{:S(2)}) copy-start(bf16[1280,256]{1,0:T(8,128)(2,1)S(1)} %all-gather.1) | copy-start | bytes 1966084
  84.5 28.6 %all-to-all-start = ((bf16[16,8,32,256]{3,2,1,0:T(8,128)(2,1)}), bf16[16,8,32,256]{3,2,1,0:T(8,128)(2,1)}, u32[]{:S(2)}, u32[]{:S(2)}) async-start(bf16[16,8,32,256]{3,2,1,0:T(8,128)(2,1)} %shard_map.82), calls=%async_computation | async-start | bytes 4194304 | tf_op jit(solution)/shard_map/all_to_all | solution.py:209
  113.2 26.4 %all-to-all-start.1 = ((bf16[16,8,32,256]{3,2,1,0:T(8,128)(2,1)}), bf16[16,8,32,256]{3,2,1,0:T(8,128)(2,1)}, u32[]{:S(2)}, u32[]{:S(2)}) async-start(bf16[16,8,32,256]{3,2,1,0:T(8,128)(2,1)} %shard_map.84), calls=%async_computation.1 | async-start | bytes 4194304 | tf_op jit(solution)/shard_map/all_to_all | solution.py:209
  139.5 25.5 %all-to-all-start.2 = ((bf16[16,8,32,256]{3,2,1,0:T(8,128)(2,1)}), bf16[16,8,32,256]{3,2,1,0:T(8,128)(2,1)}, u32[]{:S(2)}, u32[]{:S(2)}) async-start(bf16[16,8,32,256]{3,2,1,0:T(8,128)(2,1)} %shard_map.83), calls=%async_computation.2 | async-start | bytes 4194304 | tf_op jit(solution)/shard_map/all_to_all | solution.py:209
  165.0 25.1 %all-to-all-start.3 = ((bf16[16,8,32,256]{3,2,1,0:T(8,128)(2,1)}), bf16[16,8,32,256]{3,2,1,0:T(8,128)(2,1)S(1)}, u32[]{:S(2)}, u32[]{:S(2)}) async-start(bf16[16,8,32,256]{3,2,1,0:T(8,128)(2,1)} %shard_map.86), calls=%async_computation.3 | async-start | bytes 4194304 | tf_op jit(solution)/shard_map/all_to_all | solution.py:209
  182.3 0.8 copy-start.2
  190.1 1.0 copy-start.3
Sparse Core Ops, SparseCore 0:
  9.5 28.5 all-gather.4
  48.7 19.8 all-gather.6

commit v10 on v9

--- a/solution.py
+++ b/solution.py
@@ -28,8 +28,20 @@
     return lax.ppermute(x, "core", [(0, 1), (1, 0)])
 
 
-def swap_chips(x):
-    return lax.all_to_all(x, "z", split_axis=0, concat_axis=0, tiled=True)
+def fold(x, bit):
+    mine = (lax.axis_index("z") >> bit) & 1
+    pairs = x.reshape((x.shape[0] // 2, 2) + x.shape[1:])
+    kept = lax.dynamic_index_in_dim(pairs, mine, 1, keepdims=False)
+    sent = lax.dynamic_index_in_dim(pairs, 1 - mine, 1, keepdims=False)
+    came = lax.ppermute(sent, "z", [(i, i ^ (1 << bit)) for i in range(Z)])
+    return (kept.astype(jnp.float32) + came.astype(jnp.float32)).astype(x.dtype)
+
+
+def join(lower, upper):
+    high = lax.axis_index("z") >= Z // 2
+    kept, sent = jnp.where(high, upper, lower), jnp.where(high, lower, upper)
+    came = lax.ppermute(sent, "z", [(i, i ^ 8) for i in range(Z)])
+    return kept[0].astype(jnp.float32) + came[0].astype(jnp.float32)
 
 
 def gather_kv(keys, values):
@@ -222,12 +234,18 @@
     plane = lax.all_gather(sent, "z", axis=0)
     plane_slots, plane_gates = read_notes(plane[:, BLOCK:])
     slots_t, gates_t = plane_slots.transpose(0, 2, 1), plane_gates.transpose(0, 2, 1)
-    rows = [swap_columns(place_rows(plane, part)) for part in range(PARTS)]
-    outs = [experts(part, w_in, w_down) for part in rows]
-    outs[0], rows[1] = lax.optimization_barrier((outs[0], rows[1]))
-    mixes = [mix_rows(slots_t, gates_t, swap_columns(out), part) for part, out in enumerate(outs)]
-    mix = swap_chips(jnp.concatenate(mixes, axis=0))
-    mixture = jnp.sum(mix.astype(jnp.float32), axis=0)
+    first = swap_columns(place_rows(plane, 0))
+    second, first = lax.optimization_barrier((place_rows(plane, 1), first))
+    second = swap_columns(second)
+    out = experts(first, w_in, w_down)
+    out, second, slots_t, gates_t = lax.optimization_barrier((out, second, slots_t, gates_t))
+    first = swap_columns(out)
+    out, first = lax.optimization_barrier((experts(second, w_in, w_down), first))
+    second = swap_columns(out)
+    lower = fold(fold(mix_rows(slots_t, gates_t, first, 0), 0), 1)
+    lower, second = lax.optimization_barrier((lower, second))
+    upper = fold(fold(mix_rows(slots_t, gates_t, second, 1), 0), 1)
+    mixture = join(fold(lower, 2), fold(upper, 2))
     return (state.astype(jnp.float32) + mixture).astype(jnp.bfloat16)
 
 

time: 245 us -> 252 us (1.029); the launches traced: 244 us -> 249 us
  starting transfers between devices: 29.2 us -> 75.1 us
  blocking collectives: 113 us -> 68.4 us
  waiting for transfers between devices: 47.6 us -> 52.7 us
    ppermute x0 -> x7, starting transfers between devices: none -> 45.9 us  [the longest x6 36.3 us: fold(): came = lax.ppermute(sent, 'z', [(i, i ^ 1 << bit) for i in range(Z)])]
    all_to_all x1 -> x0, blocking collectives: 44.2 us -> none  [swap_chips(): return lax.all_to_all(x, 'z', split_axis=0, concat_axis=0, tiled=True)]
    ppermute x0 -> x7, waiting for transfers between devices: none -> 17.1 us  [the longest x6 12.2 us: fold(): came = lax.ppermute(sent, 'z', [(i, i ^ 1 << bit) for i in range(Z)])]
    all_to_all x4, waiting for transfers between devices: 46 us -> 33.9 us  [swap_columns(): return lax.all_to_all(x, E, split_axis=0, concat_axis=0, tiled=True)]
  transfers between devices with their start and end apart: 7 -> 14, of which waited for: 5 -> 10; matrix products, arithmetic and copies ran while one was open for 4% -> 3% of each run, Pallas kernels for 11% -> 10%
where the time goes in v10:
time: 252 us; the launch traced here: 249 us
  starting transfers between devices  75.1 us (30%)
  blocking collectives  68.4 us (27%)
  waiting for transfers between devices  52.7 us (21%)
  Pallas kernels  27.6 us (11%)
  between operations  13.8 us (5%)
  local copies, waits for them, and re-layouts  5.94 us (2%)
  other arithmetic  4.18 us (2%)
    all_gather x1, blocking collectives, gather_kv(): mine = lax.all_gather(jnp.concatenate([k, v], axis=1), 'z', axis=0)  38.5 us
    ppermute x6, starting transfers between devices, fold(): came = lax.ppermute(sent, 'z', [(i, i ^ 1 << bit) for i in range(Z)])  36.3 us
    all_to_all x4, waiting for transfers between devices, swap_columns(): return lax.all_to_all(x, E, split_axis=0, concat_axis=0, tiled=True)  33.9 us
    all_gather x1, blocking collectives, per_device(): plane = lax.all_gather(sent, 'z', axis=0)  29.8 us
    all_to_all x4, starting transfers between devices, swap_columns(): return lax.all_to_all(x, E, split_axis=0, concat_axis=0, tiled=True)  27.3 us
    pallas_call x2, Pallas kernels, experts(): pl.pallas_call(expert_kernel, grid=(count // group,), in_specs=[spec, pl....  17.3 us
    ppermute x6, waiting for transfers between devices, fold(): came = lax.ppermute(sent, 'z', [(i, i ^ 1 << bit) for i in range(Z)])  12.2 us
    ppermute x1, starting transfers between devices, join(): came = lax.ppermute(sent, 'z', [(i, i ^ 8) for i in range(Z)])  9.57 us
  transfers between devices with their start and end apart: 14, of which 10 were waited for; matrix products, arithmetic and copies ran while one was open for 3% of the time, Pallas kernels for 10%

profile of v10, /device:TPU:6, one launch (start us, length us, event | category | flops | bytes accessed | tf_op | source)
XLA Modules:
  0.0 248.7 jit_solution(5650630059243230061)
XLA Ops:
  6.5 0.0 copy-start
  6.5 0.0 all-gather.5.cloned.1.call-start
  6.5 0.7 all-gather.5.cloned.1.call-update
  7.3 0.0 all-gather.7.cloned.1.call-start
  7.3 0.7 constant_dynamic-slice_fusion.2
  8.1 38.5 %all-gather = bf16[1024,256]{1,0:T(8,128)(2,1)S(1)} all-gather(bf16[64,256]{1,0:T(8,128)(2,1)S(1)} %pad_maximum_fusion.1), channel_id=2, replica_groups=mesh['x'=4,'y'=4,'z'=16,'core'=2] {'z'}, dimensions={0}, use_global_device_ids=true | all-gather | bytes 557056 | tf_op jit(solution)/shard_map/all_gather | solution.py:51
  46.6 1.9 collective-permute-start
  48.5 0.0 all-gather.7.cloned.1.call-update
  48.6 0.0 copy-done.5
  48.6 0.1 reshape.158
  48.7 0.1 convolution_convert_fusion
  48.9 0.1 reshape.159
  48.9 0.0 copy-done.6
  49.0 0.1 reshape.160
  49.1 0.1 reshape.161
  49.2 0.1 reshape.162
  49.3 0.1 broadcast_compare_fusion
  49.4 1.0 collective-permute-done
  50.4 0.3 pad_maximum_fusion
  50.7 0.6 fusion.45
  51.3 0.4 convolution_bitcast_fusion
  51.7 0.4 copy-done.4
  52.1 29.8 %all-gather.1 = bf16[1280,256]{1,0:T(8,128)(2,1)S(1)} all-gather(bf16[80,256]{1,0:T(8,128)(2,1)S(1)} %fusion.13), channel_id=3, replica_groups=mesh['x'=4,'y'=4,'z'=16,'core'=2] {'z'}, dimensions={0}, use_global_device_ids=true | all-gather | bytes 696320 | tf_op jit(solution)/shard_map/all_gather | solution.py:234
  82.0 2.6 %shard_map.83 = bf16[16,8,32,256]{3,2,1,0:T(8,128)(2,1)} custom-call(bf16[16,80,256]{2,1,0:T(8,128)(2,1)S(1)} %bitcast.99), custom_call_target="tpu_custom_call" | custom-call | flops 134217728 | bytes 3145728 | tf_op jit(solution)/shard_map/pallas_call | solution.py:92
  84.5 0.0 copy-done.1
  84.5 7.4 %all-to-all-start = ((bf16[16,8,32,256]{3,2,1,0:T(8,128)(2,1)}), bf16[16,8,32,256]{3,2,1,0:T(8,128)(2,1)}, u32[]{:S(2)}, u32[]{:S(2)}) async-start(bf16[16,8,32,256]{3,2,1,0:T(8,128)(2,1)} %shard_map.83), calls=%async_computation | async-start | bytes 4194304 | tf_op jit(solution)/shard_map/all_to_all | solution.py:221
  92.0 3.5 %shard_map.82 = bf16[16,8,32,256]{3,2,1,0:T(8,128)(2,1)} custom-call(bf16[16,80,256]{2,1,0:T(8,128)(2,1)} %bitcast.100), custom_call_target="tpu_custom_call" | custom-call | flops 134217728 | bytes 3145728 | tf_op jit(solution)/shard_map/pallas_call | solution.py:92
  95.5 17.7 %all-to-all-done.rows_ref = bf16[16,8,32,256]{3,2,1,0:T(8,128)(2,1)} async-done(((bf16[16,8,32,256]{3,2,1,0:T(8,128)(2,1)}), bf16[16,8,32,256]{3,2,1,0:T(8,128)(2,1)}, u32[]{:S(2)}, u32[]{:S(2)}) %all-to-all-start) | async-done | bytes 2097184 | tf_op jit(solution)/shard_map/all_to_all | solution.py:221
  113.2 6.7 %all-to-all-start.1 = ((bf16[16,8,32,256]{3,2,1,0:T(8,128)(2,1)}), bf16[16,8,32,256]{3,2,1,0:T(8,128)(2,1)}, u32[]{:S(2)}, u32[]{:S(2)}) async-start(bf16[16,8,32,256]{3,2,1,0:T(8,128)(2,1)} %shard_map.82), calls=%async_computation.1 | async-start | bytes 4194304 | tf_op jit(solution)/shard_map/all_to_all | solution.py:221
  119.9 0.8 slice_convert_fusion
  120.7 0.1 reshape.180
  120.9 0.2 copy.67
  121.1 0.2 copy.66
  121.4 0.2 copy.70
  121.6 0.2 copy.68
  121.9 1.1 copy.69
  122.9 0.1 add_bitcast_fusion.1.slots_ref
  123.0 1.9 add_bitcast_fusion.gates_ref
  124.9 8.7 %shard_map.84 = bf16[16,8,32,256]{3,2,1,0:T(8,128)(2,1)} custom-call(bf16[16,8,32,256]{3,2,1,0:T(8,128)(2,1)} %all-to-all-done.rows_ref, bf16[2,4096,256]{2,1,0:T(8,128)(2,1)} %all-gather.5.cloned.1.call-done.in_ref, bf16[2,256,4096]{2,1,0:T(8,128)(2,1)} %all-gather.7.cloned.1.call-done.down_ref), custom_call_target="tpu_custom_call" | custom-call | flops 2147483648 | bytes 12582912 | tf_op jit(solution)/shard_map/pallas_call | solution.py:170
  133.6 6.0 %all-to-all-done.1.rows_ref = bf16[16,8,32,256]{3,2,1,0:T(8,128)(2,1)} async-done(((bf16[16,8,32,256]{3,2,1,0:T(8,128)(2,1)}), bf16[16,8,32,256]{3,2,1,0:T(8,128)(2,1)}, u32[]{:S(2)}, u32[]{:S(2)}) %all-to-all-start.1) | async-done | bytes 2097184 | tf_op jit(solution)/shard_map/all_to_all | solution.py:221
  139.5 6.6 %all-to-all-start.2 = ((bf16[16,8,32,256]{3,2,1,0:T(8,128)(2,1)}), bf16[16,8,32,256]{3,2,1,0:T(8,128)(2,1)}, u32[]{:S(2)}, u32[]{:S(2)}) async-start(bf16[16,8,32,256]{3,2,1,0:T(8,128)(2,1)} %shard_map.84), calls=%async_computation.2 | async-start | bytes 4194304 | tf_op jit(solution)/shard_map/all_to_all | solution.py:221
  146.1 8.7 %shard_map.85 = bf16[16,8,32,256]{3,2,1,0:T(8,128)(2,1)} custom-call(bf16[16,8,32,256]{3,2,1,0:T(8,128)(2,1)} %all-to-all-done.1.rows_ref, bf16[2,4096,256]{2,1,0:T(8,128)(2,1)} %all-gather.5.cloned.1.call-done.in_ref, bf16[2,256,4096]{2,1,0:T(8,128)(2,1)} %all-gather.7.cloned.1.call-done.down_ref), custom_call_target="tpu_custom_call" | custom-call | flops 2147483648 | bytes 12582912 | tf_op jit(solution)/shard_map/pallas_call | solution.py:170
  154.8 10.2 %all-to-all-done.2.rows_ref = bf16[16,8,32,256]{3,2,1,0:T(8,128)(2,1)} async-done(((bf16[16,8,32,256]{3,2,1,0:T(8,128)(2,1)}), bf16[16,8,32,256]{3,2,1,0:T(8,128)(2,1)}, u32[]{:S(2)}, u32[]{:S(2)}) %all-to-all-start.2) | async-done | bytes 2097184 | tf_op jit(solution)/shard_map/all_to_all | solution.py:221
  165.0 6.6 %all-to-all-start.3 = ((bf16[16,8,32,256]{3,2,1,0:T(8,128)(2,1)}), bf16[16,8,32,256]{3,2,1,0:T(8,128)(2,1)S(1)}, u32[]{:S(2)}, u32[]{:S(2)}) async-start(bf16[16,8,32,256]{3,2,1,0:T(8,128)(2,1)} %shard_map.85), calls=%async_computation.3 | async-start | bytes 4194304 | tf_op jit(solution)/shard_map/all_to_all | solution.py:221
  171.6 1.0 copy-done.2
  172.6 2.6 %shard_map.86 = bf16[8,64,256]{2,1,0:T(8,128)(2,1)S(1)} custom-call(f32[16,64,4]{2,1,0:T(8,128)S(1)} %add_bitcast_fusion.1.slots_ref, f32[16,64,4]{2,1,0:T(8,128)S(1)} %copy-done.2, bf16[16,8,32,256]{3,2,1,0:T(8,128)(2,1)} %all-to-all-done.2.rows_ref), custom_call_target="tpu_custom_call" | custom-call | flops 268435456 | bytes 3145728 | tf_op jit(solution)/shard_map/pallas_call | solution.py:121
  175.3 4.9 %collective-permute-start.1 = (bf16[4,64,256]{2,1,0:T(8,128)(2,1)S(1)}, bf16[4,64,256]{2,1,0:T(8,128)(2,1)S(1)}, u32[]{:S(2)}, u32[]{:S(2)}) collective-permute-start(bf16[4,64,256]{2,1,0:T(8,128)(2,1)S(1)} %dynamic-slice_bitcast_fusion.1), channel_id=1, source_target_pairs={{0,2},{2,0},{4,6},{6,4},{8,10},{10,8},{12,14},{14,12},{16,18},{18,... | collective-permute-start | bytes 393224 | tf_op jit(solution)/shard_map/ppermute | solution.py:36
  180.2 2.9 %collective-permute-done.1 = bf16[4,64,256]{2,1,0:T(8,128)(2,1)S(1)} collective-permute-done((bf16[4,64,256]{2,1,0:T(8,128)(2,1)S(1)}, bf16[4,64,256]{2,1,0:T(8,128)(2,1)S(1)}, u32[]{:S(2)}, u32[]{:S(2)}) %collective-permute-start.1) | collective-permute-done | bytes 131104 | tf_op jit(solution)/shard_map/ppermute | solution.py:36
  183.2 7.5 %collective-permute-start.2 = (bf16[2,64,256]{2,1,0:T(8,128)(2,1)S(1)}, bf16[2,64,256]{2,1,0:T(8,128)(2,1)S(1)}, u32[]{:S(2)}, u32[]{:S(2)}) collective-permute-start(bf16[2,64,256]{2,1,0:T(8,128)(2,1)S(1)} %dynamic-slice_bitcast_fusion.3), channel_id=1, source_target_pairs={{0,4},{2,6},{4,0},{6,2},{8,12},{10,14},{12,8},{14,10},{16,20},{18,... | collective-permute-start | bytes 196616 | tf_op jit(solution)/shard_map/ppermute | solution.py:36
  190.8 2.2 collective-permute-done.2
  193.0 0.0 all-to-all-done.3.rows_ref
  193.0 1.0 copy-done.3
  194.1 1.5 shard_map.87
  195.6 2.9 %collective-permute-start.3 = (bf16[4,64,256]{2,1,0:T(8,128)(2,1)S(1)}, bf16[4,64,256]{2,1,0:T(8,128)(2,1)S(1)}, u32[]{:S(2)}, u32[]{:S(2)}) collective-permute-start(bf16[4,64,256]{2,1,0:T(8,128)(2,1)S(1)} %dynamic-slice_bitcast_fusion), channel_id=1, source_target_pairs={{0,2},{2,0},{4,6},{6,4},{8,10},{10,8},{12,14},{14,12},{16,18},{18,... | collective-permute-start | bytes 393224 | tf_op jit(solution)/shard_map/ppermute | solution.py:36
  198.5 4.0 %collective-permute-done.3 = bf16[4,64,256]{2,1,0:T(8,128)(2,1)S(1)} collective-permute-done((bf16[4,64,256]{2,1,0:T(8,128)(2,1)S(1)}, bf16[4,64,256]{2,1,0:T(8,128)(2,1)S(1)}, u32[]{:S(2)}, u32[]{:S(2)}) %collective-permute-start.3) | collective-permute-done | bytes 131104 | tf_op jit(solution)/shard_map/ppermute | solution.py:36
  202.6 11.2 %collective-permute-start.4 = (bf16[2,64,256]{2,1,0:T(8,128)(2,1)S(1)}, bf16[2,64,256]{2,1,0:T(8,128)(2,1)S(1)}, u32[]{:S(2)}, u32[]{:S(2)}) collective-permute-start(bf16[2,64,256]{2,1,0:T(8,128)(2,1)S(1)} %dynamic-slice_bitcast_fusion.2), channel_id=1, source_target_pairs={{0,4},{2,6},{4,0},{6,2},{8,12},{10,14},{12,8},{14,10},{16,20},{18,... | collective-permute-start | bytes 196616 | tf_op jit(solution)/shard_map/ppermute | solution.py:36
  213.8 3.1 %collective-permute-start.6 = (bf16[1,64,256]{2,1,0:T(8,128)(2,1)S(1)}, bf16[1,64,256]{2,1,0:T(8,128)(2,1)S(1)}, u32[]{:S(2)}, u32[]{:S(2)}) collective-permute-start(bf16[1,64,256]{2,1,0:T(8,128)(2,1)S(1)} %constant_dynamic-slice_fusion.1), channel_id=1, source_target_pairs={{0,8},{2,10},{4,12},{6,14},{8,0},{10,2},{12,4},{14,6},{16,24},{18,... | collective-permute-start | bytes 98312 | tf_op jit(solution)/shard_map/ppermute | solution.py:36
  216.9 0.0 collective-permute-done.4
  216.9 6.7 %collective-permute-start.5 = (bf16[1,64,256]{2,1,0:T(8,128)(2,1)S(1)}, bf16[1,64,256]{2,1,0:T(8,128)(2,1)S(1)}, u32[]{:S(2)}, u32[]{:S(2)}) collective-permute-start(bf16[1,64,256]{2,1,0:T(8,128)(2,1)S(1)} %constant_dynamic-slice_fusion), channel_id=1, source_target_pairs={{0,8},{2,10},{4,12},{6,14},{8,0},{10,2},{12,4},{14,6},{16,24},{18,... | collective-permute-start | bytes 98312 | tf_op jit(solution)/shard_map/ppermute | solution.py:36
  223.7 0.3 collective-permute-done.6
  223.9 2.7 %collective-permute-done.5 = bf16[1,64,256]{2,1,0:T(8,128)(2,1)S(1)} collective-permute-done((bf16[1,64,256]{2,1,0:T(8,128)(2,1)S(1)}, bf16[1,64,256]{2,1,0:T(8,128)(2,1)S(1)}, u32[]{:S(2)}, u32[]{:S(2)}) %collective-permute-start.5) | collective-permute-done | bytes 32800 | tf_op jit(solution)/shard_map/ppermute | solution.py:36
  226.7 9.6 %collective-permute-start.7 = (bf16[1,64,256]{2,1,0:T(8,128)(2,1)S(1)}, bf16[1,64,256]{2,1,0:T(8,128)(2,1)S(1)}, u32[]{:S(2)}, u32[]{:S(2)}) collective-permute-start(bf16[1,64,256]{2,1,0:T(8,128)(2,1)S(1)} %broadcast_select_fusion), channel_id=1, source_target_pairs={{0,16},{2,18},{4,20},{6,22},{8,24},{10,26},{12,28},{14,30},{16,0},... | collective-permute-start | bytes 98312 | tf_op jit(solution)/shard_map/ppermute | solution.py:43
  236.3 4.9 %collective-permute-done.7 = bf16[1,64,256]{2,1,0:T(8,128)(2,1)S(1)} collective-permute-done((bf16[1,64,256]{2,1,0:T(8,128)(2,1)S(1)}, bf16[1,64,256]{2,1,0:T(8,128)(2,1)S(1)}, u32[]{:S(2)}, u32[]{:S(2)}) %collective-permute-start.7) | collective-permute-done | bytes 32800 | tf_op jit(solution)/shard_map/ppermute | solution.py:43
  241.2 0.6 fusion.12
  (34 shorter events, 0.4 us)
Async XLA Ops:
  6.5 44.2 %copy-start = (bf16[64,256]{1,0:T(8,128)(2,1)S(1)}, bf16[64,256]{1,0:T(8,128)(2,1)}, u32[]{:S(2)}) copy-start(bf16[64,256]{1,0:T(8,128)(2,1)} %param.8) | copy-start | bytes 98308
  6.5 42.0 %copy-start.5 = (s32[64,4]{0,1:T(4,128)S(1)}, s32[64,4]{0,1:T(4,128)}, u32[]{:S(2)}) copy-start(s32[64,4]{0,1:T(4,128)} %param.12) | copy-start | bytes 3076
  6.5 42.4 %copy-start.6 = (f32[64,4]{0,1:T(4,128)S(1)}, f32[64,4]{0,1:T(4,128)}, u32[]{:S(2)}) copy-start(f32[64,4]{0,1:T(4,128)} %param.13) | copy-start | bytes 3076
  6.5 118.4 %all-gather.5.cloned.1.call-start = ((), (), s32[]{:S(2)}) async-start(), calls=%async_computation.4 | async-start | bytes 6291456 | tf_op jit(solution)/shard_map/all_gather | solution.py:225
  7.3 117.7 %all-gather.7.cloned.1.call-start = ((), (), s32[]{:S(2)}) async-start(), calls=%async_computation.5 | async-start | bytes 6291456 | tf_op jit(solution)/shard_map/all_gather | solution.py:226
  46.6 3.8 %collective-permute-start = (bf16[16,64,256]{2,1,0:T(8,128)(2,1)S(1)}, bf16[16,64,256]{2,1,0:T(8,128)(2,1)S(1)}, u32[]{:S(2)}, u32[]{:S(2)}) collective-permute-start(bf16[16,64,256]{2,1,0:T(8,128)(2,1)S(1)} %bitcast.106), channel_id=1, source_target_pairs={{0,1},{1,0},{2,3},{3,2},{4,5},{5,4},{6,7},{7,6},{8,9},{9,8},{10,11... | collective-permute-start | bytes 1572872 | tf_op jit(solution)/shard_map/ppermute | solution.py:28
  51.3 0.8 copy-start.4
  82.0 2.6 %copy-start.1 = (bf16[1280,256]{1,0:T(8,128)(2,1)}, bf16[1280,256]{1,0:T(8,128)(2,1)S(1)}, u32[]{:S(2)}) copy-start(bf16[1280,256]{1,0:T(8,128)(2,1)S(1)} %all-gather.1) | copy-start | bytes 1966084
  84.5 28.6 %all-to-all-start = ((bf16[16,8,32,256]{3,2,1,0:T(8,128)(2,1)}), bf16[16,8,32,256]{3,2,1,0:T(8,128)(2,1)}, u32[]{:S(2)}, u32[]{:S(2)}) async-start(bf16[16,8,32,256]{3,2,1,0:T(8,128)(2,1)} %shard_map.83), calls=%async_computation | async-start | bytes 4194304 | tf_op jit(solution)/shard_map/all_to_all | solution.py:221
  113.2 26.4 %all-to-all-start.1 = ((bf16[16,8,32,256]{3,2,1,0:T(8,128)(2,1)}), bf16[16,8,32,256]{3,2,1,0:T(8,128)(2,1)}, u32[]{:S(2)}, u32[]{:S(2)}) async-start(bf16[16,8,32,256]{3,2,1,0:T(8,128)(2,1)} %shard_map.82), calls=%async_computation.1 | async-start | bytes 4194304 | tf_op jit(solution)/shard_map/all_to_all | solution.py:221
  139.5 25.5 %all-to-all-start.2 = ((bf16[16,8,32,256]{3,2,1,0:T(8,128)(2,1)}), bf16[16,8,32,256]{3,2,1,0:T(8,128)(2,1)}, u32[]{:S(2)}, u32[]{:S(2)}) async-start(bf16[16,8,32,256]{3,2,1,0:T(8,128)(2,1)} %shard_map.84), calls=%async_computation.2 | async-start | bytes 4194304 | tf_op jit(solution)/shard_map/all_to_all | solution.py:221
  165.0 28.0 %all-to-all-start.3 = ((bf16[16,8,32,256]{3,2,1,0:T(8,128)(2,1)}), bf16[16,8,32,256]{3,2,1,0:T(8,128)(2,1)S(1)}, u32[]{:S(2)}, u32[]{:S(2)}) async-start(bf16[16,8,32,256]{3,2,1,0:T(8,128)(2,1)} %shard_map.85), calls=%async_computation.3 | async-start | bytes 4194304 | tf_op jit(solution)/shard_map/all_to_all | solution.py:221
  171.6 1.0 copy-start.2
  175.3 7.9 %collective-permute-start.1 = (bf16[4,64,256]{2,1,0:T(8,128)(2,1)S(1)}, bf16[4,64,256]{2,1,0:T(8,128)(2,1)S(1)}, u32[]{:S(2)}, u32[]{:S(2)}) collective-permute-start(bf16[4,64,256]{2,1,0:T(8,128)(2,1)S(1)} %dynamic-slice_bitcast_fusion.1), channel_id=1, source_target_pairs={{0,2},{2,0},{4,6},{6,4},{8,10},{10,8},{12,14},{14,12},{16,18},{18,... | collective-permute-start | bytes 393224 | tf_op jit(solution)/shard_map/ppermute | solution.py:36
  183.2 9.8 %collective-permute-start.2 = (bf16[2,64,256]{2,1,0:T(8,128)(2,1)S(1)}, bf16[2,64,256]{2,1,0:T(8,128)(2,1)S(1)}, u32[]{:S(2)}, u32[]{:S(2)}) collective-permute-start(bf16[2,64,256]{2,1,0:T(8,128)(2,1)S(1)} %dynamic-slice_bitcast_fusion.3), channel_id=1, source_target_pairs={{0,4},{2,6},{4,0},{6,2},{8,12},{10,14},{12,8},{14,10},{16,20},{18,... | collective-permute-start | bytes 196616 | tf_op jit(solution)/shard_map/ppermute | solution.py:36
  193.0 1.0 copy-start.3
  195.6 6.9 %collective-permute-start.3 = (bf16[4,64,256]{2,1,0:T(8,128)(2,1)S(1)}, bf16[4,64,256]{2,1,0:T(8,128)(2,1)S(1)}, u32[]{:S(2)}, u32[]{:S(2)}) collective-permute-start(bf16[4,64,256]{2,1,0:T(8,128)(2,1)S(1)} %dynamic-slice_bitcast_fusion), channel_id=1, source_target_pairs={{0,2},{2,0},{4,6},{6,4},{8,10},{10,8},{12,14},{14,12},{16,18},{18,... | collective-permute-start | bytes 393224 | tf_op jit(solution)/shard_map/ppermute | solution.py:36
  202.6 14.3 %collective-permute-start.4 = (bf16[2,64,256]{2,1,0:T(8,128)(2,1)S(1)}, bf16[2,64,256]{2,1,0:T(8,128)(2,1)S(1)}, u32[]{:S(2)}, u32[]{:S(2)}) collective-permute-start(bf16[2,64,256]{2,1,0:T(8,128)(2,1)S(1)} %dynamic-slice_bitcast_fusion.2), channel_id=1, source_target_pairs={{0,4},{2,6},{4,0},{6,2},{8,12},{10,14},{12,8},{14,10},{16,20},{18,... | collective-permute-start | bytes 196616 | tf_op jit(solution)/shard_map/ppermute | solution.py:36
  213.8 10.1 %collective-permute-start.6 = (bf16[1,64,256]{2,1,0:T(8,128)(2,1)S(1)}, bf16[1,64,256]{2,1,0:T(8,128)(2,1)S(1)}, u32[]{:S(2)}, u32[]{:S(2)}) collective-permute-start(bf16[1,64,256]{2,1,0:T(8,128)(2,1)S(1)} %constant_dynamic-slice_fusion.1), channel_id=1, source_target_pairs={{0,8},{2,10},{4,12},{6,14},{8,0},{10,2},{12,4},{14,6},{16,24},{18,... | collective-permute-start | bytes 98312 | tf_op jit(solution)/shard_map/ppermute | solution.py:36
  216.9 9.7 %collective-permute-start.5 = (bf16[1,64,256]{2,1,0:T(8,128)(2,1)S(1)}, bf16[1,64,256]{2,1,0:T(8,128)(2,1)S(1)}, u32[]{:S(2)}, u32[]{:S(2)}) collective-permute-start(bf16[1,64,256]{2,1,0:T(8,128)(2,1)S(1)} %constant_dynamic-slice_fusion), channel_id=1, source_target_pairs={{0,8},{2,10},{4,12},{6,14},{8,0},{10,2},{12,4},{14,6},{16,24},{18,... | collective-permute-start | bytes 98312 | tf_op jit(solution)/shard_map/ppermute | solution.py:36
  226.7 14.5 %collective-permute-start.7 = (bf16[1,64,256]{2,1,0:T(8,128)(2,1)S(1)}, bf16[1,64,256]{2,1,0:T(8,128)(2,1)S(1)}, u32[]{:S(2)}, u32[]{:S(2)}) collective-permute-start(bf16[1,64,256]{2,1,0:T(8,128)(2,1)S(1)} %broadcast_select_fusion), channel_id=1, source_target_pairs={{0,16},{2,18},{4,20},{6,22},{8,24},{10,26},{12,28},{14,30},{16,0},... | collective-permute-start | bytes 98312 | tf_op jit(solution)/shard_map/ppermute | solution.py:43
Sparse Core Ops, SparseCore 0:
  9.5 28.5 all-gather.4
  48.7 19.8 all-gather.6

commit v11 on v9

--- a/solution.py
+++ b/solution.py
@@ -28,8 +28,12 @@
     return lax.ppermute(x, "core", [(0, 1), (1, 0)])
 
 
-def swap_chips(x):
-    return lax.all_to_all(x, "z", split_axis=0, concat_axis=0, tiled=True)
+def sum_chips(x):
+    up = [2 * z for z in range(Z)]
+    down = [2 * z + 1 for z in reversed(range(Z))]
+    x = jnp.where(lax.axis_index("core") == 0, x, x[::-1])
+    came = lax.all_to_all(x, T, split_axis=0, concat_axis=0, axis_index_groups=[up, down], tiled=True)
+    return jnp.sum(came.astype(jnp.float32), axis=0)
 
 
 def gather_kv(keys, values):
@@ -226,8 +230,7 @@
     outs = [experts(part, w_in, w_down) for part in rows]
     outs[0], rows[1] = lax.optimization_barrier((outs[0], rows[1]))
     mixes = [mix_rows(slots_t, gates_t, swap_columns(out), part) for part, out in enumerate(outs)]
-    mix = swap_chips(jnp.concatenate(mixes, axis=0))
-    mixture = jnp.sum(mix.astype(jnp.float32), axis=0)
+    mixture = sum_chips(jnp.concatenate(mixes, axis=0))
     return (state.astype(jnp.float32) + mixture).astype(jnp.bfloat16)
 
 

time: 245 us -> 244 us (level)
  no operation moved by 1% of the time
where the time goes in v11:
time: 244 us; the launch traced here: 243 us
  blocking collectives  111 us (45%)
  waiting for transfers between devices  47.6 us (20%)
  starting transfers between devices  29.2 us (12%)
  Pallas kernels  27.6 us (11%)
  between operations  13.6 us (6%)
  local copies, waits for them, and re-layouts  8.03 us (3%)
  other arithmetic  4.81 us (2%)
    all_to_all x4, waiting for transfers between devices, swap_columns(): return lax.all_to_all(x, E, split_axis=0, concat_axis=0, tiled=True)  46 us
    all_to_all x1, blocking collectives, sum_chips(): lax.all_to_all(x, T, split_axis=0, concat_axis=0, axis_index_groups=[up,...  42.5 us
    all_gather x1, blocking collectives, gather_kv(): mine = lax.all_gather(jnp.concatenate([k, v], axis=1), 'z', axis=0)  38.5 us
    all_gather x1, blocking collectives, per_device(): plane = lax.all_gather(sent, 'z', axis=0)  29.8 us
    all_to_all x4, starting transfers between devices, swap_columns(): return lax.all_to_all(x, E, split_axis=0, concat_axis=0, tiled=True)  27.3 us
    pallas_call x2, Pallas kernels, experts(): pl.pallas_call(expert_kernel, grid=(count // group,), in_specs=[spec, pl....  17.4 us
    unnamed x19, local copies, waits for them, and re-layouts  6.69 us
    pallas_call x2, Pallas kernels, place_rows(): pl.pallas_call(place_kernel, grid=(count // step,), in_specs=[pl.BlockSpe...  6.07 us
  transfers between devices with their start and end apart: 7, of which 5 were waited for; matrix products, arithmetic and copies ran while one was open for 4% of the time, Pallas kernels for 11%

profile of v11, /device:TPU:6, one launch (start us, length us, event | category | flops | bytes accessed | tf_op | source)
XLA Modules:
  0.0 242.9 jit_solution(9269457524255574412)
XLA Ops:
  6.5 0.0 copy-start
  6.5 0.0 copy-start.5
  6.5 0.0 copy-start.6
  6.5 0.0 all-gather.5.cloned.1.call-start
  6.5 0.7 all-gather.5.cloned.1.call-update
  7.3 0.0 all-gather.7.cloned.1.call-start
  7.3 0.7 constant_dynamic-slice_fusion
  8.1 38.5 %all-gather = bf16[1024,256]{1,0:T(8,128)(2,1)S(1)} all-gather(bf16[64,256]{1,0:T(8,128)(2,1)S(1)} %pad_maximum_fusion.2), channel_id=2, replica_groups=mesh['x'=4,'y'=4,'z'=16,'core'=2] {'z'}, dimensions={0}, use_global_device_ids=true | all-gather | bytes 557056 | tf_op jit(solution)/shard_map/all_gather | solution.py:43
  46.6 1.9 collective-permute-start
  48.5 0.0 all-gather.7.cloned.1.call-update
  48.6 0.0 copy-done.5
  48.6 0.0 copy-done.6
  48.7 0.1 reshape.123
  48.8 0.1 reshape.124
  48.8 0.1 reshape.125
  48.9 0.1 convolution_convert_fusion
  49.1 0.1 reshape.122
  49.2 0.1 reshape.121
  49.3 0.1 broadcast_compare_fusion
  49.5 0.9 collective-permute-done
  50.4 0.3 pad_maximum_fusion
  50.7 0.0 copy-done
  50.7 0.6 fusion.40
  51.3 0.0 copy-start.4
  51.3 0.4 convolution_bitcast_fusion
  51.7 0.4 copy-done.4
  52.1 29.8 %all-gather.1 = bf16[1280,256]{1,0:T(8,128)(2,1)S(1)} all-gather(bf16[80,256]{1,0:T(8,128)(2,1)S(1)} %fusion.8), channel_id=3, replica_groups=mesh['x'=4,'y'=4,'z'=16,'core'=2] {'z'}, dimensions={0}, use_global_device_ids=true | all-gather | bytes 696320 | tf_op jit(solution)/shard_map/all_gather | solution.py:226
  82.0 0.0 copy-start.1
  82.0 2.6 %shard_map.82 = bf16[16,8,32,256]{3,2,1,0:T(8,128)(2,1)} custom-call(bf16[16,80,256]{2,1,0:T(8,128)(2,1)S(1)} %bitcast.63), custom_call_target="tpu_custom_call" | custom-call | flops 134217728 | bytes 3145728 | tf_op jit(solution)/shard_map/pallas_call | solution.py:84
  84.5 0.0 copy-done.1
  84.5 7.4 %all-to-all-start = ((bf16[16,8,32,256]{3,2,1,0:T(8,128)(2,1)}), bf16[16,8,32,256]{3,2,1,0:T(8,128)(2,1)}, u32[]{:S(2)}, u32[]{:S(2)}) async-start(bf16[16,8,32,256]{3,2,1,0:T(8,128)(2,1)} %shard_map.82), calls=%async_computation | async-start | bytes 4194304 | tf_op jit(solution)/shard_map/all_to_all | solution.py:213
  92.0 3.5 %shard_map.84 = bf16[16,8,32,256]{3,2,1,0:T(8,128)(2,1)} custom-call(bf16[16,80,256]{2,1,0:T(8,128)(2,1)} %bitcast.64), custom_call_target="tpu_custom_call" | custom-call | flops 134217728 | bytes 3145728 | tf_op jit(solution)/shard_map/pallas_call | solution.py:84
  95.5 17.7 %all-to-all-done.rows_ref = bf16[16,8,32,256]{3,2,1,0:T(8,128)(2,1)} async-done(((bf16[16,8,32,256]{3,2,1,0:T(8,128)(2,1)}), bf16[16,8,32,256]{3,2,1,0:T(8,128)(2,1)}, u32[]{:S(2)}, u32[]{:S(2)}) %all-to-all-start) | async-done | bytes 2097184 | tf_op jit(solution)/shard_map/all_to_all | solution.py:213
  113.2 6.7 %all-to-all-start.1 = ((bf16[16,8,32,256]{3,2,1,0:T(8,128)(2,1)}), bf16[16,8,32,256]{3,2,1,0:T(8,128)(2,1)}, u32[]{:S(2)}, u32[]{:S(2)}) async-start(bf16[16,8,32,256]{3,2,1,0:T(8,128)(2,1)} %shard_map.84), calls=%async_computation.1 | async-start | bytes 4194304 | tf_op jit(solution)/shard_map/all_to_all | solution.py:213
  119.8 0.0 all-gather.5.cloned.1.call-done.in_ref
  119.9 0.0 all-gather.7.cloned.1.call-done.down_ref
  119.9 8.7 %shard_map.83 = bf16[16,8,32,256]{3,2,1,0:T(8,128)(2,1)} custom-call(bf16[16,8,32,256]{3,2,1,0:T(8,128)(2,1)} %all-to-all-done.rows_ref, bf16[2,4096,256]{2,1,0:T(8,128)(2,1)} %all-gather.5.cloned.1.call-done.in_ref, bf16[2,256,4096]{2,1,0:T(8,128)(2,1)} %all-gather.7.cloned.1.call-done.down_ref), custom_call_target="tpu_custom_call" | custom-call | flops 2147483648 | bytes 12582912 | tf_op jit(solution)/shard_map/pallas_call | solution.py:162
  128.6 11.0 %all-to-all-done.1.rows_ref = bf16[16,8,32,256]{3,2,1,0:T(8,128)(2,1)} async-done(((bf16[16,8,32,256]{3,2,1,0:T(8,128)(2,1)}), bf16[16,8,32,256]{3,2,1,0:T(8,128)(2,1)}, u32[]{:S(2)}, u32[]{:S(2)}) %all-to-all-start.1) | async-done | bytes 2097184 | tf_op jit(solution)/shard_map/all_to_all | solution.py:213
  139.5 6.6 %all-to-all-start.2 = ((bf16[16,8,32,256]{3,2,1,0:T(8,128)(2,1)}), bf16[16,8,32,256]{3,2,1,0:T(8,128)(2,1)}, u32[]{:S(2)}, u32[]{:S(2)}) async-start(bf16[16,8,32,256]{3,2,1,0:T(8,128)(2,1)} %shard_map.83), calls=%async_computation.2 | async-start | bytes 4194304 | tf_op jit(solution)/shard_map/all_to_all | solution.py:213
  146.1 8.7 %shard_map.86 = bf16[16,8,32,256]{3,2,1,0:T(8,128)(2,1)} custom-call(bf16[16,8,32,256]{3,2,1,0:T(8,128)(2,1)} %all-to-all-done.1.rows_ref, bf16[2,4096,256]{2,1,0:T(8,128)(2,1)} %all-gather.5.cloned.1.call-done.in_ref, bf16[2,256,4096]{2,1,0:T(8,128)(2,1)} %all-gather.7.cloned.1.call-done.down_ref), custom_call_target="tpu_custom_call" | custom-call | flops 2147483648 | bytes 12582912 | tf_op jit(solution)/shard_map/pallas_call | solution.py:162
  154.8 10.2 %all-to-all-done.2.rows_ref = bf16[16,8,32,256]{3,2,1,0:T(8,128)(2,1)} async-done(((bf16[16,8,32,256]{3,2,1,0:T(8,128)(2,1)}), bf16[16,8,32,256]{3,2,1,0:T(8,128)(2,1)}, u32[]{:S(2)}, u32[]{:S(2)}) %all-to-all-start.2) | async-done | bytes 2097184 | tf_op jit(solution)/shard_map/all_to_all | solution.py:213
  165.0 6.6 %all-to-all-start.3 = ((bf16[16,8,32,256]{3,2,1,0:T(8,128)(2,1)}), bf16[16,8,32,256]{3,2,1,0:T(8,128)(2,1)S(1)}, u32[]{:S(2)}, u32[]{:S(2)}) async-start(bf16[16,8,32,256]{3,2,1,0:T(8,128)(2,1)} %shard_map.86), calls=%async_computation.3 | async-start | bytes 4194304 | tf_op jit(solution)/shard_map/all_to_all | solution.py:213
  171.6 0.8 slice_convert_fusion
  172.4 0.1 reshape.135
  172.6 1.0 copy.52
  173.6 1.1 copy.53
  174.7 1.0 copy.54
  175.8 0.2 copy.50
  176.0 1.1 copy.51
  177.1 1.1 add_bitcast_fusion.1.slots_ref
  178.2 1.5 add_bitcast_fusion.gates_ref
  179.6 2.6 %shard_map.85 = bf16[8,64,256]{2,1,0:T(8,128)(2,1)S(1)} custom-call(f32[16,64,4]{2,1,0:T(8,128)S(1)} %add_bitcast_fusion.1.slots_ref, f32[16,64,4]{2,1,0:T(8,128)S(1)} %add_bitcast_fusion.gates_ref, bf16[16,8,32,256]{3,2,1,0:T(8,128)(2,1)} %all-to-all-done.2.rows_ref), custom_call_target="tpu_custom_call" | custom-call | flops 268435456 | bytes 3145728 | tf_op jit(solution)/shard_map/pallas_call | solution.py:113
  182.3 0.0 copy-start.2
  182.3 0.8 copy-done.2
  183.1 7.1 %all-to-all-done.3.rows_ref = bf16[16,8,32,256]{3,2,1,0:T(8,128)(2,1)S(1)} async-done(((bf16[16,8,32,256]{3,2,1,0:T(8,128)(2,1)}), bf16[16,8,32,256]{3,2,1,0:T(8,128)(2,1)S(1)}, u32[]{:S(2)}, u32[]{:S(2)}) %all-to-all-start.3) | async-done | bytes 2097184 | tf_op jit(solution)/shard_map/all_to_all | solution.py:213
  190.1 0.0 copy-start.3
  190.1 1.0 copy-done.3
  191.2 1.5 shard_map.87
  192.8 0.1 reverse_select_fusion
  192.9 42.5 %all_to_all.25 = bf16[16,64,256]{2,1,0:T(8,128)(2,1)S(1)} all-to-all(bf16[16,64,256]{2,1,0:T(8,128)(2,1)S(1)} %reverse_select_fusion), channel_id=1, replica_groups={{0,2,4,6,8,10,12,14,16,18,20,22,24,26,28,30},{31,29,27,25,23,21,19,17,1..., dimensions={0} | all-to-all | bytes 1048576 | tf_op jit(solution)/shard_map/all_to_all | solution.py:35
  235.4 0.1 convert_reduce_fusion
  235.5 0.6 add_convert_fusion
  (15 shorter events, 0.2 us)
Async XLA Ops:
  6.5 44.2 %copy-start = (bf16[64,256]{1,0:T(8,128)(2,1)S(1)}, bf16[64,256]{1,0:T(8,128)(2,1)}, u32[]{:S(2)}) copy-start(bf16[64,256]{1,0:T(8,128)(2,1)} %param.8) | copy-start | bytes 98308
  6.5 42.0 %copy-start.5 = (s32[64,4]{0,1:T(4,128)S(1)}, s32[64,4]{0,1:T(4,128)}, u32[]{:S(2)}) copy-start(s32[64,4]{0,1:T(4,128)} %param.12) | copy-start | bytes 3076
  6.5 42.1 %copy-start.6 = (f32[64,4]{0,1:T(4,128)S(1)}, f32[64,4]{0,1:T(4,128)}, u32[]{:S(2)}) copy-start(f32[64,4]{0,1:T(4,128)} %param.13) | copy-start | bytes 3076
  6.5 113.3 %all-gather.5.cloned.1.call-start = ((), (), s32[]{:S(2)}) async-start(), calls=%async_computation.5 | async-start | bytes 6291456 | tf_op jit(solution)/shard_map/all_gather | solution.py:217
  7.3 112.6 %all-gather.7.cloned.1.call-start = ((), (), s32[]{:S(2)}) async-start(), calls=%async_computation.6 | async-start | bytes 6291456 | tf_op jit(solution)/shard_map/all_gather | solution.py:218
  46.6 3.8 %collective-permute-start = (bf16[16,64,256]{2,1,0:T(8,128)(2,1)S(1)}, bf16[16,64,256]{2,1,0:T(8,128)(2,1)S(1)}, u32[]{:S(2)}, u32[]{:S(2)}) collective-permute-start(bf16[16,64,256]{2,1,0:T(8,128)(2,1)S(1)} %bitcast.66), channel_id=1, source_target_pairs={{0,1},{1,0},{2,3},{3,2},{4,5},{5,4},{6,7},{7,6},{8,9},{9,8},{10,11... | collective-permute-start | bytes 1572872 | tf_op jit(solution)/shard_map/ppermute | solution.py:28
  51.3 0.8 copy-start.4
  82.0 2.6 %copy-start.1 = (bf16[1280,256]{1,0:T(8,128)(2,1)}, bf16[1280,256]{1,0:T(8,128)(2,1)S(1)}, u32[]{:S(2)}) copy-start(bf16[1280,256]{1,0:T(8,128)(2,1)S(1)} %all-gather.1) | copy-start | bytes 1966084
  84.5 28.6 %all-to-all-start = ((bf16[16,8,32,256]{3,2,1,0:T(8,128)(2,1)}), bf16[16,8,32,256]{3,2,1,0:T(8,128)(2,1)}, u32[]{:S(2)}, u32[]{:S(2)}) async-start(bf16[16,8,32,256]{3,2,1,0:T(8,128)(2,1)} %shard_map.82), calls=%async_computation | async-start | bytes 4194304 | tf_op jit(solution)/shard_map/all_to_all | solution.py:213
  113.2 26.4 %all-to-all-start.1 = ((bf16[16,8,32,256]{3,2,1,0:T(8,128)(2,1)}), bf16[16,8,32,256]{3,2,1,0:T(8,128)(2,1)}, u32[]{:S(2)}, u32[]{:S(2)}) async-start(bf16[16,8,32,256]{3,2,1,0:T(8,128)(2,1)} %shard_map.84), calls=%async_computation.1 | async-start | bytes 4194304 | tf_op jit(solution)/shard_map/all_to_all | solution.py:213
  139.5 25.5 %all-to-all-start.2 = ((bf16[16,8,32,256]{3,2,1,0:T(8,128)(2,1)}), bf16[16,8,32,256]{3,2,1,0:T(8,128)(2,1)}, u32[]{:S(2)}, u32[]{:S(2)}) async-start(bf16[16,8,32,256]{3,2,1,0:T(8,128)(2,1)} %shard_map.83), calls=%async_computation.2 | async-start | bytes 4194304 | tf_op jit(solution)/shard_map/all_to_all | solution.py:213
  165.0 25.1 %all-to-all-start.3 = ((bf16[16,8,32,256]{3,2,1,0:T(8,128)(2,1)}), bf16[16,8,32,256]{3,2,1,0:T(8,128)(2,1)S(1)}, u32[]{:S(2)}, u32[]{:S(2)}) async-start(bf16[16,8,32,256]{3,2,1,0:T(8,128)(2,1)} %shard_map.86), calls=%async_computation.3 | async-start | bytes 4194304 | tf_op jit(solution)/shard_map/all_to_all | solution.py:213
  182.3 0.8 copy-start.2
  190.1 1.0 copy-start.3
Sparse Core Ops, SparseCore 0:
  9.5 28.5 all-gather.4
  48.7 19.8 all-gather.6

commit v12 on v9

--- a/solution.py
+++ b/solution.py
@@ -116,9 +116,9 @@
         ],
         out_specs=pl.BlockSpec((step, BLOCK, WIDTH), lambda i: (i, 0, 0)),
         out_shape=jax.ShapeDtypeStruct((count, BLOCK, WIDTH), jnp.bfloat16),
-        compiler_params=pltpu.CompilerParams(vmem_limit_bytes=16 * MIB),
+        compiler_params=pltpu.CompilerParams(vmem_limit_bytes=32 * MIB),
         cost_estimate=pl.CostEstimate(flops=4 * Z * 512 * 64 * 128, bytes_accessed=3 * MIB, transcendentals=0),
-    )(slots, gates, rows)
+    )(slots, gates, in_hbm(rows))
 
 
 def expert_kernel(rows_ref, in_ref, down_ref, out_ref, raw, normed):

time: 245 us -> 245 us (level)
  waiting for transfers between devices: 47.6 us -> 54.2 us
  local copies, waits for them, and re-layouts: 8.03 us -> 2.97 us
    all_to_all x4, waiting for transfers between devices: 46 us -> 52.5 us  [swap_columns(): return lax.all_to_all(x, E, split_axis=0, concat_axis=0, tiled=True)]
    unnamed x19 -> x15, local copies, waits for them, and re-layouts: 6.69 us -> 1.62 us
  transfers between devices with their start and end apart: 7 -> 7, of which waited for: 5 -> 5; matrix products, arithmetic and copies ran while one was open for 4% -> 2% of each run, Pallas kernels for 11% -> 11%
where the time goes in v12:
time: 245 us
  blocking collectives  113 us (46%)
  waiting for transfers between devices  54.2 us (22%)
  starting transfers between devices  29.2 us (12%)
  Pallas kernels  28.6 us (12%)
  between operations  13.7 us (6%)
  local copies, waits for them, and re-layouts  2.97 us (1%)
    all_to_all x4, waiting for transfers between devices, swap_columns(): return lax.all_to_all(x, E, split_axis=0, concat_axis=0, tiled=True)  52.5 us
    all_to_all x1, blocking collectives, swap_chips(): return lax.all_to_all(x, 'z', split_axis=0, concat_axis=0, tiled=True)  44.3 us
    all_gather x1, blocking collectives, gather_kv(): mine = lax.all_gather(jnp.concatenate([k, v], axis=1), 'z', axis=0)  38.5 us
    all_gather x1, blocking collectives, per_device(): plane = lax.all_gather(sent, 'z', axis=0)  29.8 us
    all_to_all x4, starting transfers between devices, swap_columns(): return lax.all_to_all(x, E, split_axis=0, concat_axis=0, tiled=True)  27.3 us
    pallas_call x2, Pallas kernels, experts(): pl.pallas_call(expert_kernel, grid=(count // group,), in_specs=[spec, pl....  17.3 us
    pallas_call x2, Pallas kernels, place_rows(): pl.pallas_call(place_kernel, grid=(count // step,), in_specs=[pl.BlockSpe...  6.04 us
    pallas_call x2, Pallas kernels, mix_rows(): pl.pallas_call(mix_kernel, grid=(count // step,), in_specs=[pl.BlockSpec(...  5.24 us
  transfers between devices with their start and end apart: 7, of which 5 were waited for; matrix products, arithmetic and copies ran while one was open for 2% of the time, Pallas kernels for 11%

profile of v12, /device:TPU:6, one launch (start us, length us, event | category | flops | bytes accessed | tf_op | source)
XLA Modules:
  0.0 244.7 jit_solution(12155092988591188949)
XLA Ops:
  6.5 0.0 copy-start
  6.5 0.0 copy-start.3
  6.5 0.0 copy-start.4
  6.5 0.0 all-gather.5.cloned.1.call-start
  6.5 0.7 all-gather.5.cloned.1.call-update
  7.3 0.0 all-gather.7.cloned.1.call-start
  7.3 0.7 constant_dynamic-slice_fusion
  8.1 38.5 %all-gather = bf16[1024,256]{1,0:T(8,128)(2,1)S(1)} all-gather(bf16[64,256]{1,0:T(8,128)(2,1)S(1)} %pad_maximum_fusion.2), channel_id=2, replica_groups=mesh['x'=4,'y'=4,'z'=16,'core'=2] {'z'}, dimensions={0}, use_global_device_ids=true | all-gather | bytes 557056 | tf_op jit(solution)/shard_map/all_gather | solution.py:39
  46.6 1.9 collective-permute-start
  48.5 0.0 all-gather.7.cloned.1.call-update
  48.6 0.0 copy-done.3
  48.6 0.0 copy-done.4
  48.7 0.1 reshape.123
  48.8 0.1 reshape.124
  48.8 0.1 reshape.125
  48.9 0.1 convolution_convert_fusion
  49.1 0.1 reshape.122
  49.2 0.1 reshape.121
  49.3 0.1 broadcast_compare_fusion
  49.5 0.9 collective-permute-done
  50.4 0.3 pad_maximum_fusion
  50.7 0.0 copy-done
  50.7 0.6 fusion.40
  51.3 0.0 copy-start.2
  51.3 0.4 convolution_bitcast_fusion
  51.7 0.4 copy-done.2
  52.1 29.8 %all-gather.1 = bf16[1280,256]{1,0:T(8,128)(2,1)S(1)} all-gather(bf16[80,256]{1,0:T(8,128)(2,1)S(1)} %fusion.8), channel_id=3, replica_groups=mesh['x'=4,'y'=4,'z'=16,'core'=2] {'z'}, dimensions={0}, use_global_device_ids=true | all-gather | bytes 696320 | tf_op jit(solution)/shard_map/all_gather | solution.py:222
  82.0 0.0 copy-start.1
  82.0 2.6 %shard_map.82 = bf16[16,8,32,256]{3,2,1,0:T(8,128)(2,1)} custom-call(bf16[16,80,256]{2,1,0:T(8,128)(2,1)S(1)} %bitcast.63), custom_call_target="tpu_custom_call" | custom-call | flops 134217728 | bytes 3145728 | tf_op jit(solution)/shard_map/pallas_call | solution.py:80
  84.5 0.0 copy-done.1
  84.5 7.4 %all-to-all-start = ((bf16[16,8,32,256]{3,2,1,0:T(8,128)(2,1)}), bf16[16,8,32,256]{3,2,1,0:T(8,128)(2,1)}, u32[]{:S(2)}, u32[]{:S(2)}) async-start(bf16[16,8,32,256]{3,2,1,0:T(8,128)(2,1)} %shard_map.82), calls=%async_computation | async-start | bytes 4194304 | tf_op jit(solution)/shard_map/all_to_all | solution.py:209
  92.0 3.5 %shard_map.84 = bf16[16,8,32,256]{3,2,1,0:T(8,128)(2,1)} custom-call(bf16[16,80,256]{2,1,0:T(8,128)(2,1)} %bitcast.64), custom_call_target="tpu_custom_call" | custom-call | flops 134217728 | bytes 3145728 | tf_op jit(solution)/shard_map/pallas_call | solution.py:80
  95.4 17.7 %all-to-all-done.rows_ref = bf16[16,8,32,256]{3,2,1,0:T(8,128)(2,1)} async-done(((bf16[16,8,32,256]{3,2,1,0:T(8,128)(2,1)}), bf16[16,8,32,256]{3,2,1,0:T(8,128)(2,1)}, u32[]{:S(2)}, u32[]{:S(2)}) %all-to-all-start) | async-done | bytes 2097184 | tf_op jit(solution)/shard_map/all_to_all | solution.py:209
  113.2 6.7 %all-to-all-start.1 = ((bf16[16,8,32,256]{3,2,1,0:T(8,128)(2,1)}), bf16[16,8,32,256]{3,2,1,0:T(8,128)(2,1)}, u32[]{:S(2)}, u32[]{:S(2)}) async-start(bf16[16,8,32,256]{3,2,1,0:T(8,128)(2,1)} %shard_map.84), calls=%async_computation.1 | async-start | bytes 4194304 | tf_op jit(solution)/shard_map/all_to_all | solution.py:209
  119.9 0.0 all-gather.5.cloned.1.call-done.in_ref
  119.9 0.0 all-gather.7.cloned.1.call-done.down_ref
  119.9 8.7 %shard_map.83 = bf16[16,8,32,256]{3,2,1,0:T(8,128)(2,1)} custom-call(bf16[16,8,32,256]{3,2,1,0:T(8,128)(2,1)} %all-to-all-done.rows_ref, bf16[2,4096,256]{2,1,0:T(8,128)(2,1)} %all-gather.5.cloned.1.call-done.in_ref, bf16[2,256,4096]{2,1,0:T(8,128)(2,1)} %all-gather.7.cloned.1.call-done.down_ref), custom_call_target="tpu_custom_call" | custom-call | flops 2147483648 | bytes 12582912 | tf_op jit(solution)/shard_map/pallas_call | solution.py:158
  128.6 11.0 %all-to-all-done.1.rows_ref = bf16[16,8,32,256]{3,2,1,0:T(8,128)(2,1)} async-done(((bf16[16,8,32,256]{3,2,1,0:T(8,128)(2,1)}), bf16[16,8,32,256]{3,2,1,0:T(8,128)(2,1)}, u32[]{:S(2)}, u32[]{:S(2)}) %all-to-all-start.1) | async-done | bytes 2097184 | tf_op jit(solution)/shard_map/all_to_all | solution.py:209
  139.5 6.6 %all-to-all-start.2 = ((bf16[16,8,32,256]{3,2,1,0:T(8,128)(2,1)}), bf16[16,8,32,256]{3,2,1,0:T(8,128)(2,1)}, u32[]{:S(2)}, u32[]{:S(2)}) async-start(bf16[16,8,32,256]{3,2,1,0:T(8,128)(2,1)} %shard_map.83), calls=%async_computation.2 | async-start | bytes 4194304 | tf_op jit(solution)/shard_map/all_to_all | solution.py:209
  146.1 8.7 %shard_map.86 = bf16[16,8,32,256]{3,2,1,0:T(8,128)(2,1)} custom-call(bf16[16,8,32,256]{3,2,1,0:T(8,128)(2,1)} %all-to-all-done.1.rows_ref, bf16[2,4096,256]{2,1,0:T(8,128)(2,1)} %all-gather.5.cloned.1.call-done.in_ref, bf16[2,256,4096]{2,1,0:T(8,128)(2,1)} %all-gather.7.cloned.1.call-done.down_ref), custom_call_target="tpu_custom_call" | custom-call | flops 2147483648 | bytes 12582912 | tf_op jit(solution)/shard_map/pallas_call | solution.py:158
  154.8 10.2 %all-to-all-done.2.rows_ref = bf16[16,8,32,256]{3,2,1,0:T(8,128)(2,1)} async-done(((bf16[16,8,32,256]{3,2,1,0:T(8,128)(2,1)}), bf16[16,8,32,256]{3,2,1,0:T(8,128)(2,1)}, u32[]{:S(2)}, u32[]{:S(2)}) %all-to-all-start.2) | async-done | bytes 2097184 | tf_op jit(solution)/shard_map/all_to_all | solution.py:209
  165.0 6.6 %all-to-all-start.3 = ((bf16[16,8,32,256]{3,2,1,0:T(8,128)(2,1)}), bf16[16,8,32,256]{3,2,1,0:T(8,128)(2,1)}, u32[]{:S(2)}, u32[]{:S(2)}) async-start(bf16[16,8,32,256]{3,2,1,0:T(8,128)(2,1)} %shard_map.86), calls=%async_computation.3 | async-start | bytes 4194304 | tf_op jit(solution)/shard_map/all_to_all | solution.py:209
  171.6 0.8 slice_convert_fusion
  172.4 0.1 reshape.135
  172.6 0.2 copy.52
  172.9 0.2 copy.53
  173.1 0.2 copy.54
  173.3 0.2 copy.50
  173.6 0.2 copy.51
  173.8 0.1 add_bitcast_fusion.1.slots_ref
  173.9 0.1 add_bitcast_fusion.gates_ref
  174.0 2.6 %shard_map.85 = bf16[8,64,256]{2,1,0:T(8,128)(2,1)S(1)} custom-call(f32[16,64,4]{2,1,0:T(8,128)S(1)} %add_bitcast_fusion.1.slots_ref, f32[16,64,4]{2,1,0:T(8,128)S(1)} %add_bitcast_fusion.gates_ref, bf16[16,8,32,256]{3,2,1,0:T(8,128)(2,1)} %all-to-all-done.2.rows_ref), custom_call_target="tpu_custom_call" | custom-call | flops 268435456 | bytes 3145728 | tf_op jit(solution)/shard_map/pallas_call | solution.py:109
  176.7 13.6 %all-to-all-done.3.rows_ref = bf16[16,8,32,256]{3,2,1,0:T(8,128)(2,1)} async-done(((bf16[16,8,32,256]{3,2,1,0:T(8,128)(2,1)}), bf16[16,8,32,256]{3,2,1,0:T(8,128)(2,1)}, u32[]{:S(2)}, u32[]{:S(2)}) %all-to-all-start.3) | async-done | bytes 2097184 | tf_op jit(solution)/shard_map/all_to_all | solution.py:209
  190.2 2.6 %shard_map.87 = bf16[8,64,256]{2,1,0:T(8,128)(2,1)S(1)} custom-call(f32[16,64,4]{2,1,0:T(8,128)S(1)} %add_bitcast_fusion.1.slots_ref, f32[16,64,4]{2,1,0:T(8,128)S(1)} %add_bitcast_fusion.gates_ref, bf16[16,8,32,256]{3,2,1,0:T(8,128)(2,1)} %all-to-all-done.3.rows_ref), custom_call_target="tpu_custom_call" | custom-call | flops 268435456 | bytes 3145728 | tf_op jit(solution)/shard_map/pallas_call | solution.py:109
  192.9 44.3 %all_to_all.25 = bf16[16,64,256]{2,1,0:T(8,128)(2,1)S(1)} all-to-all(bf16[16,64,256]{2,1,0:T(8,128)(2,1)S(1)} %pad_maximum_fusion.1), channel_id=1, replica_groups=mesh['x'=4,'y'=4,'z'=16,'core'=2] {'z'}, dimensions={0} | all-to-all | bytes 1048576 | tf_op jit(solution)/shard_map/all_to_all | solution.py:32
  237.2 0.1 convert_reduce_fusion
  237.3 0.6 add_convert_fusion
  (15 shorter events, 0.2 us)
Async XLA Ops:
  6.5 44.2 %copy-start = (bf16[64,256]{1,0:T(8,128)(2,1)S(1)}, bf16[64,256]{1,0:T(8,128)(2,1)}, u32[]{:S(2)}) copy-start(bf16[64,256]{1,0:T(8,128)(2,1)} %param.8) | copy-start | bytes 98308
  6.5 42.0 %copy-start.3 = (s32[64,4]{0,1:T(4,128)S(1)}, s32[64,4]{0,1:T(4,128)}, u32[]{:S(2)}) copy-start(s32[64,4]{0,1:T(4,128)} %param.12) | copy-start | bytes 3076
  6.5 42.1 %copy-start.4 = (f32[64,4]{0,1:T(4,128)S(1)}, f32[64,4]{0,1:T(4,128)}, u32[]{:S(2)}) copy-start(f32[64,4]{0,1:T(4,128)} %param.13) | copy-start | bytes 3076
  6.5 113.3 %all-gather.5.cloned.1.call-start = ((), (), s32[]{:S(2)}) async-start(), calls=%async_computation.5 | async-start | bytes 6291456 | tf_op jit(solution)/shard_map/all_gather | solution.py:213
  7.3 112.6 %all-gather.7.cloned.1.call-start = ((), (), s32[]{:S(2)}) async-start(), calls=%async_computation.6 | async-start | bytes 6291456 | tf_op jit(solution)/shard_map/all_gather | solution.py:214
  46.6 3.8 %collective-permute-start = (bf16[16,64,256]{2,1,0:T(8,128)(2,1)S(1)}, bf16[16,64,256]{2,1,0:T(8,128)(2,1)S(1)}, u32[]{:S(2)}, u32[]{:S(2)}) collective-permute-start(bf16[16,64,256]{2,1,0:T(8,128)(2,1)S(1)} %bitcast.66), channel_id=1, source_target_pairs={{0,1},{1,0},{2,3},{3,2},{4,5},{5,4},{6,7},{7,6},{8,9},{9,8},{10,11... | collective-permute-start | bytes 1572872 | tf_op jit(solution)/shard_map/ppermute | solution.py:28
  51.3 0.8 copy-start.2
  82.0 2.6 %copy-start.1 = (bf16[1280,256]{1,0:T(8,128)(2,1)}, bf16[1280,256]{1,0:T(8,128)(2,1)S(1)}, u32[]{:S(2)}) copy-start(bf16[1280,256]{1,0:T(8,128)(2,1)S(1)} %all-gather.1) | copy-start | bytes 1966084
  84.5 28.6 %all-to-all-start = ((bf16[16,8,32,256]{3,2,1,0:T(8,128)(2,1)}), bf16[16,8,32,256]{3,2,1,0:T(8,128)(2,1)}, u32[]{:S(2)}, u32[]{:S(2)}) async-start(bf16[16,8,32,256]{3,2,1,0:T(8,128)(2,1)} %shard_map.82), calls=%async_computation | async-start | bytes 4194304 | tf_op jit(solution)/shard_map/all_to_all | solution.py:209
  113.2 26.4 %all-to-all-start.1 = ((bf16[16,8,32,256]{3,2,1,0:T(8,128)(2,1)}), bf16[16,8,32,256]{3,2,1,0:T(8,128)(2,1)}, u32[]{:S(2)}, u32[]{:S(2)}) async-start(bf16[16,8,32,256]{3,2,1,0:T(8,128)(2,1)} %shard_map.84), calls=%async_computation.1 | async-start | bytes 4194304 | tf_op jit(solution)/shard_map/all_to_all | solution.py:209
  139.5 25.5 %all-to-all-start.2 = ((bf16[16,8,32,256]{3,2,1,0:T(8,128)(2,1)}), bf16[16,8,32,256]{3,2,1,0:T(8,128)(2,1)}, u32[]{:S(2)}, u32[]{:S(2)}) async-start(bf16[16,8,32,256]{3,2,1,0:T(8,128)(2,1)} %shard_map.83), calls=%async_computation.2 | async-start | bytes 4194304 | tf_op jit(solution)/shard_map/all_to_all | solution.py:209
  165.0 25.2 %all-to-all-start.3 = ((bf16[16,8,32,256]{3,2,1,0:T(8,128)(2,1)}), bf16[16,8,32,256]{3,2,1,0:T(8,128)(2,1)}, u32[]{:S(2)}, u32[]{:S(2)}) async-start(bf16[16,8,32,256]{3,2,1,0:T(8,128)(2,1)} %shard_map.86), calls=%async_computation.3 | async-start | bytes 4194304 | tf_op jit(solution)/shard_map/all_to_all | solution.py:209
Sparse Core Ops, SparseCore 0:
  9.5 28.5 all-gather.4
  48.7 19.8 all-gather.6
